TPU v7x, 32 devices: a whole 2x2x4 slice. The times are simulated.
32 devices in a mesh: shots: 2 (over y), wide: 16 (over z, x, core).
Axes of the slice: x: 2, y: 2, z: 4, core: 2. Of those that a mesh axis runs over, the one named last changes fastest.
Arguments:
- src_now: float32 [32, 64, 128], P('wide', 'shots'), parts along dimension 1, may hold values from -6 to 6
- src_old: float32 [32, 64, 128], P('wide', 'shots'), parts along dimension 1, may hold values from -6 to 6
- rcv_now: float32 [32, 256, 32], P('wide', 'shots'), parts along dimension 1, may hold values from -6 to 6
- rcv_old: float32 [32, 256, 32], P('wide', 'shots'), parts along dimension 1, may hold values from -6 to 6
- medium: float32 [3, 32, 128, 32], P(None, 'wide'), may hold values from 0.04 to 0.24
- wavelet: float32 [4], replicated, may hold values from -4 to 4
- shot: int32 [6], P('shots'), parts along dimension 0, may hold values from 0 to 31
- traces: float32 [32, 128, 4], P('wide', 'shots'), parts along dimension 1, may hold values from -6 to 6
- rec_x: int32 [32, 128], P('wide', 'shots'), parts along dimension 1, may hold values from 0 to 31
- lag_order: int32 [33], replicated, may hold values from 0 to 32, each once
Outputs:
- src_next: float32 [32, 64, 128], P('wide', 'shots'), parts along dimension 1
- src_prior: float32 [32, 64, 128], P('wide', 'shots'), parts along dimension 1
- rcv_next: float32 [32, 256, 32], P('wide', 'shots'), parts along dimension 1
- rcv_prior: float32 [32, 256, 32], P('wide', 'shots'), parts along dimension 1
- image: float32 [66, 32, 128, 32], P('shots', 'wide'), parts along dimension 0
There are 2 independent parts, one for each index of `shots`. A program takes and returns all parts, laid end to end along the dimension named above; an argument that names none is the same for every part. Nothing has to cross between parts.
Inputs may be any that keep to these rules, and one draw needn't show every extreme that they name: `lag_order`: each of the 33 lag slots once.
All inputs are finite; a program needn't handle non-finite values.
Results may differ from a plain program's by a relative error of at most 0.0003.
Values sent between devices are 32-bit elements; how exact they have to be, the bound alone decides.
No kernel may reach another device: no remote copies, remote signals or barrier semaphores. Data moves between devices by JAX's collectives and lax.ppermute only.
A program may use at most 64 MiB of HBM per device.

v0:
```python
import jax
import jax.numpy as jnp
from jax import lax
from jax.sharding import PartitionSpec as P


def extended(array, sides, width):
    for axis, dim in sides:
        devices, length = (lax.axis_size(axis), array.shape[dim])
        up = [(i, (i + 1) % devices) for i in range(devices - 1)]
        down = [(j, i) for i, j in up]
        last = lax.slice_in_dim(array, length - width, length, axis=dim)
        initial = lax.slice_in_dim(array, 0, width, axis=dim)
        before = lax.ppermute(last, axis, up)
        after = lax.ppermute(initial, axis, down)
        array = jnp.concatenate([before, array, after], axis=dim)
    return array


def window_sum(padded, dim, count):

    def window_at(start):
        return lax.slice_in_dim(padded, start, start + count, axis=dim)

    return (
        -1.0 / 12.0 * (window_at(0) + window_at(4))
        + 4.0 / 3.0 * (window_at(1) + window_at(3))
        - 2.5 * window_at(2)
    )


def widen(field, dim):
    widths = [(0, 0)] * field.ndim
    widths[dim] = (2, 2)
    return jnp.pad(field, widths)


def second(field, dim):
    return window_sum(widen(field, dim), dim, field.shape[dim])


def lagged(snaps, lag_order):
    half = (lag_order.shape[0] - 1) // 2
    cells_x = snaps[0][0].shape[2]
    widths = ((0, 0), (0, 0), (half, half))
    padded = [(jnp.pad(source, widths), jnp.pad(receiver, widths)) for source, receiver in snaps]

    def one_plane(slot):
        offset = slot - half
        total = None
        for source, receiver in padded:
            moved_src = lax.dynamic_slice_in_dim(source, half - offset, cells_x, 2)
            moved_rcv = lax.dynamic_slice_in_dim(receiver, half + offset, cells_x, 2)
            product = moved_src * moved_rcv
            total = product if total is None else total + product
        return total

    return lax.map(one_plane, lag_order)


def indicator(count, first, target):
    return (jnp.arange(count, dtype=jnp.int32) + first == target).astype(jnp.float32)


def on_device(src_now, src_old, rcv_now, rcv_old, medium, wavelet, shot, traces, rec_x, lag_order):
    slab_x, cells_y, cells_z = src_now.shape
    slab_y, _, cells_x = rcv_now.shape
    device = lax.axis_index("wide")
    steps = wavelet.shape[0]
    onehot = (rec_x[:, :, None] == jnp.arange(cells_x, dtype=jnp.int32)[None, None, :]).astype(
        jnp.float32
    )
    shot_rcv = (
        indicator(slab_y, device * slab_y, shot[1])[:, None, None]
        * indicator(cells_z, 0, shot[2])[None, :, None]
        * indicator(cells_x, 0, shot[0])[None, None, :]
    )
    snaps = []
    turned_now, turned_old = (
        lax.all_to_all(src_now, "wide", split_axis=1, concat_axis=0, tiled=True),
        lax.all_to_all(src_old, "wide", split_axis=1, concat_axis=0, tiled=True),
    )
    pair_now = jnp.stack([jnp.transpose(turned_now, (1, 2, 0)), rcv_now])
    pair_old = jnp.stack([jnp.transpose(turned_old, (1, 2, 0)), rcv_old])
    for step in range(steps):
        widened = extended(pair_now, (("wide", 1),), 2)
        spread = (
            medium[0] * second(pair_now, 3)
            + medium[1] * window_sum(widened, 1, slab_y)
            + medium[2] * second(pair_now, 2)
        )
        pair_new = 2.0 * pair_now - pair_old + spread
        pair_new = pair_new.at[0].add(-wavelet[step] * shot_rcv)
        pair_new = pair_new.at[1, :, 0, :].add(
            jnp.einsum("yr,yrx->yx", traces[:, :, step], onehot, precision=lax.Precision.HIGHEST)
        )
        pair_old, pair_now = (pair_now, pair_new)
        if step % 2 == 1:
            snaps.append((pair_now[0], pair_now[1]))
    back_now, back_old = (
        lax.all_to_all(pair_now[0], "wide", split_axis=2, concat_axis=0, tiled=True),
        lax.all_to_all(pair_old[0], "wide", split_axis=2, concat_axis=0, tiled=True),
    )
    src_next = jnp.transpose(back_now, (2, 0, 1))
    src_prior = jnp.transpose(back_old, (2, 0, 1))
    return (src_next, src_prior, pair_now[1], pair_old[1], lagged(snaps, lag_order))


def solution(mesh):
    return jax.shard_map(
        on_device,
        mesh=mesh,
        in_specs=(
            P("wide", "shots", None),
            P("wide", "shots", None),
            P("wide", "shots", None),
            P("wide", "shots", None),
            P(None, "wide", None, None),
            P(),
            P("shots"),
            P("wide", "shots", None),
            P("wide", "shots"),
            P(),
        ),
        out_specs=(
            P("wide", "shots", None),
            P("wide", "shots", None),
            P("wide", "shots", None),
            P("wide", "shots", None),
            P("shots", "wide", None, None),
        ),
        check_vma=False,
    )
```

profile of v0, /device:TPU:0, one launch (start us, length us, event | category | flops | bytes accessed | tf_op | source)
XLA Modules:
  0.0 220.1 jit_solution(10086139652803222354)
XLA Ops:
  0.7 1.4 copy.55
  2.1 7.4 %all-to-all-start = ((f32[2,32,128]{2,0,1:T(2,128)}), f32[2,32,128]{2,0,1:T(2,128)S(1)}, u32[]{:S(2)}, u32[]{:S(2)}) async-start(f32[2,32,128]{2,0,1:T(2,128)} %copy.55), calls=%async_computation | async-start | bytes 65536 | tf_op jit(solution)/shard_map/all_to_all | solution.py:80
  9.4 0.8 slice_bitcast_fusion.8
  10.3 1.4 copy.57
  11.6 1.4 fusion.109
  13.0 0.6 compare_convert_fusion.1
  13.7 0.7 compare_convert_fusion.2
  14.4 1.4 fusion.108
  16.4 6.0 %all-to-all-start.1 = ((f32[2,32,128]{2,0,1:T(2,128)}), f32[2,32,128]{2,0,1:T(2,128)S(1)}, u32[]{:S(2)}, u32[]{:S(2)}) async-start(f32[2,32,128]{2,0,1:T(2,128)} %copy.57), calls=%async_computation.1 | async-start | bytes 65536 | tf_op jit(solution)/shard_map/all_to_all | solution.py:81
  22.5 0.8 pad_maximum_fusion.10
  23.2 2.3 %collective-permute-start = (f32[2,2,128,32]{2,3,1,0:T(8,128)S(1)}, f32[2,2,128,32]{2,3,1,0:T(8,128)S(1)}, u32[]{:S(2)}, u32[]{:S(2)}) collective-permute-start(f32[2,2,128,32]{2,3,1,0:T(8,128)S(1)} %pad_maximum_fusion.10), channel_id=1, source_target_pairs={{0,1},{1,2},{2,3},{3,4},{4,5},{5,6},{6,7},{7,8},{8,9},{9,10},{10,1... | collective-permute-start | bytes 196616 | tf_op jit(solution)/shard_map/ppermute | solution.py:14
  25.6 1.3 collective-permute-start.1
  26.9 0.7 compare_convert_fusion
  27.5 1.6 all-to-all-done.1
  29.1 0.7 collective-permute-done.1
  29.8 0.9 fusion.11
  31.3 4.8 %collective-permute-start.2 = (f32[2,2,128,32]{2,3,1,0:T(8,128)S(1)}, f32[2,2,128,32]{2,3,1,0:T(8,128)S(1)}, u32[]{:S(2)}, u32[]{:S(2)}) collective-permute-start(f32[2,2,128,32]{2,3,1,0:T(8,128)S(1)} %scatter-add.29), channel_id=1, source_target_pairs={{0,1},{1,2},{2,3},{3,4},{4,5},{5,6},{6,7},{7,8},{8,9},{9,10},{10,1... | collective-permute-start | bytes 196616 | tf_op jit(solution)/shard_map/ppermute | solution.py:14
  36.1 1.3 collective-permute-start.3
  38.1 1.2 collective-permute-done.3
  40.0 5.1 %collective-permute-start.4 = (f32[2,2,128,32]{2,3,1,0:T(8,128)S(1)}, f32[2,2,128,32]{2,3,1,0:T(8,128)S(1)}, u32[]{:S(2)}, u32[]{:S(2)}) collective-permute-start(f32[2,2,128,32]{2,3,1,0:T(8,128)S(1)} %scatter-add.31), channel_id=1, source_target_pairs={{0,1},{1,2},{2,3},{3,4},{4,5},{5,6},{6,7},{7,8},{8,9},{9,10},{10,1... | collective-permute-start | bytes 196616 | tf_op jit(solution)/shard_map/ppermute | solution.py:14
  45.0 1.3 collective-permute-start.5
  48.9 5.3 %collective-permute-start.6 = (f32[2,2,128,32]{2,3,1,0:T(8,128)S(1)}, f32[2,2,128,32]{2,3,1,0:T(8,128)S(1)}, u32[]{:S(2)}, u32[]{:S(2)}) collective-permute-start(f32[2,2,128,32]{2,3,1,0:T(8,128)S(1)} %scatter-add.35), channel_id=1, source_target_pairs={{0,1},{1,2},{2,3},{3,4},{4,5},{5,6},{6,7},{7,8},{8,9},{9,10},{10,1... | collective-permute-start | bytes 196616 | tf_op jit(solution)/shard_map/ppermute | solution.py:14
  54.1 1.3 collective-permute-start.7
  56.0 0.6 copy.66
  56.7 7.4 %all-to-all-start.3 = ((f32[2,128,32]{1,0,2:T(2,128)}), f32[2,128,32]{1,0,2:T(2,128)S(1)}, u32[]{:S(2)}, u32[]{:S(2)}) async-start(f32[2,128,32]{1,0,2:T(2,128)} %copy.66), calls=%async_computation.3 | async-start | bytes 65536 | tf_op jit(solution)/shard_map/all_to_all | solution.py:102
  64.1 6.6 %all-to-all-done.3 = f32[2,128,32]{1,0,2:T(2,128)S(1)} async-done(((f32[2,128,32]{1,0,2:T(2,128)}), f32[2,128,32]{1,0,2:T(2,128)S(1)}, u32[]{:S(2)}, u32[]{:S(2)}) %all-to-all-start.3) | async-done | bytes 32800 | tf_op jit(solution)/shard_map/all_to_all | solution.py:102
  70.7 0.6 copy.68
  72.1 0.6 copy.63
  72.7 3.5 %all-to-all-start.2 = ((f32[2,128,32]{1,0,2:T(2,128)}), f32[2,128,32]{1,0,2:T(2,128)S(1)}, u32[]{:S(2)}, u32[]{:S(2)}) async-start(f32[2,128,32]{1,0,2:T(2,128)} %copy.63), calls=%async_computation.2 | async-start | bytes 65536 | tf_op jit(solution)/shard_map/all_to_all | solution.py:101
  76.3 143.2 %while.23 = (s32[]{:T(128)}, f32[33,2,128,32]{2,3,1,0:T(8,128)}, s32[33]{0:T(128)S(1)}, f32[2,128,64]{1,2,0:T(8,128)S(1)}, f32[2,128,64]{1,2,0:T(8,128)S(1)}, /*...) while((s32[]{:T(128)}, f32[33,2,128,32]{2,3,1,0:T(8,128)}, ...), condition=%wide.region_1.2_spmd, body=%wide.region_0.1_spmd.sunk | while | flops 24586 | bytes 819957 | solution.py:58
  80.0 0.6 constant_dynamic-update-slice_fusion.2
  84.3 0.6 constant_dynamic-update-slice_fusion.2
  88.7 0.6 constant_dynamic-update-slice_fusion.2
  93.0 0.6 constant_dynamic-update-slice_fusion.2
  97.3 0.6 constant_dynamic-update-slice_fusion.2
  101.7 0.6 constant_dynamic-update-slice_fusion.2
  106.0 0.6 constant_dynamic-update-slice_fusion.2
  110.4 0.6 constant_dynamic-update-slice_fusion.2
  114.7 0.6 constant_dynamic-update-slice_fusion.2
  119.0 0.6 constant_dynamic-update-slice_fusion.2
  123.4 0.6 constant_dynamic-update-slice_fusion.2
  127.7 0.6 constant_dynamic-update-slice_fusion.2
  132.0 0.6 constant_dynamic-update-slice_fusion.2
  136.4 0.6 constant_dynamic-update-slice_fusion.2
  140.7 0.6 constant_dynamic-update-slice_fusion.2
  145.1 0.6 constant_dynamic-update-slice_fusion.2
  149.4 0.6 constant_dynamic-update-slice_fusion.2
  153.7 0.6 constant_dynamic-update-slice_fusion.2
  158.1 0.6 constant_dynamic-update-slice_fusion.2
  162.4 0.6 constant_dynamic-update-slice_fusion.2
  166.8 0.6 constant_dynamic-update-slice_fusion.2
  171.1 0.6 constant_dynamic-update-slice_fusion.2
  175.4 0.6 constant_dynamic-update-slice_fusion.2
  179.8 0.6 constant_dynamic-update-slice_fusion.2
  184.1 0.6 constant_dynamic-update-slice_fusion.2
  188.5 0.6 constant_dynamic-update-slice_fusion.2
  192.8 0.6 constant_dynamic-update-slice_fusion.2
  197.1 0.6 constant_dynamic-update-slice_fusion.2
  201.5 0.6 constant_dynamic-update-slice_fusion.2
  205.8 0.6 constant_dynamic-update-slice_fusion.2
  210.2 0.6 constant_dynamic-update-slice_fusion.2
  214.5 0.6 constant_dynamic-update-slice_fusion.2
  218.8 0.6 constant_dynamic-update-slice_fusion.2
  219.5 0.6 copy.65
  (343 shorter events, 41.0 us)
Async XLA Ops:
  0.6 38.7 %copy-start = (f32[2,128,32]{1,2,0:T(8,128)S(1)}, f32[2,128,32]{1,2,0:T(8,128)}, u32[]{:S(2)}) copy-start(f32[2,128,32]{1,2,0:T(8,128)} %param.30) | copy-start | bytes 98308
  0.6 30.2 %copy-start.2 = (f32[2,64,4]{1,2,0:T(4,128)S(1)}, f32[2,64,4]{1,2,0:T(4,128)}, u32[]{:S(2)}) copy-start(f32[2,64,4]{1,2,0:T(4,128)} %param.35) | copy-start | bytes 6148
  0.7 30.2 %copy-start.3 = (s32[2,64]{1,0:T(2,128)S(1)}, s32[2,64]{1,0:T(2,128)}, u32[]{:S(2)}) copy-start(s32[2,64]{1,0:T(2,128)} %param.36) | copy-start | bytes 1540
  2.1 14.4 %all-to-all-start = ((f32[2,32,128]{2,0,1:T(2,128)}), f32[2,32,128]{2,0,1:T(2,128)S(1)}, u32[]{:S(2)}, u32[]{:S(2)}) async-start(f32[2,32,128]{2,0,1:T(2,128)} %copy.55), calls=%async_computation | async-start | bytes 65536 | tf_op jit(solution)/shard_map/all_to_all | solution.py:80
  16.4 12.7 %all-to-all-start.1 = ((f32[2,32,128]{2,0,1:T(2,128)}), f32[2,32,128]{2,0,1:T(2,128)S(1)}, u32[]{:S(2)}, u32[]{:S(2)}) async-start(f32[2,32,128]{2,0,1:T(2,128)} %copy.57), calls=%async_computation.1 | async-start | bytes 65536 | tf_op jit(solution)/shard_map/all_to_all | solution.py:81
  23.2 5.9 %collective-permute-start = (f32[2,2,128,32]{2,3,1,0:T(8,128)S(1)}, f32[2,2,128,32]{2,3,1,0:T(8,128)S(1)}, u32[]{:S(2)}, u32[]{:S(2)}) collective-permute-start(f32[2,2,128,32]{2,3,1,0:T(8,128)S(1)} %pad_maximum_fusion.10), channel_id=1, source_target_pairs={{0,1},{1,2},{2,3},{3,4},{4,5},{5,6},{6,7},{7,8},{8,9},{9,10},{10,1... | collective-permute-start | bytes 196616 | tf_op jit(solution)/shard_map/ppermute | solution.py:14
  25.6 4.3 %collective-permute-start.1 = (f32[2,2,128,32]{2,3,1,0:T(8,128)S(1)}, f32[2,2,128,32]{2,3,1,0:T(8,128)S(1)}, u32[]{:S(2)}, u32[]{:S(2)}) collective-permute-start(f32[2,2,128,32]{2,3,1,0:T(8,128)S(1)} %pad_maximum_fusion.10), channel_id=1, source_target_pairs={{1,0},{2,1},{3,2},{4,3},{5,4},{6,5},{7,6},{8,7},{9,8},{10,9},{11,1... | collective-permute-start | bytes 196616 | tf_op jit(solution)/shard_map/ppermute | solution.py:15
  31.3 6.8 %collective-permute-start.2 = (f32[2,2,128,32]{2,3,1,0:T(8,128)S(1)}, f32[2,2,128,32]{2,3,1,0:T(8,128)S(1)}, u32[]{:S(2)}, u32[]{:S(2)}) collective-permute-start(f32[2,2,128,32]{2,3,1,0:T(8,128)S(1)} %scatter-add.29), channel_id=1, source_target_pairs={{0,1},{1,2},{2,3},{3,4},{4,5},{5,6},{6,7},{7,8},{8,9},{9,10},{10,1... | collective-permute-start | bytes 196616 | tf_op jit(solution)/shard_map/ppermute | solution.py:14
  36.1 3.1 %collective-permute-start.3 = (f32[2,2,128,32]{2,3,1,0:T(8,128)S(1)}, f32[2,2,128,32]{2,3,1,0:T(8,128)S(1)}, u32[]{:S(2)}, u32[]{:S(2)}) collective-permute-start(f32[2,2,128,32]{2,3,1,0:T(8,128)S(1)} %scatter-add.29), channel_id=1, source_target_pairs={{1,0},{2,1},{3,2},{4,3},{5,4},{6,5},{7,6},{8,7},{9,8},{10,9},{11,1... | collective-permute-start | bytes 196616 | tf_op jit(solution)/shard_map/ppermute | solution.py:15
  40.0 7.7 %collective-permute-start.4 = (f32[2,2,128,32]{2,3,1,0:T(8,128)S(1)}, f32[2,2,128,32]{2,3,1,0:T(8,128)S(1)}, u32[]{:S(2)}, u32[]{:S(2)}) collective-permute-start(f32[2,2,128,32]{2,3,1,0:T(8,128)S(1)} %scatter-add.31), channel_id=1, source_target_pairs={{0,1},{1,2},{2,3},{3,4},{4,5},{5,6},{6,7},{7,8},{8,9},{9,10},{10,1... | collective-permute-start | bytes 196616 | tf_op jit(solution)/shard_map/ppermute | solution.py:14
  45.0 3.1 %collective-permute-start.5 = (f32[2,2,128,32]{2,3,1,0:T(8,128)S(1)}, f32[2,2,128,32]{2,3,1,0:T(8,128)S(1)}, u32[]{:S(2)}, u32[]{:S(2)}) collective-permute-start(f32[2,2,128,32]{2,3,1,0:T(8,128)S(1)} %scatter-add.31), channel_id=1, source_target_pairs={{1,0},{2,1},{3,2},{4,3},{5,4},{6,5},{7,6},{8,7},{9,8},{10,9},{11,1... | collective-permute-start | bytes 196616 | tf_op jit(solution)/shard_map/ppermute | solution.py:15
  48.3 27.9 %copy-start.4 = (s32[33]{0:T(128)S(1)}, s32[33]{0:T(128)}, u32[]{:S(2)}) copy-start(s32[33]{0:T(128)} %param.37) | copy-start | bytes 400
  48.9 22.5 %collective-permute-start.6 = (f32[2,2,128,32]{2,3,1,0:T(8,128)S(1)}, f32[2,2,128,32]{2,3,1,0:T(8,128)S(1)}, u32[]{:S(2)}, u32[]{:S(2)}) collective-permute-start(f32[2,2,128,32]{2,3,1,0:T(8,128)S(1)} %scatter-add.35), channel_id=1, source_target_pairs={{0,1},{1,2},{2,3},{3,4},{4,5},{5,6},{6,7},{7,8},{8,9},{9,10},{10,1... | collective-permute-start | bytes 196616 | tf_op jit(solution)/shard_map/ppermute | solution.py:14
  54.1 17.3 %collective-permute-start.7 = (f32[2,2,128,32]{2,3,1,0:T(8,128)S(1)}, f32[2,2,128,32]{2,3,1,0:T(8,128)S(1)}, u32[]{:S(2)}, u32[]{:S(2)}) collective-permute-start(f32[2,2,128,32]{2,3,1,0:T(8,128)S(1)} %scatter-add.35), channel_id=1, source_target_pairs={{1,0},{2,1},{3,2},{4,3},{5,4},{6,5},{7,6},{8,7},{9,8},{10,9},{11,1... | collective-permute-start | bytes 196616 | tf_op jit(solution)/shard_map/ppermute | solution.py:15
  56.7 14.0 %all-to-all-start.3 = ((f32[2,128,32]{1,0,2:T(2,128)}), f32[2,128,32]{1,0,2:T(2,128)S(1)}, u32[]{:S(2)}, u32[]{:S(2)}) async-start(f32[2,128,32]{1,0,2:T(2,128)} %copy.66), calls=%async_computation.3 | async-start | bytes 65536 | tf_op jit(solution)/shard_map/all_to_all | solution.py:102
  72.1 4.2 %copy-start.1 = (f32[2,128,32]{1,2,0:T(8,128)}, f32[2,128,32]{1,2,0:T(8,128)S(1)}, u32[]{:S(2)}) copy-start(f32[2,128,32]{1,2,0:T(8,128)S(1)} %get-tuple-element.340) | copy-start | bytes 98308
  72.7 146.7 %all-to-all-start.2 = ((f32[2,128,32]{1,0,2:T(2,128)}), f32[2,128,32]{1,0,2:T(2,128)S(1)}, u32[]{:S(2)}, u32[]{:S(2)}) async-start(f32[2,128,32]{1,0,2:T(2,128)} %copy.63), calls=%async_computation.2 | async-start | bytes 65536 | tf_op jit(solution)/shard_map/all_to_all | solution.py:101
where the time goes:
time: 224 us; the launch traced here: 220 us
  loops' own time  85 us (38%)
  local copies, waits for them, and re-layouts  67.3 us (30%)
  starting transfers between devices  46.9 us (21%)
  waiting for transfers between devices  10.6 us (5%)
  other arithmetic  5.48 us (2%)
  between operations  3.54 us (2%)
    another operation x1, loops' own time, lagged(): return lax.map(one_plane, lag_order)  85 us
    dynamic_update_slice x66, local copies, waits for them, and re-layouts, lagged(): return lax.map(one_plane, lag_order)  23 us
    dynamic_slice x33, local copies, waits for them, and re-layouts, lagged(): return lax.map(one_plane, lag_order)  19.9 us
    ppermute x4, starting transfers between devices, extended(): before = lax.ppermute(last, axis, up)  17.5 us
    dynamic_slice x132, local copies, waits for them, and re-layouts, one_plane(): moved_rcv = lax.dynamic_slice_in_dim(receiver, half + offset, cells_x, 2)  7.68 us
    all_to_all x1, starting transfers between devices, on_device(): lax.all_to_all(pair_old[0], 'wide', split_axis=2, concat_axis=0, tiled=True)  7.41 us
    all_to_all x1, starting transfers between devices, on_device(): lax.all_to_all(src_now, 'wide', split_axis=1, concat_axis=0, tiled=True)  7.36 us
    all_to_all x1, waiting for transfers between devices, on_device(): lax.all_to_all(pair_old[0], 'wide', split_axis=2, concat_axis=0, tiled=True)  6.59 us
  transfers between devices with their start and end apart: 12, of which 5 were waited for; matrix products, arithmetic and copies ran while one was open for 31% of the time, Pallas kernels for 0%

commit v1 on v0

v1 whole, which is shorter than its diff:
```python
import functools

import jax
import jax.numpy as jnp
from jax import lax
from jax.experimental import pallas as pl
from jax.experimental.pallas import tpu as pltpu
from jax.sharding import PartitionSpec as P

SLAB, CHIP, STEPS, EDGE = 2, 4, 4, 8
NEAR, FAR = 4.0 / 3.0, -1.0 / 12.0
CHAINS = 3
RCV, SRC_X, SRC_Y = range(CHAINS)
HALF_NOW = (CHIP + 2 * CHIP) // 2
HALF_OLD = (CHIP + CHIP) // 2
FETCH = 24

VMEM = pl.BlockSpec(memory_space=pltpu.VMEM)
SMEM = pl.BlockSpec(memory_space=pltpu.SMEM)


def call(kernel, operands, outs, scratch, scalars):
    size = sum(4 * o.size for o in operands[scalars:])
    size += sum(4 * functools.reduce(lambda a, b: a * b, s) for s in (*outs, *scratch))
    return pl.pallas_call(
        kernel,
        out_shape=[jax.ShapeDtypeStruct(s, jnp.float32) for s in outs],
        in_specs=[SMEM] * scalars + [VMEM] * (len(operands) - scalars),
        out_specs=[VMEM] * len(outs),
        scratch_shapes=[pltpu.VMEM(s, jnp.float32) for s in scratch],
        compiler_params=pltpu.CompilerParams(vmem_limit_bytes=size + size // 4 + (8 << 20)),
    )(*operands)


def each(count, rows, body):
    if rows <= 32:
        for i in range(count):
            body(i)
    else:
        lax.fori_loop(0, count, lambda i, _: (body(i), 0)[1], 0)


def blocks(rows):
    size = min(rows, 32)
    return [(b, size) for b in range(0, rows, size)]


def pack(src_now, src_old, rcv_now, rcv_old, med, traces, rec_x, send, loc, wide_now, wide_rest):
    rows, depth = src_now.shape[1:]
    steps, cells = traces.shape[1], loc.shape[1]
    for wide in (wide_now, wide_rest):
        count = wide.shape[0]
        wide[:, 0:EDGE, :] = jnp.zeros((count, EDGE, depth), jnp.float32)
        wide[:, EDGE + rows :, :] = jnp.zeros((count, EDGE, depth), jnp.float32)
    for h in range(SLAB):
        wide_now[h, EDGE : EDGE + rows, :] = src_now[h]
        wide_rest[h, EDGE : EDGE + rows, :] = src_old[h]
        for k in range(3):
            wide_rest[SLAB * (k + 1) + h, EDGE : EDGE + rows, :] = med[k, h]
    for j in range(send.shape[0]):
        chip, core = divmod(j, 2)
        now_at = EDGE + CHIP * chip - CHIP + HALF_NOW * core
        old_at = EDGE + CHIP * chip - SLAB + HALF_OLD * core
        for h in range(SLAB):
            base = FETCH * h
            send[j, base : base + HALF_NOW, :] = wide_now[h, now_at : now_at + HALF_NOW, :]
            for k in range(4):
                at = base + HALF_NOW + HALF_OLD * k
                send[j, at : at + HALF_OLD, :] = wide_rest[
                    SLAB * k + h, old_at : old_at + HALF_OLD, :
                ]
    for h in range(SLAB):
        loc[h] = rcv_now[h]
        loc[SLAB + h] = src_now[h]
        loc[2 * SLAB + h] = rcv_old[h]
        loc[3 * SLAB + h] = src_old[h]
        for k in range(3):
            loc[(4 + k) * SLAB + h] = med[k, h]
    lane = lax.broadcasted_iota(jnp.int32, (cells, depth), 1)
    place = lax.broadcasted_iota(jnp.int32, (cells, rec_x.shape[1]), 0)
    surface = jnp.zeros((cells, depth), jnp.float32)
    for h in range(SLAB):
        hit = rec_x[h : h + 1, :] == place
        for s in range(steps):
            column = jnp.sum(jnp.where(hit, traces[h, s : s + 1, :], 0.0), axis=1, keepdims=True)
            surface = jnp.where(lane == steps * h + s, column, surface)
    loc[7 * SLAB] = surface


def advance(now, now_at, old, old_at, med, med_at, new, new_pad, count, pad, rows, across, extra):
    depth = now.shape[2]
    lane = lax.broadcasted_iota(jnp.int32, (8, depth), 1)
    weight = [
        jnp.where(lane >= 1, NEAR, 0.0),
        jnp.where(lane < depth - 1, NEAR, 0.0),
        jnp.where(lane >= 2, FAR, 0.0),
        jnp.where(lane < depth - 2, FAR, 0.0),
    ]

    def one(i):
        w = now_at + i
        for b, size in blocks(rows):
            taps = [jnp.concatenate([t] * (size // 8), axis=0) for t in weight]

            def at(plane, shift):
                return now[plane, pad + b + shift : pad + b + shift + size, :]

            here = at(w, 0)
            centre = -2.5 * here
            plane_sum = (
                centre
                + NEAR * (at(w - 1, 0) + at(w + 1, 0))
                + FAR * (at(w - 2, 0) + at(w + 2, 0))
            )
            row_sum = (
                centre
                + NEAR * (at(w, -1) + at(w, 1))
                + FAR * (at(w, -2) + at(w, 2))
            )
            depth_sum = (
                centre
                + taps[0] * pltpu.roll(here, 1, 1)
                + taps[1] * pltpu.roll(here, depth - 1, 1)
                + taps[2] * pltpu.roll(here, 2, 1)
                + taps[3] * pltpu.roll(here, depth - 2, 1)
            )
            m = [med(k, med_at + i)[b : b + size, :] for k in range(3)]
            value = 2.0 * here - old(old_at + i)[b : b + size, :]
            value = value + m[across] * plane_sum + m[1 - across] * row_sum + m[2] * depth_sum
            if extra is not None:
                value = value + extra(i, b, size)
            new[i, new_pad + b : new_pad + b + size, :] = value

    each(count, rows, one)


def shoot(new, pad, first, count, plane, row, depth_at, amount):
    local = plane - first

    @pl.when((local >= 0) & (local < count))
    def _():
        lane = lax.broadcasted_iota(jnp.int32, (1, new.shape[2]), 1)
        spot = (pl.ds(local, 1), pl.ds(pad + row, 1), slice(None))
        new[spot] = new[spot] + jnp.where(lane == depth_at, -amount, 0.0)[None]


def surface_at(surf, first, step, steps):
    def extra(i, b, size):
        held = surf(first + i // SLAB)[b : b + size, :]
        depth = held.shape[1]
        lane = lax.broadcasted_iota(jnp.int32, (size, depth), 1)
        total = jnp.zeros_like(held)
        shift = (i % SLAB) * steps + step
        if isinstance(shift, int):
            return jnp.where(lane == 0, pltpu.roll(held, (depth - shift) % depth, 1), 0.0)
        for s in range(SLAB):
            moved = pltpu.roll(held, (depth - s * steps - step) % depth, 1)
            total = jnp.where((lane == 0) & (i % SLAB == s), moved, total)
        return total

    return extra


def clear(window, pad, rows):
    count, _, depth = window.shape
    zero = jnp.zeros((count, pad, depth), jnp.float32)
    window[:, 0:pad, :] = zero
    window[:, pad + rows :, :] = zero


def place(window, at, pad, value):
    window[at, pad : pad + value.shape[0], :] = value


def first_half(
    where, shot, wavelet, loc, sib, near, near_sib, got, got_sib, edge, carry,
    now_r, now_x, now_y, old_r, old_x, old_y, med_y, med_x, surf, new_r, new_x, new_y,
):
    rows = loc.shape[1]
    core, right, chip = where[0], where[1], where[2]
    nows, olds, news = (now_r, now_x, now_y), (old_r, old_x, old_y), (new_r, new_x, new_y)
    for window in (*nows, *news):
        clear(window, EDGE, rows)
    window_old = 2 * HALF_OLD
    for src, q in ((loc, core), (sib, 1 - core)):
        for p in range(SLAB):
            place(now_r, CHIP + SLAB * q + p, EDGE, src[p])
            place(now_x, CHIP + SLAB * q + p, EDGE, src[SLAB + p])
            old_r[SLAB + SLAB * q + p] = src[2 * SLAB + p]
            old_x[SLAB + SLAB * q + p] = src[3 * SLAB + p]
            for k in range(3):
                med_y[window_old * k + SLAB + SLAB * q + p] = src[(4 + k) * SLAB + p]
        surf[1 + q] = src[7 * SLAB]
    for src, side in ((near, right), (near_sib, 1 - right)):
        for p in range(SLAB):
            for low in range(2):
                at = 2 * CHIP * side + SLAB * low + p
                place(now_r, at, EDGE, src[2 * SLAB * low + p])
                place(now_x, at, EDGE, src[2 * SLAB * low + SLAB + p])
            at = (SLAB + CHIP) * side + p
            old_r[at] = src[4 * SLAB + p]
            old_x[at] = src[5 * SLAB + p]
            for k in range(3):
                med_y[window_old * k + at] = src[(6 + k) * SLAB + p]
        surf[3 * side] = src[9 * SLAB]
    for src, q in ((got, core), (got_sib, 1 - core)):
        for p in range(HALF_NOW):
            place(now_y, HALF_NOW * q + p, EDGE, src[pl.ds(p, rows, stride=FETCH), :])
        for p in range(HALF_OLD):
            old_y[HALF_OLD * q + p] = src[pl.ds(HALF_NOW + p, rows, stride=FETCH), :]
            for k in range(3):
                med_x[window_old * k + HALF_OLD * q + p] = src[
                    pl.ds(HALF_NOW + HALF_OLD * (k + 1) + p, rows, stride=FETCH), :
                ]

    def medium_of(ref):
        return lambda k, i: ref[window_old * k + i]

    first = CHIP * chip - SLAB
    media = (med_y, med_x, med_y)
    spot = (None, (shot[0], shot[1]), (shot[1], shot[0]))
    for c in range(CHAINS):
        across = 0 if c == SRC_X else 1
        advance(
            nows[c], SLAB, lambda i: olds[c][i], 0, medium_of(media[c]), 0, news[c], EDGE,
            window_old, EDGE, rows, across,
            surface_at(lambda i: surf[i], 0, 0, STEPS) if c == RCV else None,
        )
        if c != RCV:
            shoot(news[c], EDGE, first, window_old, *spot[c], shot[2], wavelet[0])
        advance(
            news[c], SLAB, lambda i: nows[c][CHIP + i, EDGE : EDGE + rows, :], 0,
            medium_of(media[c]), SLAB, edge.at[c], 0, CHIP, EDGE, rows, across,
            surface_at(lambda i: surf[i], 1, 1, STEPS) if c == RCV else None,
        )
        if c != RCV:
            shoot(edge.at[c], 0, first + SLAB, CHIP, *spot[c], shot[2], wavelet[1])
    span = SLAB + 2 * SLAB
    for i in range(span):
        at = SLAB * core + i
        for c in range(CHAINS):
            carry[span * c + i] = news[c][at, EDGE : EDGE + rows, :]
        for k in range(3):
            carry[span * (CHAINS + k) + i] = med_y[window_old * k + at]
            carry[span * (CHAINS + 3 + k) + i] = med_x[window_old * k + at]
    for i in range(3):
        carry[span * (CHAINS + 6) + i] = surf[core + i]


def second_half(
    where, shot, wavelet, lag_order, edge, near, near_sib, carry,
    src_next, src_prior, rcv_next, rcv_prior, image,
    now_r, now_x, now_y, new_r, new_x, new_y, end_r, end_x, end_y, slot_of,
):
    rows, depth = carry.shape[1:]
    lags = lag_order.shape[0]
    half = (lags - 1) // 2
    pad = (now_r.shape[1] - rows) // 2
    core, right, chip = where[0], where[1], where[2]
    nows, news, ends = (now_r, now_x, now_y), (new_r, new_x, new_y), (end_r, end_x, end_y)
    for window in (*nows, *news, *ends):
        clear(window, pad, rows)

    def note(k, _):
        slot_of[lag_order[k]] = k
        return 0

    lax.fori_loop(0, lags, note, 0)
    for c in range(CHAINS):
        for p in range(CHIP):
            place(nows[c], CHIP + p, pad, edge[c, p])
            place(nows[c], 2 * CHIP * right + p, pad, near[c, p])
            place(nows[c], 2 * CHIP * (1 - right) + p, pad, near_sib[c, p])
    span = SLAB + 2 * SLAB
    first = CHIP * chip + SLAB * core - SLAB
    spot = (None, (shot[0], shot[1]), (shot[1], shot[0]))
    at_surf = span * (CHAINS + 6)
    for c in (RCV, SRC_Y, SRC_X):
        across = 0 if c == SRC_X else 1
        base = span * (CHAINS + (3 if c == SRC_X else 0))

        def med(k, i):
            return carry[base + span * k + i]

        advance(
            nows[c], SLAB * core + SLAB, lambda i: carry[span * c + i], 0, med, 0, news[c], pad,
            span, pad, rows, across,
            surface_at(lambda i: carry[at_surf + i], 0, 2, STEPS) if c == RCV else None,
        )
        if c != RCV:
            shoot(news[c], pad, first, span, *spot[c], shot[2], wavelet[2])
        advance(
            news[c], SLAB, lambda i: nows[c][CHIP + SLAB * core + i, pad : pad + rows, :], 0,
            med, SLAB, ends[c], pad, SLAB, pad, rows, across,
            surface_at(lambda i: carry[at_surf + i], 1, 3, STEPS) if c == RCV else None,
        )
        if c != RCV:
            shoot(ends[c], pad, first + SLAB, SLAB, *spot[c], shot[2], wavelet[3])
    for p in range(SLAB):
        src_next[p] = end_x[p, pad : pad + rows, :]
        src_prior[p] = new_x[SLAB + p, pad : pad + rows, :]
        rcv_next[p] = end_r[p, pad : pad + rows, :]
        rcv_prior[p] = new_r[SLAB + p, pad : pad + rows, :]
    own = CHIP + SLAB * core
    for slot in range(lags):
        lag = slot - half
        k = slot_of[slot]

        def one(p):
            for b in range(0, rows, 8):
                if b + 8 <= abs(lag) or b >= rows - abs(lag):
                    image[k, p, b : b + 8, :] = jnp.zeros((8, depth), jnp.float32)
                    continue
                back, ahead = pad + b - lag, pad + b + lag
                image[k, p, b : b + 8, :] = (
                    now_y[own + p, back : back + 8, :] * now_r[own + p, ahead : ahead + 8, :]
                    + end_y[p, back : back + 8, :] * end_r[p, ahead : ahead + 8, :]
                )

        for p in range(SLAB):
            one(p)


def on_device(src_now, src_old, rcv_now, rcv_old, medium, wavelet, shot, traces, rec_x, lag_order):
    devices = lax.axis_size("wide")
    chips = devices // 2
    slab, rows, depth = src_now.shape
    assert slab == SLAB and rcv_now.shape == (SLAB, depth, rows) and wavelet.shape[0] == STEPS
    assert rows % 8 == 0 and rows == SLAB * devices
    lags = lag_order.shape[0]
    half = (lags - 1) // 2
    device = lax.axis_index("wide")
    chip, core = device // 2, device % 2
    right = (core == chip % 2).astype(jnp.int32)
    where = jnp.stack([core, right, chip]).astype(jnp.int32)
    swap = [(i, i ^ 1) for i in range(devices)]
    ties = [(2 * c + c % 2, 2 * c + 2 + c % 2) for c in range(chips - 1)]
    ties = ties + [(b, a) for a, b in ties]

    def turned(x):
        return jnp.swapaxes(x, -1, -2)

    rcv_now, rcv_old, medium, traces = map(turned, (rcv_now, rcv_old, medium, traces))
    send, loc = call(
        pack,
        (src_now, src_old, rcv_now, rcv_old, medium, traces, rec_x),
        [(devices, SLAB * FETCH, depth), (7 * SLAB + 1, rows, depth)],
        [(SLAB, rows + 2 * EDGE, depth), (4 * SLAB, rows + 2 * EDGE, depth)],
        0,
    )
    got = lax.all_to_all(send, "wide", 0, 0, tiled=True)
    sib = lax.ppermute(loc, "wide", swap)
    low, high = jnp.where(core == 0, loc, sib), jnp.where(core == 0, sib, loc)
    rim = jnp.where(right == 1, high[2 * SLAB :], low[2 * SLAB :])
    near = lax.ppermute(jnp.concatenate([low[: 2 * SLAB], high[: 2 * SLAB], rim]), "wide", ties)
    near_sib = lax.ppermute(near, "wide", swap)
    got = got.reshape(devices * SLAB * FETCH, depth)
    got_sib = lax.ppermute(got, "wide", swap)

    window, narrow, span = 3 * CHIP, 2 * CHIP, 3 * SLAB
    wide_rows = rows + 2 * EDGE
    edge, carry = call(
        first_half,
        (where, shot, wavelet, loc, sib, near, near_sib, got, got_sib),
        [(CHAINS, CHIP, rows, depth), (span * (CHAINS + 6) + 3, rows, depth)],
        [(window, wide_rows, depth)] * 3
        + [(narrow, rows, depth)] * 3
        + [(3 * narrow, rows, depth)] * 2
        + [(4, rows, depth)]
        + [(narrow, wide_rows, depth)] * 3,
        3,
    )
    near = lax.ppermute(edge, "wide", ties)
    near_sib = lax.ppermute(near, "wide", swap)

    pad = -(-max(half, 2) // 8) * 8
    wide_rows = rows + 2 * pad
    field = (SLAB, rows, depth)
    operands = (where, shot, wavelet, lag_order, edge, near, near_sib, carry)
    outs = [field] * 4 + [(lags, SLAB, rows, depth)]
    scratch = [(window, wide_rows, depth)] * 3 + [(span, wide_rows, depth)] * 3 + [field[:1] + (wide_rows, depth)] * 3
    size = sum(4 * o.size for o in operands[4:])
    size += sum(4 * functools.reduce(lambda a, b: a * b, s) for s in (*outs, *scratch))
    src_next, src_prior, rcv_next, rcv_prior, image = pl.pallas_call(
        second_half,
        out_shape=[jax.ShapeDtypeStruct(s, jnp.float32) for s in outs],
        in_specs=[SMEM] * 4 + [VMEM] * 4,
        out_specs=[VMEM] * 5,
        scratch_shapes=[pltpu.VMEM(s, jnp.float32) for s in scratch] + [pltpu.SMEM((lags,), jnp.int32)],
        compiler_params=pltpu.CompilerParams(vmem_limit_bytes=size + size // 4 + (8 << 20)),
    )(*operands)
    return src_next, src_prior, turned(rcv_next), turned(rcv_prior), turned(image)


def solution(mesh):
    return jax.shard_map(
        on_device,
        mesh=mesh,
        in_specs=(
            P("wide", "shots", None),
            P("wide", "shots", None),
            P("wide", "shots", None),
            P("wide", "shots", None),
            P(None, "wide", None, None),
            P(),
            P("shots"),
            P("wide", "shots", None),
            P("wide", "shots"),
            P(),
        ),
        out_specs=(
            P("wide", "shots", None),
            P("wide", "shots", None),
            P("wide", "shots", None),
            P("wide", "shots", None),
            P("shots", "wide", None, None),
        ),
        check_vma=False,
    )
```

time: 224 us -> 46.1 us (0.21); the launches traced: 220 us -> 45.3 us
  loops' own time: 85 us -> 0 us
  local copies, waits for them, and re-layouts: 67.3 us -> 5.31 us
  starting transfers between devices: 46.9 us -> 15.8 us
  waiting for transfers between devices: 10.6 us -> 17.9 us
  Pallas kernels: 0 us -> 5.41 us
  other arithmetic: 5.48 us -> 0.17 us
  between operations: 3.54 us -> 0.8 us
    another operation x1 -> x0, loops' own time: 85 us -> none  [lagged(): return lax.map(one_plane, lag_order)]
    dynamic_slice x231 -> x0, local copies, waits for them, and re-layouts: 34.2 us -> none  [the longest x33 19.9 us: lagged(): return lax.map(one_plane, lag_order)]
    dynamic_update_slice x66 -> x0, local copies, waits for them, and re-layouts: 23 us -> none  [lagged(): return lax.map(one_plane, lag_order)]
    all_to_all x4 -> x1, starting transfers between devices: 24.3 us -> 7.02 us  [on_device(): got = lax.all_to_all(send, 'wide', 0, 0, tiled=True)]
    ppermute x8 -> x6, starting transfers between devices: 22.7 us -> 8.75 us  [the longest x1 4.39 us: on_device(): near = lax.ppermute(edge, 'wide', ties)]
    ppermute x8 -> x6, waiting for transfers between devices: 2.47 us -> 9.72 us  [the longest x1 5.27 us: on_device(): near = lax.ppermute(edge, 'wide', ties)]
    pallas_call x0 -> x3, Pallas kernels: none -> 5.41 us  [the longest x1 2.89 us: on_device(): pl.pallas_call(second_half, out_shape=[jax.ShapeDtypeStruct(s, jnp.float3...]
    slice x2, local copies, waits for them, and re-layouts: 2.77 us -> 0.01 us  [the longest x1 0.01 us: on_device(): low[:2 * SLAB]]
  transfers between devices with their start and end apart: 12 -> 7, of which waited for: 5 -> 5; matrix products, arithmetic and copies ran while one was open for 31% -> 0% of each run, Pallas kernels for 0% -> 0%
where the time goes in v1:
time: 46.1 us; the launch traced here: 45.3 us
  waiting for transfers between devices  17.9 us (39%)
  starting transfers between devices  15.8 us (34%)
  Pallas kernels  5.41 us (12%)
  local copies, waits for them, and re-layouts  5.31 us (12%)
  between operations  0.8 us (2%)
    all_to_all x1, waiting for transfers between devices, on_device(): got = lax.all_to_all(send, 'wide', 0, 0, tiled=True)  8.17 us
    all_to_all x1, starting transfers between devices, on_device(): got = lax.all_to_all(send, 'wide', 0, 0, tiled=True)  7.02 us
    unnamed x20, local copies, waits for them, and re-layouts  5.3 us
    ppermute x1, waiting for transfers between devices, on_device(): near = lax.ppermute(edge, 'wide', ties)  5.27 us
    ppermute x1, starting transfers between devices, on_device(): near = lax.ppermute(edge, 'wide', ties)  4.39 us
    ppermute x1, starting transfers between devices, on_device(): lax.ppermute(jnp.concatenate([low[:2 * SLAB], high[:2 * SLAB], rim]), 'wi...  3.79 us
    ppermute x2, waiting for transfers between devices, on_device(): near_sib = lax.ppermute(near, 'wide', swap)  2.97 us
    pallas_call x1, Pallas kernels, on_device(): pl.pallas_call(second_half, out_shape=[jax.ShapeDtypeStruct(s, jnp.float3...  2.89 us
  transfers between devices with their start and end apart: 7, of which 5 were waited for; matrix products, arithmetic and copies ran while one was open for 0% of the time, Pallas kernels for 0%

profile of v1, /device:TPU:0, one launch (start us, length us, event | category | flops | bytes accessed | tf_op | source)
XLA Modules:
  0.0 45.3 jit_solution(15299295722887245451)
XLA Ops:
  0.6 0.0 copy-start
  0.6 0.9 %copy-done = f32[3,2,128,32]{2,3,1,0:T(8,128)S(1)} copy-done((f32[3,2,128,32]{2,3,1,0:T(8,128)S(1)}, f32[3,2,128,32]{2,3,1,0:T(8,128)}, u32[]{:S(2)}) %copy-start) | copy-done | bytes 98328
  1.5 0.0 copy-start.1
  1.5 0.8 %copy-done.1 = f32[2,32,128]{2,1,0:T(8,128)S(1)} copy-done((f32[2,32,128]{2,1,0:T(8,128)S(1)}, f32[2,32,128]{2,1,0:T(8,128)}, u32[]{:S(2)}) %copy-start.1) | copy-done | bytes 32792
  2.3 0.0 copy-start.2
  2.3 0.8 %copy-done.2 = f32[2,32,128]{2,1,0:T(8,128)S(1)} copy-done((f32[2,32,128]{2,1,0:T(8,128)S(1)}, f32[2,32,128]{2,1,0:T(8,128)}, u32[]{:S(2)}) %copy-start.2) | copy-done | bytes 32792
  3.0 0.0 copy-start.3
  3.0 0.8 %copy-done.3 = f32[2,128,32]{1,2,0:T(8,128)S(1)} copy-done((f32[2,128,32]{1,2,0:T(8,128)S(1)}, f32[2,128,32]{1,2,0:T(8,128)}, u32[]{:S(2)}) %copy-start.3) | copy-done | bytes 32792
  3.8 0.0 copy-start.4
  3.8 0.8 %copy-done.4 = f32[2,128,32]{1,2,0:T(8,128)S(1)} copy-done((f32[2,128,32]{1,2,0:T(8,128)S(1)}, f32[2,128,32]{1,2,0:T(8,128)}, u32[]{:S(2)}) %copy-start.4) | copy-done | bytes 32792
  4.6 0.0 copy-start.5
  4.6 0.7 %copy-done.5 = f32[2,64,4]{1,2,0:T(4,128)S(1)} copy-done((f32[2,64,4]{1,2,0:T(4,128)S(1)}, f32[2,64,4]{1,2,0:T(4,128)}, u32[]{:S(2)}) %copy-start.5) | copy-done | bytes 2072
  5.2 0.0 copy-start.8
  5.3 0.7 %copy-done.8 = s32[2,64]{1,0:T(2,128)S(1)} copy-done((s32[2,64]{1,0:T(2,128)S(1)}, s32[2,64]{1,0:T(2,128)}, u32[]{:S(2)}) %copy-start.8) | copy-done | bytes 536
  5.9 0.8 %shard_map.137 = (f32[16,48,128]{2,1,0:T(8,128)}, f32[15,32,128]{2,1,0:T(8,128)S(1)}) custom-call(f32[2,32,128]{2,1,0:T(8,128)S(1)} %copy-done.1, f32[2,32,128]{2,1,0:T(8,128)S(1)} %copy-done.2, f32[2,32,128]{2,1,0:T(8,128)S(1)} %bitcast.14, f32[2,32,128]{2,1,0:T(8,128)S(1)} %bitcast.15, f32[3,2,32,128]{3,2,1,0:T(8,128)S(1)} %bitcast.13, ...), custom_call_target="tpu_custom_call" | custom-call | tf_op jit(solution)/shard_map/pallas_call | solution.py:25
  6.8 0.5 collective-permute-start
  7.2 7.0 %all-to-all-start = ((f32[16,48,128]{2,1,0:T(8,128)}), f32[16,48,128]{2,1,0:T(8,128)S(1)}, u32[]{:S(2)}, u32[]{:S(2)}) async-start(f32[16,48,128]{2,1,0:T(8,128)} %get-tuple-element.15), calls=%async_computation | async-start | bytes 786432 | tf_op jit(solution)/shard_map/all_to_all | solution.py:351
  14.3 0.0 copy-start.6
  14.3 0.0 copy-start.7
  14.3 0.0 collective-permute-done.sib
  14.5 0.0 copy-start.9
  14.5 3.8 %collective-permute-start.1 = (f32[19,32,128]{2,1,0:T(8,128)S(1)}, f32[19,32,128]{2,1,0:T(8,128)S(1)}, u32[]{:S(2)}, u32[]{:S(2)}) collective-permute-start(f32[19,32,128]{2,1,0:T(8,128)S(1)} %pad_maximum_fusion), channel_id=1, source_target_pairs={{0,2},{3,5},{4,6},{7,9},{8,10},{11,13},{12,14},{2,0},{5,3},{6,4},{... | collective-permute-start | bytes 933896 | tf_op jit(solution)/shard_map/ppermute | solution.py:355
  18.3 8.2 %all-to-all-done = f32[16,48,128]{2,1,0:T(8,128)S(1)} async-done(((f32[16,48,128]{2,1,0:T(8,128)}), f32[16,48,128]{2,1,0:T(8,128)S(1)}, u32[]{:S(2)}, u32[]{:S(2)}) %all-to-all-start) | async-done | bytes 393248 | tf_op jit(solution)/shard_map/all_to_all | solution.py:351
  26.4 0.1 collective-permute-start.3
  26.6 1.5 %collective-permute-done.1.near = f32[19,32,128]{2,1,0:T(8,128)S(1)} collective-permute-done((f32[19,32,128]{2,1,0:T(8,128)S(1)}, f32[19,32,128]{2,1,0:T(8,128)S(1)}, u32[]{:S(2)}, u32[]{:S(2)}) %collective-permute-start.1) | collective-permute-done | bytes 311328 | tf_op jit(solution)/shard_map/ppermute | solution.py:355
  28.0 0.0 collective-permute-start.2
  28.0 0.1 pad_add_fusion.where
  28.1 1.5 %collective-permute-done.2.near_sib = f32[19,32,128]{2,1,0:T(8,128)S(1)} collective-permute-done((f32[19,32,128]{2,1,0:T(8,128)S(1)}, f32[19,32,128]{2,1,0:T(8,128)S(1)}, u32[]{:S(2)}, u32[]{:S(2)}) %collective-permute-start.2) | collective-permute-done | bytes 311328 | tf_op jit(solution)/shard_map/ppermute | solution.py:356
  29.6 0.0 collective-permute-done.3.got_sib
  29.6 0.0 copy-done.6
  29.6 0.0 copy-done.7
  29.6 1.7 %shard_map.138 = (f32[3,4,32,128]{3,2,1,0:T(8,128)S(1)}, f32[57,32,128]{2,1,0:T(8,128)S(1)}) custom-call(s32[3]{0:T(128)S(1)} %pad_add_fusion.where, s32[3]{0:T(128)S(1)} %copy-done.6, f32[4]{0:T(128)S(1)} %copy-done.7, f32[15,32,128]{2,1,0:T(8,128)S(1)} %get-tuple-element.14.loc, f32[15,32,128]{2,1,0:T(8,128)S(1)} %collective-permute-done.sib, ...), custom_call_target="tpu_custom_call" | custom-call | tf_op jit(solution)/shard_map/pallas_call | solution.py:25
  31.3 4.4 %collective-permute-start.4 = (f32[3,4,32,128]{3,2,1,0:T(8,128)S(1)}, f32[3,4,32,128]{3,2,1,0:T(8,128)S(1)}, u32[]{:S(2)}, u32[]{:S(2)}) collective-permute-start(f32[3,4,32,128]{3,2,1,0:T(8,128)S(1)} %get-tuple-element.16.edge), channel_id=1, source_target_pairs={{0,2},{3,5},{4,6},{7,9},{8,10},{11,13},{12,14},{2,0},{5,3},{6,4},{... | collective-permute-start | bytes 589832 | tf_op jit(solution)/shard_map/ppermute | solution.py:373
  35.7 5.3 %collective-permute-done.4.near = f32[3,4,32,128]{3,2,1,0:T(8,128)S(1)} collective-permute-done((f32[3,4,32,128]{3,2,1,0:T(8,128)S(1)}, f32[3,4,32,128]{3,2,1,0:T(8,128)S(1)}, u32[]{:S(2)}, u32[]{:S(2)}) %collective-permute-start.4) | collective-permute-done | bytes 196640 | tf_op jit(solution)/shard_map/ppermute | solution.py:373
  41.0 0.0 collective-permute-start.5
  41.0 1.4 %collective-permute-done.5.near_sib = f32[3,4,32,128]{3,2,1,0:T(8,128)S(1)} collective-permute-done((f32[3,4,32,128]{3,2,1,0:T(8,128)S(1)}, f32[3,4,32,128]{3,2,1,0:T(8,128)S(1)}, u32[]{:S(2)}, u32[]{:S(2)}) %collective-permute-start.5) | collective-permute-done | bytes 196640 | tf_op jit(solution)/shard_map/ppermute | solution.py:374
  42.5 0.0 copy-done.9
  42.5 2.9 %shard_map.139 = (f32[2,32,128]{2,1,0:T(8,128)}, f32[2,32,128]{2,1,0:T(8,128)}, f32[2,32,128]{2,1,0:T(8,128)}, f32[2,32,128]{2,1,0:T(8,128)}, f32[33,2,32,128]{3,2,1,0:T(8,128)}) custom-call(s32[3]{0:T(128)S(1)} %pad_add_fusion.where, s32[3]{0:T(128)S(1)} %copy-done.6, f32[4]{0:T(128)S(1)} %copy-done.7, s32[33]{0:T(128)S(1)} %copy-done.9, ...), custom_call_target="tpu_custom_call" | custom-call | tf_op jit(solution)/shard_map/pallas_call | solution.py:384
  (5 shorter events, 0.1 us)
Async XLA Ops:
  0.6 0.9 %copy-start = (f32[3,2,128,32]{2,3,1,0:T(8,128)S(1)}, f32[3,2,128,32]{2,3,1,0:T(8,128)}, u32[]{:S(2)}) copy-start(f32[3,2,128,32]{2,3,1,0:T(8,128)} %param.14) | copy-start | bytes 294916
  1.5 0.8 %copy-start.1 = (f32[2,32,128]{2,1,0:T(8,128)S(1)}, f32[2,32,128]{2,1,0:T(8,128)}, u32[]{:S(2)}) copy-start(f32[2,32,128]{2,1,0:T(8,128)} %src_now.1) | copy-start | bytes 98308
  2.3 0.8 %copy-start.2 = (f32[2,32,128]{2,1,0:T(8,128)S(1)}, f32[2,32,128]{2,1,0:T(8,128)}, u32[]{:S(2)}) copy-start(f32[2,32,128]{2,1,0:T(8,128)} %src_old.1) | copy-start | bytes 98308
  3.0 0.8 %copy-start.3 = (f32[2,128,32]{1,2,0:T(8,128)S(1)}, f32[2,128,32]{1,2,0:T(8,128)}, u32[]{:S(2)}) copy-start(f32[2,128,32]{1,2,0:T(8,128)} %param.12) | copy-start | bytes 98308
  3.8 0.8 %copy-start.4 = (f32[2,128,32]{1,2,0:T(8,128)S(1)}, f32[2,128,32]{1,2,0:T(8,128)}, u32[]{:S(2)}) copy-start(f32[2,128,32]{1,2,0:T(8,128)} %param.13) | copy-start | bytes 98308
  4.6 0.7 %copy-start.5 = (f32[2,64,4]{1,2,0:T(4,128)S(1)}, f32[2,64,4]{1,2,0:T(4,128)}, u32[]{:S(2)}) copy-start(f32[2,64,4]{1,2,0:T(4,128)} %param.17) | copy-start | bytes 6148
  5.2 0.7 %copy-start.8 = (s32[2,64]{1,0:T(2,128)S(1)}, s32[2,64]{1,0:T(2,128)}, u32[]{:S(2)}) copy-start(s32[2,64]{1,0:T(2,128)} %rec_x.1) | copy-start | bytes 1540
  6.8 7.5 %collective-permute-start = (f32[15,32,128]{2,1,0:T(8,128)S(1)}, f32[15,32,128]{2,1,0:T(8,128)S(1)}, u32[]{:S(2)}, u32[]{:S(2)}) collective-permute-start(f32[15,32,128]{2,1,0:T(8,128)S(1)} %get-tuple-element.14.loc), channel_id=1, source_target_pairs={{0,1},{1,0},{2,3},{3,2},{4,5},{5,4},{6,7},{7,6},{8,9},{9,8},{10,11... | collective-permute-start | bytes 737288 | tf_op jit(solution)/shard_map/ppermute | solution.py:352
  7.2 19.2 %all-to-all-start = ((f32[16,48,128]{2,1,0:T(8,128)}), f32[16,48,128]{2,1,0:T(8,128)S(1)}, u32[]{:S(2)}, u32[]{:S(2)}) async-start(f32[16,48,128]{2,1,0:T(8,128)} %get-tuple-element.15), calls=%async_computation | async-start | bytes 786432 | tf_op jit(solution)/shard_map/all_to_all | solution.py:351
  14.3 15.4 %copy-start.6 = (s32[3]{0:T(128)S(1)}, s32[3]{0:T(128)}, u32[]{:S(2)}) copy-start(s32[3]{0:T(128)} %shot.3) | copy-start | bytes 40
  14.3 15.3 %copy-start.7 = (f32[4]{0:T(128)S(1)}, f32[4]{0:T(128)}, u32[]{:S(2)}) copy-start(f32[4]{0:T(128)} %wavelet.3) | copy-start | bytes 52
  14.5 28.0 %copy-start.9 = (s32[33]{0:T(128)S(1)}, s32[33]{0:T(128)}, u32[]{:S(2)}) copy-start(s32[33]{0:T(128)} %lag_order.1) | copy-start | bytes 400
  14.5 13.6 %collective-permute-start.1 = (f32[19,32,128]{2,1,0:T(8,128)S(1)}, f32[19,32,128]{2,1,0:T(8,128)S(1)}, u32[]{:S(2)}, u32[]{:S(2)}) collective-permute-start(f32[19,32,128]{2,1,0:T(8,128)S(1)} %pad_maximum_fusion), channel_id=1, source_target_pairs={{0,2},{3,5},{4,6},{7,9},{8,10},{11,13},{12,14},{2,0},{5,3},{6,4},{... | collective-permute-start | bytes 933896 | tf_op jit(solution)/shard_map/ppermute | solution.py:355
  26.4 3.2 %collective-permute-start.3 = (f32[768,128]{1,0:T(8,128)S(1)}, f32[768,128]{1,0:T(8,128)S(1)}, u32[]{:S(2)}, u32[]{:S(2)}) collective-permute-start(f32[768,128]{1,0:T(8,128)S(1)} %bitcast.11), channel_id=1, source_target_pairs={{0,1},{1,0},{2,3},{3,2},{4,5},{5,4},{6,7},{7,6},{8,9},{9,8},{10,11... | collective-permute-start | bytes 1179656 | tf_op jit(solution)/shard_map/ppermute | solution.py:358
  28.0 1.6 %collective-permute-start.2 = (f32[19,32,128]{2,1,0:T(8,128)S(1)}, f32[19,32,128]{2,1,0:T(8,128)S(1)}, u32[]{:S(2)}, u32[]{:S(2)}) collective-permute-start(f32[19,32,128]{2,1,0:T(8,128)S(1)} %collective-permute-done.1.near), channel_id=1, source_target_pairs={{0,1},{1,0},{2,3},{3,2},{4,5},{5,4},{6,7},{7,6},{8,9},{9,8},{10,11... | collective-permute-start | bytes 933896 | tf_op jit(solution)/shard_map/ppermute | solution.py:356
  31.3 9.7 %collective-permute-start.4 = (f32[3,4,32,128]{3,2,1,0:T(8,128)S(1)}, f32[3,4,32,128]{3,2,1,0:T(8,128)S(1)}, u32[]{:S(2)}, u32[]{:S(2)}) collective-permute-start(f32[3,4,32,128]{3,2,1,0:T(8,128)S(1)} %get-tuple-element.16.edge), channel_id=1, source_target_pairs={{0,2},{3,5},{4,6},{7,9},{8,10},{11,13},{12,14},{2,0},{5,3},{6,4},{... | collective-permute-start | bytes 589832 | tf_op jit(solution)/shard_map/ppermute | solution.py:373
  41.0 1.4 %collective-permute-start.5 = (f32[3,4,32,128]{3,2,1,0:T(8,128)S(1)}, f32[3,4,32,128]{3,2,1,0:T(8,128)S(1)}, u32[]{:S(2)}, u32[]{:S(2)}) collective-permute-start(f32[3,4,32,128]{3,2,1,0:T(8,128)S(1)} %collective-permute-done.4.near), channel_id=1, source_target_pairs={{0,1},{1,0},{2,3},{3,2},{4,5},{5,4},{6,7},{7,6},{8,9},{9,8},{10,11... | collective-permute-start | bytes 589832 | tf_op jit(solution)/shard_map/ppermute | solution.py:374

commit v2 on v1

--- a/solution.py
+++ b/solution.py
@@ -17,17 +17,20 @@
 
 VMEM = pl.BlockSpec(memory_space=pltpu.VMEM)
 SMEM = pl.BlockSpec(memory_space=pltpu.SMEM)
-
-
-def call(kernel, operands, outs, scratch, scalars):
+HBM = pl.BlockSpec(memory_space=pltpu.HBM)
+
+
+def call(kernel, operands, outs, scratch, scalars, held=(), far_in=False, far_out=()):
     size = sum(4 * o.size for o in operands[scalars:])
     size += sum(4 * functools.reduce(lambda a, b: a * b, s) for s in (*outs, *scratch))
+    if far_in:
+        operands = [pltpu.with_memory_space_constraint(o, pltpu.HBM) for o in operands]
     return pl.pallas_call(
         kernel,
         out_shape=[jax.ShapeDtypeStruct(s, jnp.float32) for s in outs],
-        in_specs=[SMEM] * scalars + [VMEM] * (len(operands) - scalars),
-        out_specs=[VMEM] * len(outs),
-        scratch_shapes=[pltpu.VMEM(s, jnp.float32) for s in scratch],
+        in_specs=[SMEM] * scalars + [HBM if far_in else VMEM] * (len(operands) - scalars),
+        out_specs=[HBM if n in far_out else VMEM for n in range(len(outs))],
+        scratch_shapes=[pltpu.VMEM(s, jnp.float32) for s in scratch] + list(held),
         compiler_params=pltpu.CompilerParams(vmem_limit_bytes=size + size // 4 + (8 << 20)),
     )(*operands)
 
@@ -45,18 +48,39 @@
     return [(b, size) for b in range(0, rows, size)]
 
 
-def pack(src_now, src_old, rcv_now, rcv_old, med, traces, rec_x, send, loc, wide_now, wide_rest):
+def pack(
+    src_now, src_old, rcv_now, rcv_old, med, traces, rec_x, send, loc,
+    wide_now, wide_rest, traces_in, rec_in, sems,
+):
     rows, depth = src_now.shape[1:]
     steps, cells = traces.shape[1], loc.shape[1]
+    inner = pl.ds(EDGE, rows)
+    pairs = [(traces, traces_in), (rec_x, rec_in)]
+    pairs += [(src_now, wide_now.at[:, inner]), (src_old, wide_rest.at[pl.ds(0, SLAB), inner])]
+    pairs += [(med.at[k], wide_rest.at[pl.ds(SLAB * (k + 1), SLAB), inner]) for k in range(3)]
+    for n, own in enumerate((rcv_now, src_now, rcv_old, src_old)):
+        pairs.append((own, loc.at[pl.ds(n * SLAB, SLAB)]))
+    pairs += [(med.at[k], loc.at[pl.ds((4 + k) * SLAB, SLAB)]) for k in range(3)]
+    copies = [pltpu.make_async_copy(a, b, sems.at[n]) for n, (a, b) in enumerate(pairs)]
+    for copy in copies:
+        copy.start()
     for wide in (wide_now, wide_rest):
         count = wide.shape[0]
         wide[:, 0:EDGE, :] = jnp.zeros((count, EDGE, depth), jnp.float32)
         wide[:, EDGE + rows :, :] = jnp.zeros((count, EDGE, depth), jnp.float32)
+    for copy in copies[:2]:
+        copy.wait()
+    lane = lax.broadcasted_iota(jnp.int32, (cells, depth), 1)
+    place = lax.broadcasted_iota(jnp.int32, (cells, rec_x.shape[1]), 0)
+    surface = jnp.zeros((cells, depth), jnp.float32)
     for h in range(SLAB):
-        wide_now[h, EDGE : EDGE + rows, :] = src_now[h]
-        wide_rest[h, EDGE : EDGE + rows, :] = src_old[h]
-        for k in range(3):
-            wide_rest[SLAB * (k + 1) + h, EDGE : EDGE + rows, :] = med[k, h]
+        hit = rec_in[h : h + 1, :] == place
+        for s in range(steps):
+            column = jnp.sum(jnp.where(hit, traces_in[h, s : s + 1, :], 0.0), axis=1, keepdims=True)
+            surface = jnp.where(lane == steps * h + s, column, surface)
+    loc[7 * SLAB] = surface
+    for copy in copies[2:]:
+        copy.wait()
     for j in range(send.shape[0]):
         chip, core = divmod(j, 2)
         now_at = EDGE + CHIP * chip - CHIP + HALF_NOW * core
@@ -69,22 +93,6 @@
                 send[j, at : at + HALF_OLD, :] = wide_rest[
                     SLAB * k + h, old_at : old_at + HALF_OLD, :
                 ]
-    for h in range(SLAB):
-        loc[h] = rcv_now[h]
-        loc[SLAB + h] = src_now[h]
-        loc[2 * SLAB + h] = rcv_old[h]
-        loc[3 * SLAB + h] = src_old[h]
-        for k in range(3):
-            loc[(4 + k) * SLAB + h] = med[k, h]
-    lane = lax.broadcasted_iota(jnp.int32, (cells, depth), 1)
-    place = lax.broadcasted_iota(jnp.int32, (cells, rec_x.shape[1]), 0)
-    surface = jnp.zeros((cells, depth), jnp.float32)
-    for h in range(SLAB):
-        hit = rec_x[h : h + 1, :] == place
-        for s in range(steps):
-            column = jnp.sum(jnp.where(hit, traces[h, s : s + 1, :], 0.0), axis=1, keepdims=True)
-            surface = jnp.where(lane == steps * h + s, column, surface)
-    loc[7 * SLAB] = surface
 
 
 def advance(now, now_at, old, old_at, med, med_at, new, new_pad, count, pad, rows, across, extra):
@@ -250,7 +258,7 @@
 def second_half(
     where, shot, wavelet, lag_order, edge, near, near_sib, carry,
     src_next, src_prior, rcv_next, rcv_prior, image,
-    now_r, now_x, now_y, new_r, new_x, new_y, end_r, end_x, end_y, slot_of,
+    now_r, now_x, now_y, new_r, new_x, new_y, end_r, end_x, end_y, planes, slot_of, sems,
 ):
     rows, depth = carry.shape[1:]
     lags = lag_order.shape[0]
@@ -302,23 +310,25 @@
         rcv_next[p] = end_r[p, pad : pad + rows, :]
         rcv_prior[p] = new_r[SLAB + p, pad : pad + rows, :]
     own = CHIP + SLAB * core
+    copies = []
     for slot in range(lags):
         lag = slot - half
-        k = slot_of[slot]
-
-        def one(p):
+        for p in range(SLAB):
             for b in range(0, rows, 8):
                 if b + 8 <= abs(lag) or b >= rows - abs(lag):
-                    image[k, p, b : b + 8, :] = jnp.zeros((8, depth), jnp.float32)
+                    planes[slot, p, b : b + 8, :] = jnp.zeros((8, depth), jnp.float32)
                     continue
                 back, ahead = pad + b - lag, pad + b + lag
-                image[k, p, b : b + 8, :] = (
+                planes[slot, p, b : b + 8, :] = (
                     now_y[own + p, back : back + 8, :] * now_r[own + p, ahead : ahead + 8, :]
                     + end_y[p, back : back + 8, :] * end_r[p, ahead : ahead + 8, :]
                 )
-
-        for p in range(SLAB):
-            one(p)
+        copies.append(
+            pltpu.make_async_copy(planes.at[slot], image.at[slot_of[slot]], sems.at[slot])
+        )
+        copies[-1].start()
+    for copy in copies:
+        copy.wait()
 
 
 def on_device(src_now, src_old, rcv_now, rcv_old, medium, wavelet, shot, traces, rec_x, lag_order):
@@ -345,8 +355,10 @@
         pack,
         (src_now, src_old, rcv_now, rcv_old, medium, traces, rec_x),
         [(devices, SLAB * FETCH, depth), (7 * SLAB + 1, rows, depth)],
-        [(SLAB, rows + 2 * EDGE, depth), (4 * SLAB, rows + 2 * EDGE, depth)],
+        [(SLAB, rows + 2 * EDGE, depth), (4 * SLAB, rows + 2 * EDGE, depth), traces.shape],
         0,
+        [pltpu.VMEM(rec_x.shape, jnp.int32), pltpu.SemaphoreType.DMA((14,))],
+        far_in=True,
     )
     got = lax.all_to_all(send, "wide", 0, 0, tiled=True)
     sib = lax.ppermute(loc, "wide", swap)
@@ -376,19 +388,18 @@
     pad = -(-max(half, 2) // 8) * 8
     wide_rows = rows + 2 * pad
     field = (SLAB, rows, depth)
-    operands = (where, shot, wavelet, lag_order, edge, near, near_sib, carry)
-    outs = [field] * 4 + [(lags, SLAB, rows, depth)]
-    scratch = [(window, wide_rows, depth)] * 3 + [(span, wide_rows, depth)] * 3 + [field[:1] + (wide_rows, depth)] * 3
-    size = sum(4 * o.size for o in operands[4:])
-    size += sum(4 * functools.reduce(lambda a, b: a * b, s) for s in (*outs, *scratch))
-    src_next, src_prior, rcv_next, rcv_prior, image = pl.pallas_call(
+    src_next, src_prior, rcv_next, rcv_prior, image = call(
         second_half,
-        out_shape=[jax.ShapeDtypeStruct(s, jnp.float32) for s in outs],
-        in_specs=[SMEM] * 4 + [VMEM] * 4,
-        out_specs=[VMEM] * 5,
-        scratch_shapes=[pltpu.VMEM(s, jnp.float32) for s in scratch] + [pltpu.SMEM((lags,), jnp.int32)],
-        compiler_params=pltpu.CompilerParams(vmem_limit_bytes=size + size // 4 + (8 << 20)),
-    )(*operands)
+        (where, shot, wavelet, lag_order, edge, near, near_sib, carry),
+        [field] * 4 + [(lags, SLAB, rows, depth)],
+        [(window, wide_rows, depth)] * 3
+        + [(span, wide_rows, depth)] * 3
+        + [(SLAB, wide_rows, depth)] * 3
+        + [(lags, SLAB, rows, depth)],
+        4,
+        [pltpu.SMEM((lags,), jnp.int32), pltpu.SemaphoreType.DMA((lags,))],
+        far_out=(4,),
+    )
     return src_next, src_prior, turned(rcv_next), turned(rcv_prior), turned(image)
 
 

time: 46.1 us -> 42.4 us (0.920)
  local copies, waits for them, and re-layouts: 5.31 us -> 0.03 us
  Pallas kernels: 5.41 us -> 7.23 us
    unnamed x20 -> x6, local copies, waits for them, and re-layouts: 5.3 us -> 0.02 us
    pallas_call x2 -> x3, Pallas kernels: 2.52 us -> 7.23 us  [call(): pl.pallas_call(kernel, out_shape=[jax.ShapeDtypeStruct(s, jnp.float32) fo...]
    pallas_call x1 -> x0, Pallas kernels: 2.89 us -> none  [on_device(): pl.pallas_call(second_half, out_shape=[jax.ShapeDtypeStruct(s, jnp.float3...]
where the time goes in v2:
time: 42.4 us; the launch traced here: 41.9 us
  waiting for transfers between devices  17.9 us (42%)
  starting transfers between devices  15.8 us (37%)
  Pallas kernels  7.23 us (17%)
  between operations  0.8 us (2%)
    all_to_all x1, waiting for transfers between devices, on_device(): got = lax.all_to_all(send, 'wide', 0, 0, tiled=True)  8.17 us
    pallas_call x3, Pallas kernels, call(): pl.pallas_call(kernel, out_shape=[jax.ShapeDtypeStruct(s, jnp.float32) fo...  7.23 us
    all_to_all x1, starting transfers between devices, on_device(): got = lax.all_to_all(send, 'wide', 0, 0, tiled=True)  7.02 us
    ppermute x1, waiting for transfers between devices, on_device(): near = lax.ppermute(edge, 'wide', ties)  5.27 us
    ppermute x1, starting transfers between devices, on_device(): near = lax.ppermute(edge, 'wide', ties)  4.38 us
    ppermute x1, starting transfers between devices, on_device(): lax.ppermute(jnp.concatenate([low[:2 * SLAB], high[:2 * SLAB], rim]), 'wi...  3.79 us
    ppermute x2, waiting for transfers between devices, on_device(): near_sib = lax.ppermute(near, 'wide', swap)  2.97 us
    ppermute x1, waiting for transfers between devices, on_device(): lax.ppermute(jnp.concatenate([low[:2 * SLAB], high[:2 * SLAB], rim]), 'wi...  1.47 us
  transfers between devices with their start and end apart: 7, of which 5 were waited for; matrix products, arithmetic and copies ran while one was open for 0% of the time, Pallas kernels for 0%

profile of v2, /device:TPU:0, one launch (start us, length us, event | category | flops | bytes accessed | tf_op | source)
XLA Modules:
  0.0 41.9 jit_solution(6970211883654961771)
XLA Ops:
  0.6 1.9 %shard_map.137 = (f32[16,48,128]{2,1,0:T(8,128)}, f32[15,32,128]{2,1,0:T(8,128)S(1)}) custom-call(f32[2,32,128]{2,1,0:T(8,128)} %src_now.1, f32[2,32,128]{2,1,0:T(8,128)} %src_old.1, f32[2,32,128]{2,1,0:T(8,128)} %bitcast.14, f32[2,32,128]{2,1,0:T(8,128)} %bitcast.15, f32[3,2,32,128]{3,2,1,0:T(8,128)} %bitcast.13, f32[2,4,64]{2,1,0:T(4,128)} %bitcast.16, ...), custom_call_target="tpu_custom_call" | custom-call | tf_op jit(solution)/shard_map/pallas_call | solution.py:28
  2.5 0.5 %collective-permute-start = (f32[15,32,128]{2,1,0:T(8,128)S(1)}, f32[15,32,128]{2,1,0:T(8,128)S(1)}, u32[]{:S(2)}, u32[]{:S(2)}) collective-permute-start(f32[15,32,128]{2,1,0:T(8,128)S(1)} %get-tuple-element.14.loc), channel_id=1, source_target_pairs={{0,1},{1,0},{2,3},{3,2},{4,5},{5,4},{6,7},{7,6},{8,9},{9,8},{10,11... | collective-permute-start | bytes 737288 | tf_op jit(solution)/shard_map/ppermute | solution.py:364
  3.1 7.0 %all-to-all-start = ((f32[16,48,128]{2,1,0:T(8,128)}), f32[16,48,128]{2,1,0:T(8,128)S(1)}, u32[]{:S(2)}, u32[]{:S(2)}) async-start(f32[16,48,128]{2,1,0:T(8,128)} %get-tuple-element.15), calls=%async_computation | async-start | bytes 786432 | tf_op jit(solution)/shard_map/all_to_all | solution.py:363
  10.1 0.0 copy-start
  10.1 0.0 copy-start.1
  10.2 0.0 collective-permute-done.sib
  10.3 0.0 copy-start.2
  10.3 3.8 %collective-permute-start.1 = (f32[19,32,128]{2,1,0:T(8,128)S(1)}, f32[19,32,128]{2,1,0:T(8,128)S(1)}, u32[]{:S(2)}, u32[]{:S(2)}) collective-permute-start(f32[19,32,128]{2,1,0:T(8,128)S(1)} %pad_maximum_fusion), channel_id=1, source_target_pairs={{0,2},{3,5},{4,6},{7,9},{8,10},{11,13},{12,14},{2,0},{5,3},{6,4},{... | collective-permute-start | bytes 933896 | tf_op jit(solution)/shard_map/ppermute | solution.py:367
  14.1 8.2 %all-to-all-done = f32[16,48,128]{2,1,0:T(8,128)S(1)} async-done(((f32[16,48,128]{2,1,0:T(8,128)}), f32[16,48,128]{2,1,0:T(8,128)S(1)}, u32[]{:S(2)}, u32[]{:S(2)}) %all-to-all-start) | async-done | bytes 393248 | tf_op jit(solution)/shard_map/all_to_all | solution.py:363
  22.3 0.1 collective-permute-start.3
  22.4 1.5 %collective-permute-done.1.near = f32[19,32,128]{2,1,0:T(8,128)S(1)} collective-permute-done((f32[19,32,128]{2,1,0:T(8,128)S(1)}, f32[19,32,128]{2,1,0:T(8,128)S(1)}, u32[]{:S(2)}, u32[]{:S(2)}) %collective-permute-start.1) | collective-permute-done | bytes 311328 | tf_op jit(solution)/shard_map/ppermute | solution.py:367
  23.9 0.0 collective-permute-start.2
  23.9 0.1 pad_add_fusion.where
  23.9 1.5 %collective-permute-done.2.near_sib = f32[19,32,128]{2,1,0:T(8,128)S(1)} collective-permute-done((f32[19,32,128]{2,1,0:T(8,128)S(1)}, f32[19,32,128]{2,1,0:T(8,128)S(1)}, u32[]{:S(2)}, u32[]{:S(2)}) %collective-permute-start.2) | collective-permute-done | bytes 311328 | tf_op jit(solution)/shard_map/ppermute | solution.py:368
  25.5 0.0 collective-permute-done.3.got_sib
  25.5 0.0 copy-done
  25.5 0.0 copy-done.1
  25.5 1.7 %shard_map.138 = (f32[3,4,32,128]{3,2,1,0:T(8,128)S(1)}, f32[57,32,128]{2,1,0:T(8,128)S(1)}) custom-call(s32[3]{0:T(128)S(1)} %pad_add_fusion.where, s32[3]{0:T(128)S(1)} %copy-done, f32[4]{0:T(128)S(1)} %copy-done.1, f32[15,32,128]{2,1,0:T(8,128)S(1)} %get-tuple-element.14.loc, f32[15,32,128]{2,1,0:T(8,128)S(1)} %collective-permute-done.sib, ...), custom_call_target="tpu_custom_call" | custom-call | tf_op jit(solution)/shard_map/pallas_call | solution.py:28
  27.2 4.4 %collective-permute-start.4 = (f32[3,4,32,128]{3,2,1,0:T(8,128)S(1)}, f32[3,4,32,128]{3,2,1,0:T(8,128)S(1)}, u32[]{:S(2)}, u32[]{:S(2)}) collective-permute-start(f32[3,4,32,128]{3,2,1,0:T(8,128)S(1)} %get-tuple-element.16.edge), channel_id=1, source_target_pairs={{0,2},{3,5},{4,6},{7,9},{8,10},{11,13},{12,14},{2,0},{5,3},{6,4},{... | collective-permute-start | bytes 589832 | tf_op jit(solution)/shard_map/ppermute | solution.py:385
  31.6 5.3 %collective-permute-done.4.near = f32[3,4,32,128]{3,2,1,0:T(8,128)S(1)} collective-permute-done((f32[3,4,32,128]{3,2,1,0:T(8,128)S(1)}, f32[3,4,32,128]{3,2,1,0:T(8,128)S(1)}, u32[]{:S(2)}, u32[]{:S(2)}) %collective-permute-start.4) | collective-permute-done | bytes 196640 | tf_op jit(solution)/shard_map/ppermute | solution.py:385
  36.8 0.0 collective-permute-start.5
  36.9 1.4 %collective-permute-done.5.near_sib = f32[3,4,32,128]{3,2,1,0:T(8,128)S(1)} collective-permute-done((f32[3,4,32,128]{3,2,1,0:T(8,128)S(1)}, f32[3,4,32,128]{3,2,1,0:T(8,128)S(1)}, u32[]{:S(2)}, u32[]{:S(2)}) %collective-permute-start.5) | collective-permute-done | bytes 196640 | tf_op jit(solution)/shard_map/ppermute | solution.py:386
  38.3 0.0 copy-done.2
  38.3 3.6 %shard_map.139 = (f32[2,32,128]{2,1,0:T(8,128)}, f32[2,32,128]{2,1,0:T(8,128)}, f32[2,32,128]{2,1,0:T(8,128)}, f32[2,32,128]{2,1,0:T(8,128)}, f32[33,2,32,128]{3,2,1,0:T(8,128)}) custom-call(s32[3]{0:T(128)S(1)} %pad_add_fusion.where, s32[3]{0:T(128)S(1)} %copy-done, f32[4]{0:T(128)S(1)} %copy-done.1, s32[33]{0:T(128)S(1)} %copy-done.2, ...), custom_call_target="tpu_custom_call" | custom-call | tf_op jit(solution)/shard_map/pallas_call | solution.py:28
  (5 shorter events, 0.1 us)
Async XLA Ops:
  2.5 7.6 %collective-permute-start = (f32[15,32,128]{2,1,0:T(8,128)S(1)}, f32[15,32,128]{2,1,0:T(8,128)S(1)}, u32[]{:S(2)}, u32[]{:S(2)}) collective-permute-start(f32[15,32,128]{2,1,0:T(8,128)S(1)} %get-tuple-element.14.loc), channel_id=1, source_target_pairs={{0,1},{1,0},{2,3},{3,2},{4,5},{5,4},{6,7},{7,6},{8,9},{9,8},{10,11... | collective-permute-start | bytes 737288 | tf_op jit(solution)/shard_map/ppermute | solution.py:364
  3.1 19.2 %all-to-all-start = ((f32[16,48,128]{2,1,0:T(8,128)}), f32[16,48,128]{2,1,0:T(8,128)S(1)}, u32[]{:S(2)}, u32[]{:S(2)}) async-start(f32[16,48,128]{2,1,0:T(8,128)} %get-tuple-element.15), calls=%async_computation | async-start | bytes 786432 | tf_op jit(solution)/shard_map/all_to_all | solution.py:363
  10.1 15.4 %copy-start = (s32[3]{0:T(128)S(1)}, s32[3]{0:T(128)}, u32[]{:S(2)}) copy-start(s32[3]{0:T(128)} %shot.3) | copy-start | bytes 40
  10.1 15.3 %copy-start.1 = (f32[4]{0:T(128)S(1)}, f32[4]{0:T(128)}, u32[]{:S(2)}) copy-start(f32[4]{0:T(128)} %wavelet.3) | copy-start | bytes 52
  10.3 28.0 %copy-start.2 = (s32[33]{0:T(128)S(1)}, s32[33]{0:T(128)}, u32[]{:S(2)}) copy-start(s32[33]{0:T(128)} %lag_order.1) | copy-start | bytes 400
  10.3 13.6 %collective-permute-start.1 = (f32[19,32,128]{2,1,0:T(8,128)S(1)}, f32[19,32,128]{2,1,0:T(8,128)S(1)}, u32[]{:S(2)}, u32[]{:S(2)}) collective-permute-start(f32[19,32,128]{2,1,0:T(8,128)S(1)} %pad_maximum_fusion), channel_id=1, source_target_pairs={{0,2},{3,5},{4,6},{7,9},{8,10},{11,13},{12,14},{2,0},{5,3},{6,4},{... | collective-permute-start | bytes 933896 | tf_op jit(solution)/shard_map/ppermute | solution.py:367
  22.3 3.2 %collective-permute-start.3 = (f32[768,128]{1,0:T(8,128)S(1)}, f32[768,128]{1,0:T(8,128)S(1)}, u32[]{:S(2)}, u32[]{:S(2)}) collective-permute-start(f32[768,128]{1,0:T(8,128)S(1)} %bitcast.11), channel_id=1, source_target_pairs={{0,1},{1,0},{2,3},{3,2},{4,5},{5,4},{6,7},{7,6},{8,9},{9,8},{10,11... | collective-permute-start | bytes 1179656 | tf_op jit(solution)/shard_map/ppermute | solution.py:370
  23.9 1.6 %collective-permute-start.2 = (f32[19,32,128]{2,1,0:T(8,128)S(1)}, f32[19,32,128]{2,1,0:T(8,128)S(1)}, u32[]{:S(2)}, u32[]{:S(2)}) collective-permute-start(f32[19,32,128]{2,1,0:T(8,128)S(1)} %collective-permute-done.1.near), channel_id=1, source_target_pairs={{0,1},{1,0},{2,3},{3,2},{4,5},{5,4},{6,7},{7,6},{8,9},{9,8},{10,11... | collective-permute-start | bytes 933896 | tf_op jit(solution)/shard_map/ppermute | solution.py:368
  27.2 9.7 %collective-permute-start.4 = (f32[3,4,32,128]{3,2,1,0:T(8,128)S(1)}, f32[3,4,32,128]{3,2,1,0:T(8,128)S(1)}, u32[]{:S(2)}, u32[]{:S(2)}) collective-permute-start(f32[3,4,32,128]{3,2,1,0:T(8,128)S(1)} %get-tuple-element.16.edge), channel_id=1, source_target_pairs={{0,2},{3,5},{4,6},{7,9},{8,10},{11,13},{12,14},{2,0},{5,3},{6,4},{... | collective-permute-start | bytes 589832 | tf_op jit(solution)/shard_map/ppermute | solution.py:385
  36.8 1.4 %collective-permute-start.5 = (f32[3,4,32,128]{3,2,1,0:T(8,128)S(1)}, f32[3,4,32,128]{3,2,1,0:T(8,128)S(1)}, u32[]{:S(2)}, u32[]{:S(2)}) collective-permute-start(f32[3,4,32,128]{3,2,1,0:T(8,128)S(1)} %collective-permute-done.4.near), channel_id=1, source_target_pairs={{0,1},{1,0},{2,3},{3,2},{4,5},{5,4},{6,7},{7,6},{8,9},{9,8},{10,11... | collective-permute-start | bytes 589832 | tf_op jit(solution)/shard_map/ppermute | solution.py:386

commit v3 on v2

v3 whole, which is shorter than its diff:
```python
import functools

import jax
import jax.numpy as jnp
from jax import lax
from jax.experimental import pallas as pl
from jax.experimental.pallas import tpu as pltpu
from jax.sharding import PartitionSpec as P

SLAB, CHIP, STEPS, EDGE = 2, 4, 4, 8
NEAR, FAR = 4.0 / 3.0, -1.0 / 12.0
RCV, SRC = 0, 1
SPAN = 3 * SLAB
HALF_NOW = (CHIP + 2 * CHIP) // 2
HALF_OLD = (CHIP + CHIP) // 2
FETCH = 24

VMEM = pl.BlockSpec(memory_space=pltpu.VMEM)
SMEM = pl.BlockSpec(memory_space=pltpu.SMEM)
HBM = pl.BlockSpec(memory_space=pltpu.HBM)


def call(kernel, operands, outs, scratch, scalars, held=(), far_in=False, far_out=()):
    size = sum(4 * o.size for o in operands[scalars:])
    size += sum(4 * functools.reduce(lambda a, b: a * b, s) for s in (*outs, *scratch))
    if far_in:
        operands = [pltpu.with_memory_space_constraint(o, pltpu.HBM) for o in operands]
    return pl.pallas_call(
        kernel,
        out_shape=[jax.ShapeDtypeStruct(s, jnp.float32) for s in outs],
        in_specs=[SMEM] * scalars + [HBM if far_in else VMEM] * (len(operands) - scalars),
        out_specs=[HBM if n in far_out else VMEM for n in range(len(outs))],
        scratch_shapes=[pltpu.VMEM(s, jnp.float32) for s in scratch] + list(held),
        compiler_params=pltpu.CompilerParams(vmem_limit_bytes=size + size // 4 + (8 << 20)),
    )(*operands)


def each(count, rows, body):
    if rows <= 32:
        for i in range(count):
            body(i)
    else:
        lax.fori_loop(0, count, lambda i, _: (body(i), 0)[1], 0)


def blocks(rows):
    size = min(rows, 32)
    return [(b, size) for b in range(0, rows, size)]


def gather(
    src_now, src_old, rcv_now, rcv_old, med, traces, rec_x, wide, loc, traces_in, rec_in, sems
):
    rows, depth = src_now.shape[1:]
    steps, cells = traces.shape[1], loc.shape[1]
    inner = pl.ds(EDGE, rows)
    pairs = [(traces, traces_in), (rec_x, rec_in)]
    for n, own in enumerate((rcv_now, src_now, rcv_old, src_old)):
        pairs.append((own, loc.at[pl.ds(n * SLAB, SLAB)]))
    pairs += [(med.at[k], loc.at[pl.ds((4 + k) * SLAB, SLAB)]) for k in range(3)]
    for n, own in enumerate((src_now, src_old, med.at[0], med.at[1], med.at[2])):
        pairs.append((own, wide.at[pl.ds(n * SLAB, SLAB), inner]))
    copies = [pltpu.make_async_copy(a, b, sems.at[n]) for n, (a, b) in enumerate(pairs)]
    for copy in copies:
        copy.start()
    clear(wide, EDGE, rows)
    for copy in copies[:2]:
        copy.wait()
    lane = lax.broadcasted_iota(jnp.int32, (cells, depth), 1)
    place = lax.broadcasted_iota(jnp.int32, (cells, rec_x.shape[1]), 0)
    surface = jnp.zeros((cells, depth), jnp.float32)
    for h in range(SLAB):
        hit = rec_in[h : h + 1, :] == place
        for s in range(steps):
            column = jnp.sum(jnp.where(hit, traces_in[h, s : s + 1, :], 0.0), axis=1, keepdims=True)
            surface = jnp.where(lane == steps * h + s, column, surface)
    loc[7 * SLAB] = surface
    for copy in copies[2:]:
        copy.wait()


def pack(wide, send):
    for j in range(send.shape[0]):
        chip, core = divmod(j, 2)
        now_at = EDGE + CHIP * chip - CHIP + HALF_NOW * core
        old_at = EDGE + CHIP * chip - SLAB + HALF_OLD * core
        for h in range(SLAB):
            at = FETCH * h
            send[j, at : at + HALF_NOW, :] = wide[h, now_at : now_at + HALF_NOW, :]
            for k in range(4):
                at = FETCH * h + HALF_NOW + HALF_OLD * k
                plane = SLAB * (k + 1) + h
                send[j, at : at + HALF_OLD, :] = wide[plane, old_at : old_at + HALF_OLD, :]


def advance(now, now_at, old, old_at, med, med_at, new, new_pad, count, pad, rows, across, extra):
    depth = now.shape[2]
    lane = lax.broadcasted_iota(jnp.int32, (8, depth), 1)
    weight = [
        jnp.where(lane >= 1, NEAR, 0.0),
        jnp.where(lane < depth - 1, NEAR, 0.0),
        jnp.where(lane >= 2, FAR, 0.0),
        jnp.where(lane < depth - 2, FAR, 0.0),
    ]

    def one(i):
        w = now_at + i
        for b, size in blocks(rows):
            taps = [jnp.concatenate([t] * (size // 8), axis=0) for t in weight]

            def at(plane, shift):
                return now[plane, pad + b + shift : pad + b + shift + size, :]

            here = at(w, 0)
            centre = -2.5 * here
            plane_sum = (
                centre
                + NEAR * (at(w - 1, 0) + at(w + 1, 0))
                + FAR * (at(w - 2, 0) + at(w + 2, 0))
            )
            row_sum = (
                centre
                + NEAR * (at(w, -1) + at(w, 1))
                + FAR * (at(w, -2) + at(w, 2))
            )
            depth_sum = (
                centre
                + taps[0] * pltpu.roll(here, 1, 1)
                + taps[1] * pltpu.roll(here, depth - 1, 1)
                + taps[2] * pltpu.roll(here, 2, 1)
                + taps[3] * pltpu.roll(here, depth - 2, 1)
            )
            m = [med(k, med_at + i)[b : b + size, :] for k in range(3)]
            value = 2.0 * here - old(old_at + i)[b : b + size, :]
            value = value + m[across] * plane_sum + m[1 - across] * row_sum + m[2] * depth_sum
            if extra is not None:
                value = value + extra(i, b, size)
            new[i, new_pad + b : new_pad + b + size, :] = value

    each(count, rows, one)


def shoot(new, pad, first, count, plane, row, depth_at, amount):
    local = plane - first

    @pl.when((local >= 0) & (local < count))
    def _():
        lane = lax.broadcasted_iota(jnp.int32, (1, new.shape[2]), 1)
        spot = (pl.ds(local, 1), pl.ds(pad + row, 1), slice(None))
        new[spot] = new[spot] + jnp.where(lane == depth_at, -amount, 0.0)[None]


def surface_at(surf, first, step, steps):
    def extra(i, b, size):
        held = surf(first + i // SLAB)[b : b + size, :]
        depth = held.shape[1]
        lane = lax.broadcasted_iota(jnp.int32, (size, depth), 1)
        total = jnp.zeros_like(held)
        shift = (i % SLAB) * steps + step
        if isinstance(shift, int):
            return jnp.where(lane == 0, pltpu.roll(held, (depth - shift) % depth, 1), 0.0)
        for s in range(SLAB):
            moved = pltpu.roll(held, (depth - s * steps - step) % depth, 1)
            total = jnp.where((lane == 0) & (i % SLAB == s), moved, total)
        return total

    return extra


def clear(window, pad, rows):
    count, _, depth = window.shape
    zero = jnp.zeros((count, pad, depth), jnp.float32)
    window[:, 0:pad, :] = zero
    window[:, pad + rows :, :] = zero


def place(window, at, pad, value):
    window[at, pad : pad + value.shape[0], :] = value


def own_planes(refs, window, pad, base, at, core):
    for src, q in ((refs[0], core), (refs[1], 1 - core)):
        for p in range(SLAB):
            place(window, base + SLAB * q + p, pad, src[at + p])


def side_planes(refs, window, pad, base, ats, core):
    for src, side in ((refs[0], core), (refs[1], 1 - core)):
        for n, at in enumerate(ats):
            for p in range(SLAB):
                place(window, base * side + SLAB * n + p, pad, src[at + p])


def now_window(refs, window, kind, core):
    own_planes(refs[:2], window, EDGE, CHIP, SLAB * kind, core)
    side_planes(refs[2:], window, EDGE, 2 * CHIP, (SLAB * kind, SLAB * (2 + kind)), core)


def rim_window(refs, window, kind, core):
    own_planes(refs[:2], window, 0, SLAB, SLAB * (2 + kind), core)
    side_planes(refs[2:], window, 0, SLAB + CHIP, (SLAB * (4 + kind),), core)


def two_steps(now, old, med, new, edge, across, surface, shots):
    rows = edge.shape[1]
    count = old.shape[0]
    held = count // SLAB

    def medium(k, i):
        return med[k][i]

    extra = [None if surface is None else surface_at(lambda i: surface[i], n, n, STEPS) for n in range(2)]
    clear(now, EDGE, rows)
    clear(new, EDGE, rows)
    advance(now, SLAB, lambda i: old[i], 0, medium, 0, new, EDGE, count, EDGE, rows, across, extra[0])
    if shots:
        first, plane, row, deep, amounts = shots
        shoot(new, EDGE, first, count, plane, row, deep, amounts[0])
    advance(
        new, SLAB, lambda i: now[CHIP + i, EDGE : EDGE + rows, :], 0, medium, SLAB, edge, 0,
        CHIP, EDGE, rows, across, extra[1],
    )
    if shots:
        shoot(edge, 0, first + SLAB, CHIP, plane, row, deep, amounts[1])


def fetched(pair, window, pad, count, at, core):
    rows = window.shape[1] - 2 * pad
    for src, q in ((pair[0], core), (pair[1], 1 - core)):
        for p in range(count):
            place(window, count * q + p, pad, src[pl.ds(at + p, rows, stride=FETCH), :])


def first_y(
    where, shot, wavelet, loc, sib, near, near_sib, got, got_sib, edge, carry,
    now_r, now_s, old_r, old_s, med_0, med_1, med_2, surf, new_r, new_s,
):
    core, chip = where[0], where[1]
    refs = (loc, sib, near, near_sib)
    rows = loc.shape[1]
    med = (med_0, med_1, med_2)
    now_window(refs, now_r, RCV, core)
    rim_window(refs, old_r, RCV, core)
    for k in range(3):
        rim_window(refs, med[k], 2 + k, core)
    for n, ref in enumerate(refs):
        flip = core if n % 2 == 0 else 1 - core
        surf[1 + flip if n < 2 else 3 * flip] = ref[ref.shape[0] - 1]
    fetched((got, got_sib), now_s, EDGE, HALF_NOW, 0, core)
    fetched((got, got_sib), old_s, 0, HALF_OLD, HALF_NOW, core)
    two_steps(now_r, old_r, med, new_r, edge.at[0], 1, surf, None)
    shots = (CHIP * chip - SLAB, shot[1], shot[0], shot[2], (wavelet[0], wavelet[1]))
    two_steps(now_s, old_s, med, new_s, edge.at[1], 1, None, shots)
    for i in range(SPAN):
        at = SLAB * core + i
        carry[i] = new_r[at, EDGE : EDGE + rows, :]
        carry[SPAN + i] = new_s[at, EDGE : EDGE + rows, :]
        for k in range(3):
            carry[SPAN * (2 + k) + i] = med[k][at]
    for i in range(3):
        carry[SPAN * 5 + i] = surf[core + i]


def first_x(
    where, shot, wavelet, loc, sib, near, near_sib, got, got_sib, edge, carry,
    now, old, med_0, med_1, med_2, new,
):
    core, chip = where[0], where[1]
    refs = (loc, sib, near, near_sib)
    rows = loc.shape[1]
    med = (med_0, med_1, med_2)
    now_window(refs, now, SRC, core)
    rim_window(refs, old, SRC, core)
    for k in range(3):
        fetched((got, got_sib), med[k], 0, HALF_OLD, HALF_NOW + HALF_OLD * (k + 1), core)
    shots = (CHIP * chip - SLAB, shot[0], shot[1], shot[2], (wavelet[0], wavelet[1]))
    two_steps(now, old, med, new, edge.at[0], 0, None, shots)
    for i in range(SPAN):
        at = SLAB * core + i
        carry[i] = new[at, EDGE : EDGE + rows, :]
        for k in range(3):
            carry[SPAN * (1 + k) + i] = med[k][at]


def last_steps(where, edges, n, now, old, med, new, end, across, surface, shots):
    core = where[0]
    edge, near, near_sib = edges
    rows = edge.shape[2]
    pad = (now.shape[1] - rows) // 2
    for window in (now, new, end):
        clear(window, pad, rows)
    for p in range(CHIP):
        place(now, CHIP + p, pad, edge[n, p])
        for src, side in ((near, core), (near_sib, 1 - core)):
            plane = jnp.where(where[2 + side] == 1, src[n, p], 0.0)
            place(now, 2 * CHIP * side + p, pad, plane)
    extra = [None if surface is None else surface_at(surface, s, 2 + s, STEPS) for s in range(2)]
    advance(now, SLAB * core + SLAB, old, 0, med, 0, new, pad, SPAN, pad, rows, across, extra[0])
    if shots:
        first, plane, row, deep, amounts = shots
        shoot(new, pad, first, SPAN, plane, row, deep, amounts[0])

    def older(i):
        return now[CHIP + SLAB * core + i, pad : pad + rows, :]

    advance(new, SLAB, older, 0, med, SLAB, end, pad, SLAB, pad, rows, across, extra[1])
    if shots:
        shoot(end, pad, first + SLAB, SLAB, plane, row, deep, amounts[1])


def finish(end, new, following, prior, sems, at):
    rows = following.shape[1]
    inner = pl.ds((end.shape[1] - rows) // 2, rows)
    copies = [
        pltpu.make_async_copy(end.at[:, inner], following, sems.at[at]),
        pltpu.make_async_copy(new.at[pl.ds(SLAB, SLAB), inner], prior, sems.at[at + 1]),
    ]
    for copy in copies:
        copy.start()
    return copies


def second_half(
    where, shot, wavelet, lag_order, edge, near, near_sib, carry, edge_x, near_x, sib_x, carry_x,
    src_next, src_prior, rcv_next, rcv_prior, image,
    now_r, now_s, now_x, new_r, new_s, new_x, end_r, end_s, end_x, planes, slot_of, sems,
):
    rows, depth = carry.shape[1:]
    lags = lag_order.shape[0]
    half = (lags - 1) // 2
    pad = (now_r.shape[1] - rows) // 2
    core, chip = where[0], where[1]

    def note(k, _):
        slot_of[lag_order[k]] = k
        return 0

    lax.fori_loop(0, lags, note, 0)

    def med(k, i):
        return carry[SPAN * (2 + k) + i]

    edges = (edge, near, near_sib)
    last_steps(
        where, edges, 0, now_r, lambda i: carry[i], med, new_r, end_r, 1,
        lambda i: carry[SPAN * 5 + i], None,
    )
    copies = finish(end_r, new_r, rcv_next, rcv_prior, sems, lags)
    first = CHIP * chip + SLAB * core - SLAB
    last_steps(
        where, edges, 1, now_s, lambda i: carry[SPAN + i], med, new_s, end_s, 1, None,
        (first, shot[1], shot[0], shot[2], (wavelet[2], wavelet[3])),
    )
    last_steps(
        where, (edge_x, near_x, sib_x), 0, now_x, lambda i: carry_x[i],
        lambda k, i: carry_x[SPAN * (1 + k) + i], new_x, end_x, 0, None,
        (first, shot[0], shot[1], shot[2], (wavelet[2], wavelet[3])),
    )
    copies += finish(end_x, new_x, src_next, src_prior, sems, lags + 2)
    own = CHIP + SLAB * core
    for slot in range(lags):
        lag = slot - half
        for p in range(SLAB):
            for b in range(0, rows, 8):
                if b + 8 <= abs(lag) or b >= rows - abs(lag):
                    planes[slot, p, b : b + 8, :] = jnp.zeros((8, depth), jnp.float32)
                    continue
                back, ahead = pad + b - lag, pad + b + lag
                planes[slot, p, b : b + 8, :] = (
                    now_s[own + p, back : back + 8, :] * now_r[own + p, ahead : ahead + 8, :]
                    + end_s[p, back : back + 8, :] * end_r[p, ahead : ahead + 8, :]
                )
        copies.append(
            pltpu.make_async_copy(planes.at[slot], image.at[slot_of[slot]], sems.at[slot])
        )
        copies[-1].start()
    for copy in copies:
        copy.wait()


def on_device(src_now, src_old, rcv_now, rcv_old, medium, wavelet, shot, traces, rec_x, lag_order):
    devices = lax.axis_size("wide")
    chips = devices // 2
    slab, rows, depth = src_now.shape
    assert slab == SLAB and rcv_now.shape == (SLAB, depth, rows) and wavelet.shape[0] == STEPS
    assert rows % 8 == 0 and rows == SLAB * devices
    lags = lag_order.shape[0]
    half = (lags - 1) // 2
    device = lax.axis_index("wide")
    chip, core = device // 2, device % 2
    last = chips - 1
    turning = chip == jnp.where(core == 0, last, 0)
    where = jnp.stack([core, chip, chip > 0, chip < last]).astype(jnp.int32)
    swap = [(i, i ^ 1) for i in range(devices)]
    order = [*range(0, devices, 2), *range(devices - 1, 0, -2)]
    ring = list(zip(order, order[1:] + order[:1]))

    def turned(x):
        return jnp.swapaxes(x, -1, -2)

    rcv_now, rcv_old, medium, traces = map(turned, (rcv_now, rcv_old, medium, traces))
    wide, loc = call(
        gather,
        (src_now, src_old, rcv_now, rcv_old, medium, traces, rec_x),
        [(5 * SLAB, rows + 2 * EDGE, depth), (7 * SLAB + 1, rows, depth)],
        [traces.shape],
        0,
        [pltpu.VMEM(rec_x.shape, jnp.int32), pltpu.SemaphoreType.DMA((14,))],
        far_in=True,
    )
    (send,) = call(pack, (wide,), [(devices, SLAB * FETCH, depth)], [], 0)
    got = lax.all_to_all(send, "wide", 0, 0, tiled=True).reshape(-1, depth)
    sib = lax.ppermute(loc, "wide", swap)
    low, high = jnp.where(core == 0, loc, sib), jnp.where(core == 0, sib, loc)
    rim = jnp.where(core == 0, high[2 * SLAB :], low[2 * SLAB :])
    ours = jnp.concatenate([low[: 2 * SLAB], high[: 2 * SLAB], rim])
    near = lax.ppermute(jnp.where(turning, 0.0, ours), "wide", ring)
    near_sib = lax.ppermute(near, "wide", swap)
    got_sib = lax.ppermute(got, "wide", swap)

    window, narrow = 3 * CHIP, 2 * CHIP
    padded, plain = (window, rows + 2 * EDGE, depth), (narrow, rows, depth)
    edge_y, carry_y = call(
        first_y,
        (where, shot, wavelet, loc, sib, near, near_sib, got, got_sib),
        [(2, CHIP, rows, depth), (SPAN * 5 + 3, rows, depth)],
        [padded] * 2 + [plain] * 5 + [(4, rows, depth)] + [(narrow, *padded[1:])] * 2,
        3,
    )
    mid_y = lax.ppermute(edge_y, "wide", ring)
    mid_y_sib = lax.ppermute(mid_y, "wide", swap)
    edge_x, carry_x = call(
        first_x,
        (where, shot, wavelet, loc, sib, near, near_sib, got, got_sib),
        [(1, CHIP, rows, depth), (SPAN * 4, rows, depth)],
        [padded] + [plain] * 4 + [(narrow, *padded[1:])],
        3,
    )
    mid_x = lax.ppermute(edge_x, "wide", ring)
    mid_x_sib = lax.ppermute(mid_x, "wide", swap)

    field = (SLAB, rows, depth)
    pad = -(-max(half, 2) // 8) * 8
    padded = (rows + 2 * pad, depth)
    src_next, src_prior, rcv_next, rcv_prior, image = call(
        second_half,
        (where, shot, wavelet, lag_order, edge_y, mid_y, mid_y_sib, carry_y)
        + (edge_x, mid_x, mid_x_sib, carry_x),
        [field] * 4 + [(lags, *field)],
        [(window, *padded)] * 3 + [(SPAN, *padded)] * 3 + [(SLAB, *padded)] * 3 + [(lags, *field)],
        4,
        [pltpu.SMEM((lags,), jnp.int32), pltpu.SemaphoreType.DMA((lags + 4,))],
        far_out=range(5),
    )
    return src_next, src_prior, turned(rcv_next), turned(rcv_prior), turned(image)


def solution(mesh):
    return jax.shard_map(
        on_device,
        mesh=mesh,
        in_specs=(
            P("wide", "shots", None),
            P("wide", "shots", None),
            P("wide", "shots", None),
            P("wide", "shots", None),
            P(None, "wide", None, None),
            P(),
            P("shots"),
            P("wide", "shots", None),
            P("wide", "shots"),
            P(),
        ),
        out_specs=(
            P("wide", "shots", None),
            P("wide", "shots", None),
            P("wide", "shots", None),
            P("wide", "shots", None),
            P("shots", "wide", None, None),
        ),
        check_vma=False,
    )
```

time: 42.4 us -> 38.4 us (0.906)
  starting transfers between devices: 15.8 us -> 13.4 us
  waiting for transfers between devices: 17.9 us -> 16.4 us
    ppermute x2 -> x5, starting transfers between devices: 8.17 us -> 5.78 us  [the longest x1 2.55 us: on_device(): mid_y = lax.ppermute(edge_y, 'wide', ring)]
    ppermute x2 -> x5, waiting for transfers between devices: 6.74 us -> 4.8 us  [the longest x1 2.35 us: on_device(): mid_y = lax.ppermute(edge_y, 'wide', ring)]
    all_to_all x1, waiting for transfers between devices: 8.17 us -> 10 us  [on_device(): got = lax.all_to_all(send, 'wide', 0, 0, tiled=True).reshape(-1, depth)]
    ppermute x2 -> x1, waiting for transfers between devices: 2.97 us -> 1.53 us  [on_device(): near_sib = lax.ppermute(near, 'wide', swap)]
    pallas_call x3 -> x5, Pallas kernels: 7.23 us -> 7.1 us  [call(): pl.pallas_call(kernel, out_shape=[jax.ShapeDtypeStruct(s, jnp.float32) fo...]
  transfers between devices with their start and end apart: 7 -> 9, of which waited for: 5 -> 6; matrix products, arithmetic and copies ran while one was open for 0% -> 0% of each run, Pallas kernels for 0% -> 5%
where the time goes in v3:
time: 38.4 us; the launch traced here: 37.9 us
  waiting for transfers between devices  16.4 us (43%)
  starting transfers between devices  13.4 us (35%)
  Pallas kernels  7.1 us (18%)
  between operations  0.78 us (2%)
    all_to_all x1, waiting for transfers between devices, on_device(): got = lax.all_to_all(send, 'wide', 0, 0, tiled=True).reshape(-1, depth)  10 us
    pallas_call x5, Pallas kernels, call(): pl.pallas_call(kernel, out_shape=[jax.ShapeDtypeStruct(s, jnp.float32) fo...  7.1 us
    all_to_all x1, starting transfers between devices, on_device(): got = lax.all_to_all(send, 'wide', 0, 0, tiled=True).reshape(-1, depth)  7.02 us
    ppermute x1, starting transfers between devices, on_device(): mid_y = lax.ppermute(edge_y, 'wide', ring)  2.55 us
    ppermute x1, waiting for transfers between devices, on_device(): mid_y = lax.ppermute(edge_y, 'wide', ring)  2.35 us
    ppermute x1, starting transfers between devices, on_device(): near = lax.ppermute(jnp.where(turning, 0.0, ours), 'wide', ring)  1.95 us
    ppermute x1, waiting for transfers between devices, on_device(): near_sib = lax.ppermute(near, 'wide', swap)  1.53 us
    ppermute x1, starting transfers between devices, on_device(): mid_x = lax.ppermute(edge_x, 'wide', ring)  1.28 us
  transfers between devices with their start and end apart: 9, of which 6 were waited for; matrix products, arithmetic and copies ran while one was open for 0% of the time, Pallas kernels for 5%

profile of v3, /device:TPU:0, one launch (start us, length us, event | category | flops | bytes accessed | tf_op | source)
XLA Modules:
  0.0 37.9 jit_solution(4689005961503612012)
XLA Ops:
  0.6 1.1 %shard_map.137 = (f32[10,48,128]{2,1,0:T(8,128)S(1)}, f32[15,32,128]{2,1,0:T(8,128)S(1)}) custom-call(f32[2,32,128]{2,1,0:T(8,128)} %src_now.1, f32[2,32,128]{2,1,0:T(8,128)} %src_old.1, f32[2,32,128]{2,1,0:T(8,128)} %bitcast.16, f32[2,32,128]{2,1,0:T(8,128)} %bitcast.17, f32[3,2,32,128]{3,2,1,0:T(8,128)} %bitcast.15, f32[2,4,64]{2,1,0:T(4,128)} %bitcast.18, ...), custom_call_target="tpu_custom_call" | custom-call | tf_op jit(solution)/shard_map/pallas_call | solution.py:28
  1.8 0.5 %collective-permute-start = (f32[15,32,128]{2,1,0:T(8,128)S(1)}, f32[15,32,128]{2,1,0:T(8,128)S(1)}, u32[]{:S(2)}, u32[]{:S(2)}) collective-permute-start(f32[15,32,128]{2,1,0:T(8,128)S(1)} %get-tuple-element.16.loc), channel_id=1, source_target_pairs={{0,1},{1,0},{2,3},{3,2},{4,5},{5,4},{6,7},{7,6},{8,9},{9,8},{10,11... | collective-permute-start | bytes 737288 | tf_op jit(solution)/shard_map/ppermute | solution.py:413
  2.3 0.8 %shard_map.138 = f32[16,48,128]{2,1,0:T(8,128)} custom-call(f32[10,48,128]{2,1,0:T(8,128)S(1)} %get-tuple-element.17.wide), custom_call_target="tpu_custom_call" | custom-call | tf_op jit(solution)/shard_map/pallas_call | solution.py:28
  3.1 7.0 %all-to-all-start = ((f32[16,48,128]{2,1,0:T(8,128)}), f32[16,48,128]{2,1,0:T(8,128)S(1)}, u32[]{:S(2)}, u32[]{:S(2)}) async-start(f32[16,48,128]{2,1,0:T(8,128)} %shard_map.138), calls=%async_computation | async-start | bytes 786432 | tf_op jit(solution)/shard_map/all_to_all | solution.py:412
  10.1 0.0 copy-start
  10.1 0.0 copy-start.1
  10.1 0.0 collective-permute-done.sib
  10.3 2.0 %collective-permute-start.1 = (f32[19,32,128]{2,1,0:T(8,128)S(1)}, f32[19,32,128]{2,1,0:T(8,128)S(1)}, u32[]{:S(2)}, u32[]{:S(2)}) collective-permute-start(f32[19,32,128]{2,1,0:T(8,128)S(1)} %maximum_select_fusion), channel_id=1, source_target_pairs={{0,2},{2,4},{4,6},{6,8},{8,10},{10,12},{12,14},{14,15},{15,13},{13... | collective-permute-start | bytes 933896 | tf_op jit(solution)/shard_map/ppermute | solution.py:417
  12.2 10.0 %all-to-all-done = f32[16,48,128]{2,1,0:T(8,128)S(1)} async-done(((f32[16,48,128]{2,1,0:T(8,128)}), f32[16,48,128]{2,1,0:T(8,128)S(1)}, u32[]{:S(2)}, u32[]{:S(2)}) %all-to-all-start) | async-done | bytes 393248 | tf_op jit(solution)/shard_map/all_to_all | solution.py:412
  22.3 0.1 collective-permute-start.3
  22.4 0.5 %collective-permute-done.1.near = f32[19,32,128]{2,1,0:T(8,128)S(1)} collective-permute-done((f32[19,32,128]{2,1,0:T(8,128)S(1)}, f32[19,32,128]{2,1,0:T(8,128)S(1)}, u32[]{:S(2)}, u32[]{:S(2)}) %collective-permute-start.1) | collective-permute-done | bytes 311328 | tf_op jit(solution)/shard_map/ppermute | solution.py:417
  22.9 0.0 collective-permute-start.2
  22.9 0.1 pad_add_fusion.where
  23.0 1.5 %collective-permute-done.2.near_sib = f32[19,32,128]{2,1,0:T(8,128)S(1)} collective-permute-done((f32[19,32,128]{2,1,0:T(8,128)S(1)}, f32[19,32,128]{2,1,0:T(8,128)S(1)}, u32[]{:S(2)}, u32[]{:S(2)}) %collective-permute-start.2) | collective-permute-done | bytes 311328 | tf_op jit(solution)/shard_map/ppermute | solution.py:418
  24.5 0.0 collective-permute-done.3.got_sib
  24.5 0.0 copy-done
  24.5 0.0 copy-done.1
  24.5 1.2 %shard_map.139 = (f32[2,4,32,128]{3,2,1,0:T(8,128)S(1)}, f32[33,32,128]{2,1,0:T(8,128)S(1)}) custom-call(s32[4]{0:T(128)S(1)} %pad_add_fusion.where, s32[3]{0:T(128)S(1)} %copy-done, f32[4]{0:T(128)S(1)} %copy-done.1, f32[15,32,128]{2,1,0:T(8,128)S(1)} %get-tuple-element.16.loc, f32[15,32,128]{2,1,0:T(8,128)S(1)} %collective-permute-done.sib, ...), custom_call_target="tpu_custom_call" | custom-call | tf_op jit(solution)/shard_map/pallas_call | solution.py:28
  25.7 0.0 copy-start.2
  25.8 2.5 %collective-permute-start.4 = (f32[2,4,32,128]{3,2,1,0:T(8,128)S(1)}, f32[2,4,32,128]{3,2,1,0:T(8,128)S(1)}, u32[]{:S(2)}, u32[]{:S(2)}) collective-permute-start(f32[2,4,32,128]{3,2,1,0:T(8,128)S(1)} %get-tuple-element.18.edge), channel_id=1, source_target_pairs={{0,2},{2,4},{4,6},{6,8},{8,10},{10,12},{12,14},{14,15},{15,13},{13... | collective-permute-start | bytes 393224 | tf_op jit(solution)/shard_map/ppermute | solution.py:430
  28.3 1.0 %shard_map.140 = (f32[1,4,32,128]{3,2,1,0:T(8,128)S(1)}, f32[24,32,128]{2,1,0:T(8,128)S(1)}) custom-call(s32[4]{0:T(128)S(1)} %pad_add_fusion.where, s32[3]{0:T(128)S(1)} %copy-done, f32[4]{0:T(128)S(1)} %copy-done.1, f32[15,32,128]{2,1,0:T(8,128)S(1)} %get-tuple-element.16.loc, f32[15,32,128]{2,1,0:T(8,128)S(1)} %collective-permute-done.sib, ...), custom_call_target="tpu_custom_call" | custom-call | tf_op jit(solution)/shard_map/pallas_call | solution.py:28
  29.3 1.3 %collective-permute-start.6 = (f32[1,4,32,128]{3,2,1,0:T(8,128)S(1)}, f32[1,4,32,128]{3,2,1,0:T(8,128)S(1)}, u32[]{:S(2)}, u32[]{:S(2)}) collective-permute-start(f32[1,4,32,128]{3,2,1,0:T(8,128)S(1)} %get-tuple-element.20.edge_x), channel_id=1, source_target_pairs={{0,2},{2,4},{4,6},{6,8},{8,10},{10,12},{12,14},{14,15},{15,13},{13... | collective-permute-start | bytes 196616 | tf_op jit(solution)/shard_map/ppermute | solution.py:439
  30.5 2.4 %collective-permute-done.4.near = f32[2,4,32,128]{3,2,1,0:T(8,128)S(1)} collective-permute-done((f32[2,4,32,128]{3,2,1,0:T(8,128)S(1)}, f32[2,4,32,128]{3,2,1,0:T(8,128)S(1)}, u32[]{:S(2)}, u32[]{:S(2)}) %collective-permute-start.4) | collective-permute-done | bytes 131104 | tf_op jit(solution)/shard_map/ppermute | solution.py:430
  32.9 0.0 collective-permute-start.5
  32.9 0.7 %collective-permute-done.6.near_x = f32[1,4,32,128]{3,2,1,0:T(8,128)S(1)} collective-permute-done((f32[1,4,32,128]{3,2,1,0:T(8,128)S(1)}, f32[1,4,32,128]{3,2,1,0:T(8,128)S(1)}, u32[]{:S(2)}, u32[]{:S(2)}) %collective-permute-start.6) | collective-permute-done | bytes 65568 | tf_op jit(solution)/shard_map/ppermute | solution.py:439
  33.6 0.0 collective-permute-start.7
  33.6 1.3 %collective-permute-done.7.sib_x = f32[1,4,32,128]{3,2,1,0:T(8,128)S(1)} collective-permute-done((f32[1,4,32,128]{3,2,1,0:T(8,128)S(1)}, f32[1,4,32,128]{3,2,1,0:T(8,128)S(1)}, u32[]{:S(2)}, u32[]{:S(2)}) %collective-permute-start.7) | collective-permute-done | bytes 65568 | tf_op jit(solution)/shard_map/ppermute | solution.py:440
  34.9 0.0 collective-permute-done.5.near_sib
  34.9 0.0 copy-done.2
  34.9 3.0 %shard_map.141 = (f32[2,32,128]{2,1,0:T(8,128)}, f32[2,32,128]{2,1,0:T(8,128)}, f32[2,32,128]{2,1,0:T(8,128)}, f32[2,32,128]{2,1,0:T(8,128)}, f32[33,2,32,128]{3,2,1,0:T(8,128)}) custom-call(s32[4]{0:T(128)S(1)} %pad_add_fusion.where, s32[3]{0:T(128)S(1)} %copy-done, f32[4]{0:T(128)S(1)} %copy-done.1, s32[33]{0:T(128)S(1)} %copy-done.2, ...), custom_call_target="tpu_custom_call" | custom-call | tf_op jit(solution)/shard_map/pallas_call | solution.py:28
  (5 shorter events, 0.1 us)
Async XLA Ops:
  1.8 8.4 %collective-permute-start = (f32[15,32,128]{2,1,0:T(8,128)S(1)}, f32[15,32,128]{2,1,0:T(8,128)S(1)}, u32[]{:S(2)}, u32[]{:S(2)}) collective-permute-start(f32[15,32,128]{2,1,0:T(8,128)S(1)} %get-tuple-element.16.loc), channel_id=1, source_target_pairs={{0,1},{1,0},{2,3},{3,2},{4,5},{5,4},{6,7},{7,6},{8,9},{9,8},{10,11... | collective-permute-start | bytes 737288 | tf_op jit(solution)/shard_map/ppermute | solution.py:413
  3.1 19.2 %all-to-all-start = ((f32[16,48,128]{2,1,0:T(8,128)}), f32[16,48,128]{2,1,0:T(8,128)S(1)}, u32[]{:S(2)}, u32[]{:S(2)}) async-start(f32[16,48,128]{2,1,0:T(8,128)} %shard_map.138), calls=%async_computation | async-start | bytes 786432 | tf_op jit(solution)/shard_map/all_to_all | solution.py:412
  10.1 14.4 %copy-start = (s32[3]{0:T(128)S(1)}, s32[3]{0:T(128)}, u32[]{:S(2)}) copy-start(s32[3]{0:T(128)} %shot.5) | copy-start | bytes 40
  10.1 14.4 %copy-start.1 = (f32[4]{0:T(128)S(1)}, f32[4]{0:T(128)}, u32[]{:S(2)}) copy-start(f32[4]{0:T(128)} %wavelet.5) | copy-start | bytes 52
  10.3 12.6 %collective-permute-start.1 = (f32[19,32,128]{2,1,0:T(8,128)S(1)}, f32[19,32,128]{2,1,0:T(8,128)S(1)}, u32[]{:S(2)}, u32[]{:S(2)}) collective-permute-start(f32[19,32,128]{2,1,0:T(8,128)S(1)} %maximum_select_fusion), channel_id=1, source_target_pairs={{0,2},{2,4},{4,6},{6,8},{8,10},{10,12},{12,14},{14,15},{15,13},{13... | collective-permute-start | bytes 933896 | tf_op jit(solution)/shard_map/ppermute | solution.py:417
  22.3 2.2 %collective-permute-start.3 = (f32[768,128]{1,0:T(8,128)S(1)}, f32[768,128]{1,0:T(8,128)S(1)}, u32[]{:S(2)}, u32[]{:S(2)}) collective-permute-start(f32[768,128]{1,0:T(8,128)S(1)} %bitcast.12), channel_id=1, source_target_pairs={{0,1},{1,0},{2,3},{3,2},{4,5},{5,4},{6,7},{7,6},{8,9},{9,8},{10,11... | collective-permute-start | bytes 1179656 | tf_op jit(solution)/shard_map/ppermute | solution.py:419
  22.9 1.6 %collective-permute-start.2 = (f32[19,32,128]{2,1,0:T(8,128)S(1)}, f32[19,32,128]{2,1,0:T(8,128)S(1)}, u32[]{:S(2)}, u32[]{:S(2)}) collective-permute-start(f32[19,32,128]{2,1,0:T(8,128)S(1)} %collective-permute-done.1.near), channel_id=1, source_target_pairs={{0,1},{1,0},{2,3},{3,2},{4,5},{5,4},{6,7},{7,6},{8,9},{9,8},{10,11... | collective-permute-start | bytes 933896 | tf_op jit(solution)/shard_map/ppermute | solution.py:418
  25.7 9.1 %copy-start.2 = (s32[33]{0:T(128)S(1)}, s32[33]{0:T(128)}, u32[]{:S(2)}) copy-start(s32[33]{0:T(128)} %lag_order.1) | copy-start | bytes 400
  25.8 7.1 %collective-permute-start.4 = (f32[2,4,32,128]{3,2,1,0:T(8,128)S(1)}, f32[2,4,32,128]{3,2,1,0:T(8,128)S(1)}, u32[]{:S(2)}, u32[]{:S(2)}) collective-permute-start(f32[2,4,32,128]{3,2,1,0:T(8,128)S(1)} %get-tuple-element.18.edge), channel_id=1, source_target_pairs={{0,2},{2,4},{4,6},{6,8},{8,10},{10,12},{12,14},{14,15},{15,13},{13... | collective-permute-start | bytes 393224 | tf_op jit(solution)/shard_map/ppermute | solution.py:430
  29.3 4.3 %collective-permute-start.6 = (f32[1,4,32,128]{3,2,1,0:T(8,128)S(1)}, f32[1,4,32,128]{3,2,1,0:T(8,128)S(1)}, u32[]{:S(2)}, u32[]{:S(2)}) collective-permute-start(f32[1,4,32,128]{3,2,1,0:T(8,128)S(1)} %get-tuple-element.20.edge_x), channel_id=1, source_target_pairs={{0,2},{2,4},{4,6},{6,8},{8,10},{10,12},{12,14},{14,15},{15,13},{13... | collective-permute-start | bytes 196616 | tf_op jit(solution)/shard_map/ppermute | solution.py:439
  32.9 2.0 %collective-permute-start.5 = (f32[2,4,32,128]{3,2,1,0:T(8,128)S(1)}, f32[2,4,32,128]{3,2,1,0:T(8,128)S(1)}, u32[]{:S(2)}, u32[]{:S(2)}) collective-permute-start(f32[2,4,32,128]{3,2,1,0:T(8,128)S(1)} %collective-permute-done.4.near), channel_id=1, source_target_pairs={{0,1},{1,0},{2,3},{3,2},{4,5},{5,4},{6,7},{7,6},{8,9},{9,8},{10,11... | collective-permute-start | bytes 393224 | tf_op jit(solution)/shard_map/ppermute | solution.py:431
  33.6 1.3 %collective-permute-start.7 = (f32[1,4,32,128]{3,2,1,0:T(8,128)S(1)}, f32[1,4,32,128]{3,2,1,0:T(8,128)S(1)}, u32[]{:S(2)}, u32[]{:S(2)}) collective-permute-start(f32[1,4,32,128]{3,2,1,0:T(8,128)S(1)} %collective-permute-done.6.near_x), channel_id=1, source_target_pairs={{0,1},{1,0},{2,3},{3,2},{4,5},{5,4},{6,7},{7,6},{8,9},{9,8},{10,11... | collective-permute-start | bytes 196616 | tf_op jit(solution)/shard_map/ppermute | solution.py:440

commit v4 on v3

--- a/solution.py
+++ b/solution.py
@@ -16,23 +16,26 @@
 FETCH = 24
 
 VMEM = pl.BlockSpec(memory_space=pltpu.VMEM)
-SMEM = pl.BlockSpec(memory_space=pltpu.SMEM)
 HBM = pl.BlockSpec(memory_space=pltpu.HBM)
 
 
-def call(kernel, operands, outs, scratch, scalars, held=(), far_in=False, far_out=()):
-    size = sum(4 * o.size for o in operands[scalars:])
+def call(kernel, operands, outs, scratch, held=(), far=0, far_out=()):
+    size = sum(4 * o.size for o in operands)
     size += sum(4 * functools.reduce(lambda a, b: a * b, s) for s in (*outs, *scratch))
-    if far_in:
-        operands = [pltpu.with_memory_space_constraint(o, pltpu.HBM) for o in operands]
+    distant = [pltpu.with_memory_space_constraint(o, pltpu.HBM) for o in operands[:far]]
     return pl.pallas_call(
         kernel,
         out_shape=[jax.ShapeDtypeStruct(s, jnp.float32) for s in outs],
-        in_specs=[SMEM] * scalars + [HBM if far_in else VMEM] * (len(operands) - scalars),
+        in_specs=[HBM] * far + [VMEM] * (len(operands) - far),
         out_specs=[HBM if n in far_out else VMEM for n in range(len(outs))],
         scratch_shapes=[pltpu.VMEM(s, jnp.float32) for s in scratch] + list(held),
         compiler_params=pltpu.CompilerParams(vmem_limit_bytes=size + size // 4 + (8 << 20)),
-    )(*operands)
+    )(*distant, *operands[far:])
+
+
+def position():
+    device = lax.axis_index("wide")
+    return lax.rem(device, 2), lax.div(device, 2)
 
 
 def each(count, rows, body):
@@ -49,12 +52,13 @@
 
 
 def gather(
-    src_now, src_old, rcv_now, rcv_old, med, traces, rec_x, wide, loc, traces_in, rec_in, sems
+    src_now, src_old, rcv_now, rcv_old, med, traces, rec_x, shot, wavelet,
+    wide, loc, amount, spot, traces_in, rec_in, shot_in, wavelet_in, sems,
 ):
     rows, depth = src_now.shape[1:]
     steps, cells = traces.shape[1], loc.shape[1]
     inner = pl.ds(EDGE, rows)
-    pairs = [(traces, traces_in), (rec_x, rec_in)]
+    pairs = [(traces, traces_in), (rec_x, rec_in), (shot, shot_in), (wavelet, wavelet_in)]
     for n, own in enumerate((rcv_now, src_now, rcv_old, src_old)):
         pairs.append((own, loc.at[pl.ds(n * SLAB, SLAB)]))
     pairs += [(med.at[k], loc.at[pl.ds((4 + k) * SLAB, SLAB)]) for k in range(3)]
@@ -75,7 +79,20 @@
             column = jnp.sum(jnp.where(hit, traces_in[h, s : s + 1, :], 0.0), axis=1, keepdims=True)
             surface = jnp.where(lane == steps * h + s, column, surface)
     loc[7 * SLAB] = surface
-    for copy in copies[2:]:
+    for copy in copies[2:4]:
+        copy.wait()
+    core, chip = position()
+    own = CHIP * chip + SLAB * core
+    first = (CHIP * chip - SLAB, CHIP * chip, own - SLAB, own)
+    plane = lax.broadcasted_iota(jnp.int32, amount.shape[2:], 0)
+    row = lax.broadcasted_iota(jnp.int32, (cells, depth), 0)
+    for chain, (at_plane, at_row) in enumerate(((1, 0), (0, 1))):
+        here = (row == shot_in[at_row]) & (lane == shot_in[2])
+        spot[chain] = jnp.where(here, 1.0, 0.0)
+        for step in range(steps):
+            hit = plane == shot_in[at_plane] - first[step]
+            amount[chain, step] = jnp.where(hit, -wavelet_in[step], 0.0)
+    for copy in copies[4:]:
         copy.wait()
 
 
@@ -140,14 +157,11 @@
     each(count, rows, one)
 
 
-def shoot(new, pad, first, count, plane, row, depth_at, amount):
-    local = plane - first
-
-    @pl.when((local >= 0) & (local < count))
-    def _():
-        lane = lax.broadcasted_iota(jnp.int32, (1, new.shape[2]), 1)
-        spot = (pl.ds(local, 1), pl.ds(pad + row, 1), slice(None))
-        new[spot] = new[spot] + jnp.where(lane == depth_at, -amount, 0.0)[None]
+def shot_at(amount, spot, chain, step):
+    def extra(i, b, size):
+        return amount[chain, step, pl.ds(i, 1), :] * spot[chain, b : b + size, :]
+
+    return extra
 
 
 def surface_at(surf, first, step, steps):
@@ -201,27 +215,20 @@
     side_planes(refs[2:], window, 0, SLAB + CHIP, (SLAB * (4 + kind),), core)
 
 
-def two_steps(now, old, med, new, edge, across, surface, shots):
+def two_steps(now, old, med, new, edge, across, extras):
     rows = edge.shape[1]
     count = old.shape[0]
-    held = count // SLAB
 
     def medium(k, i):
         return med[k][i]
 
-    extra = [None if surface is None else surface_at(lambda i: surface[i], n, n, STEPS) for n in range(2)]
     clear(now, EDGE, rows)
     clear(new, EDGE, rows)
-    advance(now, SLAB, lambda i: old[i], 0, medium, 0, new, EDGE, count, EDGE, rows, across, extra[0])
-    if shots:
-        first, plane, row, deep, amounts = shots
-        shoot(new, EDGE, first, count, plane, row, deep, amounts[0])
+    advance(now, SLAB, lambda i: old[i], 0, medium, 0, new, EDGE, count, EDGE, rows, across, extras[0])
     advance(
         new, SLAB, lambda i: now[CHIP + i, EDGE : EDGE + rows, :], 0, medium, SLAB, edge, 0,
-        CHIP, EDGE, rows, across, extra[1],
-    )
-    if shots:
-        shoot(edge, 0, first + SLAB, CHIP, plane, row, deep, amounts[1])
+        CHIP, EDGE, rows, across, extras[1],
+    )
 
 
 def fetched(pair, window, pad, count, at, core):
@@ -232,10 +239,10 @@
 
 
 def first_y(
-    where, shot, wavelet, loc, sib, near, near_sib, got, got_sib, edge, carry,
+    amount, spot, loc, sib, near, near_sib, got, got_sib, edge, carry,
     now_r, now_s, old_r, old_s, med_0, med_1, med_2, surf, new_r, new_s,
 ):
-    core, chip = where[0], where[1]
+    core, _ = position()
     refs = (loc, sib, near, near_sib)
     rows = loc.shape[1]
     med = (med_0, med_1, med_2)
@@ -248,9 +255,10 @@
         surf[1 + flip if n < 2 else 3 * flip] = ref[ref.shape[0] - 1]
     fetched((got, got_sib), now_s, EDGE, HALF_NOW, 0, core)
     fetched((got, got_sib), old_s, 0, HALF_OLD, HALF_NOW, core)
-    two_steps(now_r, old_r, med, new_r, edge.at[0], 1, surf, None)
-    shots = (CHIP * chip - SLAB, shot[1], shot[0], shot[2], (wavelet[0], wavelet[1]))
-    two_steps(now_s, old_s, med, new_s, edge.at[1], 1, None, shots)
+    receivers = [surface_at(lambda i: surf[i], n, n, STEPS) for n in range(2)]
+    two_steps(now_r, old_r, med, new_r, edge.at[0], 1, receivers)
+    shots = [shot_at(amount, spot, 0, n) for n in range(2)]
+    two_steps(now_s, old_s, med, new_s, edge.at[1], 1, shots)
     for i in range(SPAN):
         at = SLAB * core + i
         carry[i] = new_r[at, EDGE : EDGE + rows, :]
@@ -262,10 +270,10 @@
 
 
 def first_x(
-    where, shot, wavelet, loc, sib, near, near_sib, got, got_sib, edge, carry,
+    amount, spot, loc, sib, near, near_sib, got, got_sib, edge, carry,
     now, old, med_0, med_1, med_2, new,
 ):
-    core, chip = where[0], where[1]
+    core, _ = position()
     refs = (loc, sib, near, near_sib)
     rows = loc.shape[1]
     med = (med_0, med_1, med_2)
@@ -273,8 +281,7 @@
     rim_window(refs, old, SRC, core)
     for k in range(3):
         fetched((got, got_sib), med[k], 0, HALF_OLD, HALF_NOW + HALF_OLD * (k + 1), core)
-    shots = (CHIP * chip - SLAB, shot[0], shot[1], shot[2], (wavelet[0], wavelet[1]))
-    two_steps(now, old, med, new, edge.at[0], 0, None, shots)
+    two_steps(now, old, med, new, edge.at[0], 0, [shot_at(amount, spot, 1, n) for n in range(2)])
     for i in range(SPAN):
         at = SLAB * core + i
         carry[i] = new[at, EDGE : EDGE + rows, :]
@@ -282,8 +289,8 @@
             carry[SPAN * (1 + k) + i] = med[k][at]
 
 
-def last_steps(where, edges, n, now, old, med, new, end, across, surface, shots):
-    core = where[0]
+def last_steps(last, edges, n, now, old, med, new, end, across, extras):
+    core, chip = position()
     edge, near, near_sib = edges
     rows = edge.shape[2]
     pad = (now.shape[1] - rows) // 2
@@ -292,20 +299,15 @@
     for p in range(CHIP):
         place(now, CHIP + p, pad, edge[n, p])
         for src, side in ((near, core), (near_sib, 1 - core)):
-            plane = jnp.where(where[2 + side] == 1, src[n, p], 0.0)
+            beyond = chip + 2 * side - 1
+            plane = jnp.where((beyond >= 0) & (beyond <= last), src[n, p], 0.0)
             place(now, 2 * CHIP * side + p, pad, plane)
-    extra = [None if surface is None else surface_at(surface, s, 2 + s, STEPS) for s in range(2)]
-    advance(now, SLAB * core + SLAB, old, 0, med, 0, new, pad, SPAN, pad, rows, across, extra[0])
-    if shots:
-        first, plane, row, deep, amounts = shots
-        shoot(new, pad, first, SPAN, plane, row, deep, amounts[0])
+    advance(now, SLAB * core + SLAB, old, 0, med, 0, new, pad, SPAN, pad, rows, across, extras[0])
 
     def older(i):
         return now[CHIP + SLAB * core + i, pad : pad + rows, :]
 
-    advance(new, SLAB, older, 0, med, SLAB, end, pad, SLAB, pad, rows, across, extra[1])
-    if shots:
-        shoot(end, pad, first + SLAB, SLAB, plane, row, deep, amounts[1])
+    advance(new, SLAB, older, 0, med, SLAB, end, pad, SLAB, pad, rows, across, extras[1])
 
 
 def finish(end, new, following, prior, sems, at):
@@ -321,42 +323,36 @@
 
 
 def second_half(
-    where, shot, wavelet, lag_order, edge, near, near_sib, carry, edge_x, near_x, sib_x, carry_x,
+    last, lag_order, amount, spot, edge, near, near_sib, carry, edge_x, near_x, sib_x, carry_x,
     src_next, src_prior, rcv_next, rcv_prior, image,
-    now_r, now_s, now_x, new_r, new_s, new_x, end_r, end_s, end_x, planes, slot_of, sems,
+    now_r, now_s, now_x, new_r, new_s, new_x, end_r, end_s, end_x, planes, order, slot_of, sems,
 ):
     rows, depth = carry.shape[1:]
     lags = lag_order.shape[0]
     half = (lags - 1) // 2
     pad = (now_r.shape[1] - rows) // 2
-    core, chip = where[0], where[1]
-
-    def note(k, _):
-        slot_of[lag_order[k]] = k
-        return 0
-
-    lax.fori_loop(0, lags, note, 0)
+    core, _ = position()
+    lags_in = pltpu.make_async_copy(lag_order, order, sems.at[lags + 4])
+    lags_in.start()
 
     def med(k, i):
         return carry[SPAN * (2 + k) + i]
 
     edges = (edge, near, near_sib)
+    receivers = [surface_at(lambda i: carry[SPAN * 5 + i], n, 2 + n, STEPS) for n in range(2)]
+    last_steps(last, edges, 0, now_r, lambda i: carry[i], med, new_r, end_r, 1, receivers)
+    copies = finish(end_r, new_r, rcv_next, rcv_prior, sems, lags)
+    shots = [shot_at(amount, spot, 0, 2 + n) for n in range(2)]
+    last_steps(last, edges, 1, now_s, lambda i: carry[SPAN + i], med, new_s, end_s, 1, shots)
+    shots = [shot_at(amount, spot, 1, 2 + n) for n in range(2)]
     last_steps(
-        where, edges, 0, now_r, lambda i: carry[i], med, new_r, end_r, 1,
-        lambda i: carry[SPAN * 5 + i], None,
-    )
-    copies = finish(end_r, new_r, rcv_next, rcv_prior, sems, lags)
-    first = CHIP * chip + SLAB * core - SLAB
-    last_steps(
-        where, edges, 1, now_s, lambda i: carry[SPAN + i], med, new_s, end_s, 1, None,
-        (first, shot[1], shot[0], shot[2], (wavelet[2], wavelet[3])),
-    )
-    last_steps(
-        where, (edge_x, near_x, sib_x), 0, now_x, lambda i: carry_x[i],
-        lambda k, i: carry_x[SPAN * (1 + k) + i], new_x, end_x, 0, None,
-        (first, shot[0], shot[1], shot[2], (wavelet[2], wavelet[3])),
+        last, (edge_x, near_x, sib_x), 0, now_x, lambda i: carry_x[i],
+        lambda k, i: carry_x[SPAN * (1 + k) + i], new_x, end_x, 0, shots,
     )
     copies += finish(end_x, new_x, src_next, src_prior, sems, lags + 2)
+    lags_in.wait()
+    for k in range(lags):
+        slot_of[order[k]] = k
     own = CHIP + SLAB * core
     for slot in range(lags):
         lag = slot - half
@@ -390,7 +386,6 @@
     chip, core = device // 2, device % 2
     last = chips - 1
     turning = chip == jnp.where(core == 0, last, 0)
-    where = jnp.stack([core, chip, chip > 0, chip < last]).astype(jnp.int32)
     swap = [(i, i ^ 1) for i in range(devices)]
     order = [*range(0, devices, 2), *range(devices - 1, 0, -2)]
     ring = list(zip(order, order[1:] + order[:1]))
@@ -399,16 +394,17 @@
         return jnp.swapaxes(x, -1, -2)
 
     rcv_now, rcv_old, medium, traces = map(turned, (rcv_now, rcv_old, medium, traces))
-    wide, loc = call(
+    scalars = [pltpu.SMEM(shot.shape, jnp.int32), pltpu.SMEM(wavelet.shape, jnp.float32)]
+    wide, loc, amount, spot = call(
         gather,
-        (src_now, src_old, rcv_now, rcv_old, medium, traces, rec_x),
-        [(5 * SLAB, rows + 2 * EDGE, depth), (7 * SLAB + 1, rows, depth)],
+        (src_now, src_old, rcv_now, rcv_old, medium, traces, rec_x, shot, wavelet),
+        [(5 * SLAB, rows + 2 * EDGE, depth), (7 * SLAB + 1, rows, depth)]
+        + [(2, STEPS, 2 * CHIP, depth), (2, rows, depth)],
         [traces.shape],
-        0,
-        [pltpu.VMEM(rec_x.shape, jnp.int32), pltpu.SemaphoreType.DMA((14,))],
-        far_in=True,
-    )
-    (send,) = call(pack, (wide,), [(devices, SLAB * FETCH, depth)], [], 0)
+        [pltpu.VMEM(rec_x.shape, jnp.int32), *scalars, pltpu.SemaphoreType.DMA((16,))],
+        far=9,
+    )
+    (send,) = call(pack, (wide,), [(devices, SLAB * FETCH, depth)], [])
     got = lax.all_to_all(send, "wide", 0, 0, tiled=True).reshape(-1, depth)
     sib = lax.ppermute(loc, "wide", swap)
     low, high = jnp.where(core == 0, loc, sib), jnp.where(core == 0, sib, loc)
@@ -422,19 +418,17 @@
     padded, plain = (window, rows + 2 * EDGE, depth), (narrow, rows, depth)
     edge_y, carry_y = call(
         first_y,
-        (where, shot, wavelet, loc, sib, near, near_sib, got, got_sib),
+        (amount, spot, loc, sib, near, near_sib, got, got_sib),
         [(2, CHIP, rows, depth), (SPAN * 5 + 3, rows, depth)],
         [padded] * 2 + [plain] * 5 + [(4, rows, depth)] + [(narrow, *padded[1:])] * 2,
-        3,
     )
     mid_y = lax.ppermute(edge_y, "wide", ring)
     mid_y_sib = lax.ppermute(mid_y, "wide", swap)
     edge_x, carry_x = call(
         first_x,
-        (where, shot, wavelet, loc, sib, near, near_sib, got, got_sib),
+        (amount, spot, loc, sib, near, near_sib, got, got_sib),
         [(1, CHIP, rows, depth), (SPAN * 4, rows, depth)],
         [padded] + [plain] * 4 + [(narrow, *padded[1:])],
-        3,
     )
     mid_x = lax.ppermute(edge_x, "wide", ring)
     mid_x_sib = lax.ppermute(mid_x, "wide", swap)
@@ -443,13 +437,13 @@
     pad = -(-max(half, 2) // 8) * 8
     padded = (rows + 2 * pad, depth)
     src_next, src_prior, rcv_next, rcv_prior, image = call(
-        second_half,
-        (where, shot, wavelet, lag_order, edge_y, mid_y, mid_y_sib, carry_y)
+        functools.partial(second_half, last),
+        (lag_order, amount, spot, edge_y, mid_y, mid_y_sib, carry_y)
         + (edge_x, mid_x, mid_x_sib, carry_x),
         [field] * 4 + [(lags, *field)],
         [(window, *padded)] * 3 + [(SPAN, *padded)] * 3 + [(SLAB, *padded)] * 3 + [(lags, *field)],
-        4,
-        [pltpu.SMEM((lags,), jnp.int32), pltpu.SemaphoreType.DMA((lags + 4,))],
+        [pltpu.SMEM((lags,), jnp.int32)] * 2 + [pltpu.SemaphoreType.DMA((lags + 5,))],
+        far=1,
         far_out=range(5),
     )
     return src_next, src_prior, turned(rcv_next), turned(rcv_prior), turned(image)

time: 38.4 us -> 37.1 us (0.966)
  Pallas kernels: 7.1 us -> 5.15 us
  waiting for transfers between devices: 16.4 us -> 17 us
    pallas_call x5, Pallas kernels: 7.1 us -> 5.15 us  [call(): pl.pallas_call(kernel, out_shape=[jax.ShapeDtypeStruct(s, jnp.float32) fo...]
    ppermute x1, waiting for transfers between devices: 2.35 us -> 2.91 us  [on_device(): mid_y = lax.ppermute(edge_y, 'wide', ring)]
  transfers between devices with their start and end apart: 9 -> 9, of which waited for: 6 -> 6; matrix products, arithmetic and copies ran while one was open for 0% -> 0% of each run, Pallas kernels for 5% -> 3%
where the time goes in v4:
time: 37.1 us; the launch traced here: 36.5 us
  waiting for transfers between devices  17 us (46%)
  starting transfers between devices  13.5 us (36%)
  Pallas kernels  5.15 us (14%)
  between operations  0.74 us (2%)
    all_to_all x1, waiting for transfers between devices, on_device(): got = lax.all_to_all(send, 'wide', 0, 0, tiled=True).reshape(-1, depth)  10.1 us
    all_to_all x1, starting transfers between devices, on_device(): got = lax.all_to_all(send, 'wide', 0, 0, tiled=True).reshape(-1, depth)  7.02 us
    pallas_call x5, Pallas kernels, call(): pl.pallas_call(kernel, out_shape=[jax.ShapeDtypeStruct(s, jnp.float32) fo...  5.15 us
    ppermute x1, waiting for transfers between devices, on_device(): mid_y = lax.ppermute(edge_y, 'wide', ring)  2.91 us
    ppermute x1, starting transfers between devices, on_device(): mid_y = lax.ppermute(edge_y, 'wide', ring)  2.54 us
    ppermute x1, starting transfers between devices, on_device(): near = lax.ppermute(jnp.where(turning, 0.0, ours), 'wide', ring)  1.95 us
    ppermute x1, waiting for transfers between devices, on_device(): near_sib = lax.ppermute(near, 'wide', swap)  1.6 us
    ppermute x1, starting transfers between devices, on_device(): mid_x = lax.ppermute(edge_x, 'wide', ring)  1.31 us
  transfers between devices with their start and end apart: 9, of which 6 were waited for; matrix products, arithmetic and copies ran while one was open for 0% of the time, Pallas kernels for 3%

profile of v4, /device:TPU:0, one launch (start us, length us, event | category | flops | bytes accessed | tf_op | source)
XLA Modules:
  0.0 36.5 jit_solution(15854220801873616275)
XLA Ops:
  0.6 1.1 %shard_map.137 = (f32[10,48,128]{2,1,0:T(8,128)S(1)}, f32[15,32,128]{2,1,0:T(8,128)S(1)}, f32[2,4,8,128]{3,2,1,0:T(8,128)S(1)}, f32[2,32,128]{2,1,0:T(8,128)S(1)}) custom-call(f32[2,32,128]{2,1,0:T(8,128)} %src_now.1, f32[2,32,128]{2,1,0:T(8,128)} %src_old.1, f32[2,32,128]{2,1,0:T(8,128)} %bitcast.12, f32[2,32,128]{2,1,0:T(8,128)} %bitcast.13, ...), custom_call_target="tpu_custom_call" | custom-call | tf_op jit(solution)/shard_map/pallas_call | solution.py:26
  1.8 0.5 %collective-permute-start = (f32[15,32,128]{2,1,0:T(8,128)S(1)}, f32[15,32,128]{2,1,0:T(8,128)S(1)}, u32[]{:S(2)}, u32[]{:S(2)}) collective-permute-start(f32[15,32,128]{2,1,0:T(8,128)S(1)} %get-tuple-element.20.loc), channel_id=1, source_target_pairs={{0,1},{1,0},{2,3},{3,2},{4,5},{5,4},{6,7},{7,6},{8,9},{9,8},{10,11... | collective-permute-start | bytes 737288 | tf_op jit(solution)/shard_map/ppermute | solution.py:409
  2.3 0.8 %shard_map.138 = f32[16,48,128]{2,1,0:T(8,128)} custom-call(f32[10,48,128]{2,1,0:T(8,128)S(1)} %get-tuple-element.21.wide), custom_call_target="tpu_custom_call" | custom-call | tf_op jit(solution)/shard_map/pallas_call | solution.py:26
  3.1 7.0 %all-to-all-start = ((f32[16,48,128]{2,1,0:T(8,128)}), f32[16,48,128]{2,1,0:T(8,128)S(1)}, u32[]{:S(2)}, u32[]{:S(2)}) async-start(f32[16,48,128]{2,1,0:T(8,128)} %shard_map.138), calls=%async_computation | async-start | bytes 786432 | tf_op jit(solution)/shard_map/all_to_all | solution.py:408
  10.1 0.0 collective-permute-done.sib
  10.3 2.0 %collective-permute-start.1 = (f32[19,32,128]{2,1,0:T(8,128)S(1)}, f32[19,32,128]{2,1,0:T(8,128)S(1)}, u32[]{:S(2)}, u32[]{:S(2)}) collective-permute-start(f32[19,32,128]{2,1,0:T(8,128)S(1)} %maximum_select_fusion), channel_id=1, source_target_pairs={{0,2},{2,4},{4,6},{6,8},{8,10},{10,12},{12,14},{14,15},{15,13},{13... | collective-permute-start | bytes 933896 | tf_op jit(solution)/shard_map/ppermute | solution.py:413
  12.2 10.1 %all-to-all-done = f32[16,48,128]{2,1,0:T(8,128)S(1)} async-done(((f32[16,48,128]{2,1,0:T(8,128)}), f32[16,48,128]{2,1,0:T(8,128)S(1)}, u32[]{:S(2)}, u32[]{:S(2)}) %all-to-all-start) | async-done | bytes 393248 | tf_op jit(solution)/shard_map/all_to_all | solution.py:408
  22.3 0.1 collective-permute-start.3
  22.4 0.5 %collective-permute-done.1.near = f32[19,32,128]{2,1,0:T(8,128)S(1)} collective-permute-done((f32[19,32,128]{2,1,0:T(8,128)S(1)}, f32[19,32,128]{2,1,0:T(8,128)S(1)}, u32[]{:S(2)}, u32[]{:S(2)}) %collective-permute-start.1) | collective-permute-done | bytes 311328 | tf_op jit(solution)/shard_map/ppermute | solution.py:413
  22.9 0.0 collective-permute-start.2
  22.9 1.6 %collective-permute-done.2.near_sib = f32[19,32,128]{2,1,0:T(8,128)S(1)} collective-permute-done((f32[19,32,128]{2,1,0:T(8,128)S(1)}, f32[19,32,128]{2,1,0:T(8,128)S(1)}, u32[]{:S(2)}, u32[]{:S(2)}) %collective-permute-start.2) | collective-permute-done | bytes 311328 | tf_op jit(solution)/shard_map/ppermute | solution.py:414
  24.5 0.0 collective-permute-done.3.got_sib
  24.5 0.6 %shard_map.139 = (f32[2,4,32,128]{3,2,1,0:T(8,128)S(1)}, f32[33,32,128]{2,1,0:T(8,128)S(1)}) custom-call(f32[2,4,8,128]{3,2,1,0:T(8,128)S(1)} %get-tuple-element.18.amount, f32[2,32,128]{2,1,0:T(8,128)S(1)} %get-tuple-element.19.spot, f32[15,32,128]{2,1,0:T(8,128)S(1)} %get-tuple-element.20.loc, f32[15,32,128]{2,1,0:T(8,128)S(1)} %collective-permute-done.sib, ...), custom_call_target="tpu_custom_call" | custom-call | tf_op jit(solution)/shard_map/pallas_call | solution.py:26
  25.2 2.5 %collective-permute-start.4 = (f32[2,4,32,128]{3,2,1,0:T(8,128)S(1)}, f32[2,4,32,128]{3,2,1,0:T(8,128)S(1)}, u32[]{:S(2)}, u32[]{:S(2)}) collective-permute-start(f32[2,4,32,128]{3,2,1,0:T(8,128)S(1)} %get-tuple-element.22.edge), channel_id=1, source_target_pairs={{0,2},{2,4},{4,6},{6,8},{8,10},{10,12},{12,14},{14,15},{15,13},{13... | collective-permute-start | bytes 393224 | tf_op jit(solution)/shard_map/ppermute | solution.py:425
  27.7 0.4 %shard_map.140 = (f32[1,4,32,128]{3,2,1,0:T(8,128)S(1)}, f32[24,32,128]{2,1,0:T(8,128)S(1)}) custom-call(f32[2,4,8,128]{3,2,1,0:T(8,128)S(1)} %get-tuple-element.18.amount, f32[2,32,128]{2,1,0:T(8,128)S(1)} %get-tuple-element.19.spot, f32[15,32,128]{2,1,0:T(8,128)S(1)} %get-tuple-element.20.loc, f32[15,32,128]{2,1,0:T(8,128)S(1)} %collective-permute-done.sib, ...), custom_call_target="tpu_custom_call" | custom-call | tf_op jit(solution)/shard_map/pallas_call | solution.py:26
  28.1 1.3 %collective-permute-start.6 = (f32[1,4,32,128]{3,2,1,0:T(8,128)S(1)}, f32[1,4,32,128]{3,2,1,0:T(8,128)S(1)}, u32[]{:S(2)}, u32[]{:S(2)}) collective-permute-start(f32[1,4,32,128]{3,2,1,0:T(8,128)S(1)} %get-tuple-element.24.edge_x), channel_id=1, source_target_pairs={{0,2},{2,4},{4,6},{6,8},{8,10},{10,12},{12,14},{14,15},{15,13},{13... | collective-permute-start | bytes 196616 | tf_op jit(solution)/shard_map/ppermute | solution.py:433
  29.4 2.9 %collective-permute-done.4.near = f32[2,4,32,128]{3,2,1,0:T(8,128)S(1)} collective-permute-done((f32[2,4,32,128]{3,2,1,0:T(8,128)S(1)}, f32[2,4,32,128]{3,2,1,0:T(8,128)S(1)}, u32[]{:S(2)}, u32[]{:S(2)}) %collective-permute-start.4) | collective-permute-done | bytes 131104 | tf_op jit(solution)/shard_map/ppermute | solution.py:425
  32.3 0.0 collective-permute-start.5
  32.3 0.7 %collective-permute-done.6.near_x = f32[1,4,32,128]{3,2,1,0:T(8,128)S(1)} collective-permute-done((f32[1,4,32,128]{3,2,1,0:T(8,128)S(1)}, f32[1,4,32,128]{3,2,1,0:T(8,128)S(1)}, u32[]{:S(2)}, u32[]{:S(2)}) %collective-permute-start.6) | collective-permute-done | bytes 65568 | tf_op jit(solution)/shard_map/ppermute | solution.py:433
  33.0 0.0 collective-permute-start.7
  33.0 1.3 %collective-permute-done.7.sib_x = f32[1,4,32,128]{3,2,1,0:T(8,128)S(1)} collective-permute-done((f32[1,4,32,128]{3,2,1,0:T(8,128)S(1)}, f32[1,4,32,128]{3,2,1,0:T(8,128)S(1)}, u32[]{:S(2)}, u32[]{:S(2)}) %collective-permute-start.7) | collective-permute-done | bytes 65568 | tf_op jit(solution)/shard_map/ppermute | solution.py:434
  34.2 0.0 collective-permute-done.5.near_sib
  34.2 2.2 %shard_map.141 = (f32[2,32,128]{2,1,0:T(8,128)}, f32[2,32,128]{2,1,0:T(8,128)}, f32[2,32,128]{2,1,0:T(8,128)}, f32[2,32,128]{2,1,0:T(8,128)}, f32[33,2,32,128]{3,2,1,0:T(8,128)}) custom-call(s32[33]{0:T(128)} %lag_order.1, f32[2,4,8,128]{3,2,1,0:T(8,128)S(1)} %get-tuple-element.18.amount, f32[2,32,128]{2,1,0:T(8,128)S(1)} %get-tuple-element.19.spot, ...), custom_call_target="tpu_custom_call" | custom-call | tf_op jit(solution)/shard_map/pallas_call | solution.py:26
  (5 shorter events, 0.1 us)
Async XLA Ops:
  1.8 8.4 %collective-permute-start = (f32[15,32,128]{2,1,0:T(8,128)S(1)}, f32[15,32,128]{2,1,0:T(8,128)S(1)}, u32[]{:S(2)}, u32[]{:S(2)}) collective-permute-start(f32[15,32,128]{2,1,0:T(8,128)S(1)} %get-tuple-element.20.loc), channel_id=1, source_target_pairs={{0,1},{1,0},{2,3},{3,2},{4,5},{5,4},{6,7},{7,6},{8,9},{9,8},{10,11... | collective-permute-start | bytes 737288 | tf_op jit(solution)/shard_map/ppermute | solution.py:409
  3.1 19.2 %all-to-all-start = ((f32[16,48,128]{2,1,0:T(8,128)}), f32[16,48,128]{2,1,0:T(8,128)S(1)}, u32[]{:S(2)}, u32[]{:S(2)}) async-start(f32[16,48,128]{2,1,0:T(8,128)} %shard_map.138), calls=%async_computation | async-start | bytes 786432 | tf_op jit(solution)/shard_map/all_to_all | solution.py:408
  10.3 12.6 %collective-permute-start.1 = (f32[19,32,128]{2,1,0:T(8,128)S(1)}, f32[19,32,128]{2,1,0:T(8,128)S(1)}, u32[]{:S(2)}, u32[]{:S(2)}) collective-permute-start(f32[19,32,128]{2,1,0:T(8,128)S(1)} %maximum_select_fusion), channel_id=1, source_target_pairs={{0,2},{2,4},{4,6},{6,8},{8,10},{10,12},{12,14},{14,15},{15,13},{13... | collective-permute-start | bytes 933896 | tf_op jit(solution)/shard_map/ppermute | solution.py:413
  22.3 2.2 %collective-permute-start.3 = (f32[768,128]{1,0:T(8,128)S(1)}, f32[768,128]{1,0:T(8,128)S(1)}, u32[]{:S(2)}, u32[]{:S(2)}) collective-permute-start(f32[768,128]{1,0:T(8,128)S(1)} %bitcast.8), channel_id=1, source_target_pairs={{0,1},{1,0},{2,3},{3,2},{4,5},{5,4},{6,7},{7,6},{8,9},{9,8},{10,11... | collective-permute-start | bytes 1179656 | tf_op jit(solution)/shard_map/ppermute | solution.py:415
  22.9 1.6 %collective-permute-start.2 = (f32[19,32,128]{2,1,0:T(8,128)S(1)}, f32[19,32,128]{2,1,0:T(8,128)S(1)}, u32[]{:S(2)}, u32[]{:S(2)}) collective-permute-start(f32[19,32,128]{2,1,0:T(8,128)S(1)} %collective-permute-done.1.near), channel_id=1, source_target_pairs={{0,1},{1,0},{2,3},{3,2},{4,5},{5,4},{6,7},{7,6},{8,9},{9,8},{10,11... | collective-permute-start | bytes 933896 | tf_op jit(solution)/shard_map/ppermute | solution.py:414
  25.2 7.1 %collective-permute-start.4 = (f32[2,4,32,128]{3,2,1,0:T(8,128)S(1)}, f32[2,4,32,128]{3,2,1,0:T(8,128)S(1)}, u32[]{:S(2)}, u32[]{:S(2)}) collective-permute-start(f32[2,4,32,128]{3,2,1,0:T(8,128)S(1)} %get-tuple-element.22.edge), channel_id=1, source_target_pairs={{0,2},{2,4},{4,6},{6,8},{8,10},{10,12},{12,14},{14,15},{15,13},{13... | collective-permute-start | bytes 393224 | tf_op jit(solution)/shard_map/ppermute | solution.py:425
  28.1 4.9 %collective-permute-start.6 = (f32[1,4,32,128]{3,2,1,0:T(8,128)S(1)}, f32[1,4,32,128]{3,2,1,0:T(8,128)S(1)}, u32[]{:S(2)}, u32[]{:S(2)}) collective-permute-start(f32[1,4,32,128]{3,2,1,0:T(8,128)S(1)} %get-tuple-element.24.edge_x), channel_id=1, source_target_pairs={{0,2},{2,4},{4,6},{6,8},{8,10},{10,12},{12,14},{14,15},{15,13},{13... | collective-permute-start | bytes 196616 | tf_op jit(solution)/shard_map/ppermute | solution.py:433
  32.3 2.0 %collective-permute-start.5 = (f32[2,4,32,128]{3,2,1,0:T(8,128)S(1)}, f32[2,4,32,128]{3,2,1,0:T(8,128)S(1)}, u32[]{:S(2)}, u32[]{:S(2)}) collective-permute-start(f32[2,4,32,128]{3,2,1,0:T(8,128)S(1)} %collective-permute-done.4.near), channel_id=1, source_target_pairs={{0,1},{1,0},{2,3},{3,2},{4,5},{5,4},{6,7},{7,6},{8,9},{9,8},{10,11... | collective-permute-start | bytes 393224 | tf_op jit(solution)/shard_map/ppermute | solution.py:426
  33.0 1.3 %collective-permute-start.7 = (f32[1,4,32,128]{3,2,1,0:T(8,128)S(1)}, f32[1,4,32,128]{3,2,1,0:T(8,128)S(1)}, u32[]{:S(2)}, u32[]{:S(2)}) collective-permute-start(f32[1,4,32,128]{3,2,1,0:T(8,128)S(1)} %collective-permute-done.6.near_x), channel_id=1, source_target_pairs={{0,1},{1,0},{2,3},{3,2},{4,5},{5,4},{6,7},{7,6},{8,9},{9,8},{10,11... | collective-permute-start | bytes 196616 | tf_op jit(solution)/shard_map/ppermute | solution.py:434

commit v5 on v4

--- a/solution.py
+++ b/solution.py
@@ -14,6 +14,7 @@
 HALF_NOW = (CHIP + 2 * CHIP) // 2
 HALF_OLD = (CHIP + CHIP) // 2
 FETCH = 24
+REST = 8
 
 VMEM = pl.BlockSpec(memory_space=pltpu.VMEM)
 HBM = pl.BlockSpec(memory_space=pltpu.HBM)
@@ -105,7 +106,7 @@
             at = FETCH * h
             send[j, at : at + HALF_NOW, :] = wide[h, now_at : now_at + HALF_NOW, :]
             for k in range(4):
-                at = FETCH * h + HALF_NOW + HALF_OLD * k
+                at = FETCH * h + REST + HALF_OLD * k
                 plane = SLAB * (k + 1) + h
                 send[j, at : at + HALF_OLD, :] = wide[plane, old_at : old_at + HALF_OLD, :]
 
@@ -158,21 +159,21 @@
 
 
 def shot_at(amount, spot, chain, step):
-    def extra(i, b, size):
-        return amount[chain, step, pl.ds(i, 1), :] * spot[chain, b : b + size, :]
+    def extra(i, b, size, at=0):
+        return amount[chain, step, pl.ds(at + i, 1), :] * spot[chain, b : b + size, :]
 
     return extra
 
 
 def surface_at(surf, first, step, steps):
-    def extra(i, b, size):
-        held = surf(first + i // SLAB)[b : b + size, :]
+    def extra(i, b, size, at=0):
+        held = surf(first + lax.div(at, SLAB) + i // SLAB)[b : b + size, :]
         depth = held.shape[1]
         lane = lax.broadcasted_iota(jnp.int32, (size, depth), 1)
+        if isinstance(i, int):
+            shift = (i % SLAB) * steps + step
+            return jnp.where(lane == 0, pltpu.roll(held, (depth - shift) % depth, 1), 0.0)
         total = jnp.zeros_like(held)
-        shift = (i % SLAB) * steps + step
-        if isinstance(shift, int):
-            return jnp.where(lane == 0, pltpu.roll(held, (depth - shift) % depth, 1), 0.0)
         for s in range(SLAB):
             moved = pltpu.roll(held, (depth - s * steps - step) % depth, 1)
             total = jnp.where((lane == 0) & (i % SLAB == s), moved, total)
@@ -254,7 +255,7 @@
         flip = core if n % 2 == 0 else 1 - core
         surf[1 + flip if n < 2 else 3 * flip] = ref[ref.shape[0] - 1]
     fetched((got, got_sib), now_s, EDGE, HALF_NOW, 0, core)
-    fetched((got, got_sib), old_s, 0, HALF_OLD, HALF_NOW, core)
+    fetched((got, got_sib), old_s, 0, HALF_OLD, REST, core)
     receivers = [surface_at(lambda i: surf[i], n, n, STEPS) for n in range(2)]
     two_steps(now_r, old_r, med, new_r, edge.at[0], 1, receivers)
     shots = [shot_at(amount, spot, 0, n) for n in range(2)]
@@ -280,7 +281,7 @@
     now_window(refs, now, SRC, core)
     rim_window(refs, old, SRC, core)
     for k in range(3):
-        fetched((got, got_sib), med[k], 0, HALF_OLD, HALF_NOW + HALF_OLD * (k + 1), core)
+        fetched((got, got_sib), med[k], 0, HALF_OLD, REST + HALF_OLD * (k + 1), core)
     two_steps(now, old, med, new, edge.at[0], 0, [shot_at(amount, spot, 1, n) for n in range(2)])
     for i in range(SPAN):
         at = SLAB * core + i
@@ -289,20 +290,70 @@
             carry[SPAN * (1 + k) + i] = med[k][at]
 
 
-def last_steps(last, edges, n, now, old, med, new, end, across, extras):
-    core, chip = position()
+def halo_planes(last, edge, sides, window, pad):
+    _, chip = position()
+    for p in range(CHIP):
+        place(window, CHIP + p, pad, edge[p])
+        for src, side in sides:
+            beyond = chip + 2 * side - 1
+            plane = jnp.where((beyond >= 0) & (beyond <= last), src[p], 0.0)
+            place(window, 2 * CHIP * side + p, pad, plane)
+
+
+def product(first, second, slot, lags, b, pad, p, q):
+    rows = first.shape[1] - 2 * pad
+    lag = slot - (lags - 1) // 2
+    if b + 8 <= abs(lag) or b >= rows - abs(lag):
+        return None
+    back, ahead = pad + b - lag, pad + b + lag
+    return first[p, back : back + 8, :] * second[q, ahead : ahead + 8, :]
+
+
+def middle(last, order, amount, spot, edge, near, carry, ahead, snap, slots, now_r, now_s):
+    rows = carry.shape[1]
+    pad = (now_r.shape[1] - rows) // 2
+    core, _ = position()
+    for n, now in enumerate((now_r, now_s)):
+        clear(now, pad, rows)
+        halo_planes(last, edge.at[n], ((near.at[n], core),), now, pad)
+        term = shot_at(amount, spot, 0, 2)
+        if n == 0:
+            term = surface_at(lambda i: carry[SPAN * 5 + i], 0, 2, STEPS)
+        advance(
+            now, SLAB + CHIP * core, lambda i: carry[SPAN * n + i], SLAB * core,
+            lambda k, i: carry[SPAN * (2 + k) + i], SLAB * core, ahead.at[n], 0,
+            CHIP, pad, rows, 1, lambda i, b, size: term(i, b, size, SLAB * core),
+        )
+    hit = lax.broadcasted_iota(jnp.int32, (slots.shape[0], order.shape[1]), 0) == order[...]
+    place_of = lax.broadcasted_iota(jnp.int32, hit.shape, 1).astype(jnp.float32)
+    found = jnp.sum(jnp.where(hit, place_of, 0.0), axis=1, keepdims=True)
+    slots[...] = jnp.broadcast_to(found, slots.shape)
+    own = CHIP + SLAB * core
+    for slot in range(snap.shape[0]):
+        for p in range(SLAB):
+            for b in range(0, rows, 8):
+                value = product(now_s, now_r, slot, snap.shape[0], b, pad, own + p, own + p)
+                if value is not None:
+                    snap[slot, p, b : b + 8, :] = value
+
+
+def last_steps(last, edges, n, now, old, med, new, end, across, extras, ahead=None):
+    core, _ = position()
     edge, near, near_sib = edges
     rows = edge.shape[2]
     pad = (now.shape[1] - rows) // 2
     for window in (now, new, end):
         clear(window, pad, rows)
-    for p in range(CHIP):
-        place(now, CHIP + p, pad, edge[n, p])
-        for src, side in ((near, core), (near_sib, 1 - core)):
-            beyond = chip + 2 * side - 1
-            plane = jnp.where((beyond >= 0) & (beyond <= last), src[n, p], 0.0)
-            place(now, 2 * CHIP * side + p, pad, plane)
-    advance(now, SLAB * core + SLAB, old, 0, med, 0, new, pad, SPAN, pad, rows, across, extras[0])
+    halo_planes(last, edge.at[n], ((near.at[n], core), (near_sib.at[n], 1 - core)), now, pad)
+    first, count = 0, SPAN
+    if ahead is not None:
+        for p in range(CHIP):
+            place(new, SLAB * core + p, pad, ahead[n, p])
+        first, count = CHIP * (1 - core), SLAB
+    advance(
+        now, SLAB * core + SLAB + first, old, first, med, first, new.at[pl.ds(first, count)], pad,
+        count, pad, rows, across, lambda i, b, size: extras[0](i, b, size, first),
+    )
 
     def older(i):
         return now[CHIP + SLAB * core + i, pad : pad + rows, :]
@@ -323,51 +374,43 @@
 
 
 def second_half(
-    last, lag_order, amount, spot, edge, near, near_sib, carry, edge_x, near_x, sib_x, carry_x,
+    last, amount, spot, edge, near, near_sib, carry, edge_x, near_x, sib_x, carry_x,
+    ahead, snap, slots,
     src_next, src_prior, rcv_next, rcv_prior, image,
-    now_r, now_s, now_x, new_r, new_s, new_x, end_r, end_s, end_x, planes, order, slot_of, sems,
+    now_r, now_s, now_x, new_r, new_s, new_x, end_r, end_s, end_x, planes, sems,
 ):
     rows, depth = carry.shape[1:]
-    lags = lag_order.shape[0]
-    half = (lags - 1) // 2
+    lags = image.shape[0]
     pad = (now_r.shape[1] - rows) // 2
     core, _ = position()
-    lags_in = pltpu.make_async_copy(lag_order, order, sems.at[lags + 4])
-    lags_in.start()
-
     def med(k, i):
         return carry[SPAN * (2 + k) + i]
 
     edges = (edge, near, near_sib)
     receivers = [surface_at(lambda i: carry[SPAN * 5 + i], n, 2 + n, STEPS) for n in range(2)]
-    last_steps(last, edges, 0, now_r, lambda i: carry[i], med, new_r, end_r, 1, receivers)
+    last_steps(last, edges, 0, now_r, lambda i: carry[i], med, new_r, end_r, 1, receivers, ahead)
     copies = finish(end_r, new_r, rcv_next, rcv_prior, sems, lags)
     shots = [shot_at(amount, spot, 0, 2 + n) for n in range(2)]
-    last_steps(last, edges, 1, now_s, lambda i: carry[SPAN + i], med, new_s, end_s, 1, shots)
+    last_steps(
+        last, edges, 1, now_s, lambda i: carry[SPAN + i], med, new_s, end_s, 1, shots, ahead
+    )
     shots = [shot_at(amount, spot, 1, 2 + n) for n in range(2)]
     last_steps(
         last, (edge_x, near_x, sib_x), 0, now_x, lambda i: carry_x[i],
         lambda k, i: carry_x[SPAN * (1 + k) + i], new_x, end_x, 0, shots,
     )
     copies += finish(end_x, new_x, src_next, src_prior, sems, lags + 2)
-    lags_in.wait()
-    for k in range(lags):
-        slot_of[order[k]] = k
-    own = CHIP + SLAB * core
     for slot in range(lags):
-        lag = slot - half
         for p in range(SLAB):
             for b in range(0, rows, 8):
-                if b + 8 <= abs(lag) or b >= rows - abs(lag):
-                    planes[slot, p, b : b + 8, :] = jnp.zeros((8, depth), jnp.float32)
-                    continue
-                back, ahead = pad + b - lag, pad + b + lag
-                planes[slot, p, b : b + 8, :] = (
-                    now_s[own + p, back : back + 8, :] * now_r[own + p, ahead : ahead + 8, :]
-                    + end_s[p, back : back + 8, :] * end_r[p, ahead : ahead + 8, :]
-                )
+                value = product(end_s, end_r, slot, lags, b, pad, p, p)
+                cut = slice(b, b + 8)
+                if value is None:
+                    planes[slot, p, cut, :] = jnp.zeros((8, depth), jnp.float32)
+                else:
+                    planes[slot, p, cut, :] = snap[slot, p, cut, :] + value
         copies.append(
-            pltpu.make_async_copy(planes.at[slot], image.at[slot_of[slot]], sems.at[slot])
+            pltpu.make_async_copy(planes.at[slot], image.at[slots[slot, 0].astype(jnp.int32)], sems.at[slot])
         )
         copies[-1].start()
     for copy in copies:
@@ -436,14 +479,19 @@
     field = (SLAB, rows, depth)
     pad = -(-max(half, 2) // 8) * 8
     padded = (rows + 2 * pad, depth)
+    ahead, snap, slots = call(
+        functools.partial(middle, last),
+        (lag_order[None], amount, spot, edge_y, mid_y, carry_y),
+        [(2, CHIP, rows, depth), (lags, *field), (-(-lags // 8) * 8, depth)],
+        [(window, *padded)] * 2,
+    )
     src_next, src_prior, rcv_next, rcv_prior, image = call(
         functools.partial(second_half, last),
-        (lag_order, amount, spot, edge_y, mid_y, mid_y_sib, carry_y)
-        + (edge_x, mid_x, mid_x_sib, carry_x),
+        (amount, spot, edge_y, mid_y, mid_y_sib, carry_y)
+        + (edge_x, mid_x, mid_x_sib, carry_x, ahead, snap, slots),
         [field] * 4 + [(lags, *field)],
         [(window, *padded)] * 3 + [(SPAN, *padded)] * 3 + [(SLAB, *padded)] * 3 + [(lags, *field)],
-        [pltpu.SMEM((lags,), jnp.int32)] * 2 + [pltpu.SemaphoreType.DMA((lags + 5,))],
-        far=1,
+        [pltpu.SemaphoreType.DMA((lags + 4,))],
         far_out=range(5),
     )
     return src_next, src_prior, turned(rcv_next), turned(rcv_prior), turned(image)

time: 37.1 us -> 36.7 us (0.989)
    pallas_call x5 -> x6, Pallas kernels: 5.15 us -> 5.11 us  [call(): pl.pallas_call(kernel, out_shape=[jax.ShapeDtypeStruct(s, jnp.float32) fo...]
  transfers between devices with their start and end apart: 9 -> 9, of which waited for: 6 -> 6; matrix products, arithmetic and copies ran while one was open for 0% -> 0% of each run, Pallas kernels for 3% -> 4%
where the time goes in v5:
time: 36.7 us; the launch traced here: 36.1 us
  waiting for transfers between devices  16.7 us (46%)
  starting transfers between devices  13.5 us (37%)
  Pallas kernels  5.11 us (14%)
  between operations  0.75 us (2%)
    all_to_all x1, waiting for transfers between devices, on_device(): got = lax.all_to_all(send, 'wide', 0, 0, tiled=True).reshape(-1, depth)  10.1 us
    all_to_all x1, starting transfers between devices, on_device(): got = lax.all_to_all(send, 'wide', 0, 0, tiled=True).reshape(-1, depth)  7.02 us
    pallas_call x6, Pallas kernels, call(): pl.pallas_call(kernel, out_shape=[jax.ShapeDtypeStruct(s, jnp.float32) fo...  5.11 us
    ppermute x1, waiting for transfers between devices, on_device(): mid_y = lax.ppermute(edge_y, 'wide', ring)  2.91 us
    ppermute x1, starting transfers between devices, on_device(): mid_y = lax.ppermute(edge_y, 'wide', ring)  2.54 us
    ppermute x1, starting transfers between devices, on_device(): near = lax.ppermute(jnp.where(turning, 0.0, ours), 'wide', ring)  1.95 us
    ppermute x1, waiting for transfers between devices, on_device(): near_sib = lax.ppermute(near, 'wide', swap)  1.6 us
    ppermute x1, starting transfers between devices, on_device(): mid_x = lax.ppermute(edge_x, 'wide', ring)  1.31 us
  transfers between devices with their start and end apart: 9, of which 6 were waited for; matrix products, arithmetic and copies ran while one was open for 0% of the time, Pallas kernels for 4%

profile of v5, /device:TPU:0, one launch (start us, length us, event | category | flops | bytes accessed | tf_op | source)
XLA Modules:
  0.0 36.1 jit_solution(13906802072074979569)
XLA Ops:
  0.6 1.1 %shard_map.137 = (f32[10,48,128]{2,1,0:T(8,128)S(1)}, f32[15,32,128]{2,1,0:T(8,128)S(1)}, f32[2,4,8,128]{3,2,1,0:T(8,128)S(1)}, f32[2,32,128]{2,1,0:T(8,128)S(1)}) custom-call(f32[2,32,128]{2,1,0:T(8,128)} %src_now.1, f32[2,32,128]{2,1,0:T(8,128)} %src_old.1, f32[2,32,128]{2,1,0:T(8,128)} %bitcast.14, f32[2,32,128]{2,1,0:T(8,128)} %bitcast.15, ...), custom_call_target="tpu_custom_call" | custom-call | tf_op jit(solution)/shard_map/pallas_call | solution.py:27
  1.8 0.5 %collective-permute-start = (f32[15,32,128]{2,1,0:T(8,128)S(1)}, f32[15,32,128]{2,1,0:T(8,128)S(1)}, u32[]{:S(2)}, u32[]{:S(2)}) collective-permute-start(f32[15,32,128]{2,1,0:T(8,128)S(1)} %get-tuple-element.23.loc), channel_id=1, source_target_pairs={{0,1},{1,0},{2,3},{3,2},{4,5},{5,4},{6,7},{7,6},{8,9},{9,8},{10,11... | collective-permute-start | bytes 737288 | tf_op jit(solution)/shard_map/ppermute | solution.py:452
  2.3 0.8 %shard_map.138 = f32[16,48,128]{2,1,0:T(8,128)} custom-call(f32[10,48,128]{2,1,0:T(8,128)S(1)} %get-tuple-element.24.wide), custom_call_target="tpu_custom_call" | custom-call | tf_op jit(solution)/shard_map/pallas_call | solution.py:27
  3.1 7.0 %all-to-all-start = ((f32[16,48,128]{2,1,0:T(8,128)}), f32[16,48,128]{2,1,0:T(8,128)S(1)}, u32[]{:S(2)}, u32[]{:S(2)}) async-start(f32[16,48,128]{2,1,0:T(8,128)} %shard_map.138), calls=%async_computation | async-start | bytes 786432 | tf_op jit(solution)/shard_map/all_to_all | solution.py:451
  10.1 0.0 collective-permute-done.sib
  10.3 2.0 %collective-permute-start.1 = (f32[19,32,128]{2,1,0:T(8,128)S(1)}, f32[19,32,128]{2,1,0:T(8,128)S(1)}, u32[]{:S(2)}, u32[]{:S(2)}) collective-permute-start(f32[19,32,128]{2,1,0:T(8,128)S(1)} %maximum_select_fusion), channel_id=1, source_target_pairs={{0,2},{2,4},{4,6},{6,8},{8,10},{10,12},{12,14},{14,15},{15,13},{13... | collective-permute-start | bytes 933896 | tf_op jit(solution)/shard_map/ppermute | solution.py:456
  12.2 10.1 %all-to-all-done = f32[16,48,128]{2,1,0:T(8,128)S(1)} async-done(((f32[16,48,128]{2,1,0:T(8,128)}), f32[16,48,128]{2,1,0:T(8,128)S(1)}, u32[]{:S(2)}, u32[]{:S(2)}) %all-to-all-start) | async-done | bytes 393248 | tf_op jit(solution)/shard_map/all_to_all | solution.py:451
  22.3 0.1 collective-permute-start.3
  22.4 0.5 %collective-permute-done.1.near = f32[19,32,128]{2,1,0:T(8,128)S(1)} collective-permute-done((f32[19,32,128]{2,1,0:T(8,128)S(1)}, f32[19,32,128]{2,1,0:T(8,128)S(1)}, u32[]{:S(2)}, u32[]{:S(2)}) %collective-permute-start.1) | collective-permute-done | bytes 311328 | tf_op jit(solution)/shard_map/ppermute | solution.py:456
  22.9 0.0 collective-permute-start.2
  22.9 1.6 %collective-permute-done.2.near_sib = f32[19,32,128]{2,1,0:T(8,128)S(1)} collective-permute-done((f32[19,32,128]{2,1,0:T(8,128)S(1)}, f32[19,32,128]{2,1,0:T(8,128)S(1)}, u32[]{:S(2)}, u32[]{:S(2)}) %collective-permute-start.2) | collective-permute-done | bytes 311328 | tf_op jit(solution)/shard_map/ppermute | solution.py:457
  24.5 0.0 collective-permute-done.3.got_sib
  24.5 0.6 %shard_map.139 = (f32[2,4,32,128]{3,2,1,0:T(8,128)S(1)}, f32[33,32,128]{2,1,0:T(8,128)S(1)}) custom-call(f32[2,4,8,128]{3,2,1,0:T(8,128)S(1)} %get-tuple-element.21.amount, f32[2,32,128]{2,1,0:T(8,128)S(1)} %get-tuple-element.22.spot, f32[15,32,128]{2,1,0:T(8,128)S(1)} %get-tuple-element.23.loc, f32[15,32,128]{2,1,0:T(8,128)S(1)} %collective-permute-done.sib, ...), custom_call_target="tpu_custom_call" | custom-call | tf_op jit(solution)/shard_map/pallas_call | solution.py:27
  25.2 0.0 copy-start
  25.2 2.5 %collective-permute-start.4 = (f32[2,4,32,128]{3,2,1,0:T(8,128)S(1)}, f32[2,4,32,128]{3,2,1,0:T(8,128)S(1)}, u32[]{:S(2)}, u32[]{:S(2)}) collective-permute-start(f32[2,4,32,128]{3,2,1,0:T(8,128)S(1)} %get-tuple-element.25.edge), channel_id=1, source_target_pairs={{0,2},{2,4},{4,6},{6,8},{8,10},{10,12},{12,14},{14,15},{15,13},{13... | collective-permute-start | bytes 393224 | tf_op jit(solution)/shard_map/ppermute | solution.py:468
  27.7 0.4 %shard_map.140 = (f32[1,4,32,128]{3,2,1,0:T(8,128)S(1)}, f32[24,32,128]{2,1,0:T(8,128)S(1)}) custom-call(f32[2,4,8,128]{3,2,1,0:T(8,128)S(1)} %get-tuple-element.21.amount, f32[2,32,128]{2,1,0:T(8,128)S(1)} %get-tuple-element.22.spot, f32[15,32,128]{2,1,0:T(8,128)S(1)} %get-tuple-element.23.loc, f32[15,32,128]{2,1,0:T(8,128)S(1)} %collective-permute-done.sib, ...), custom_call_target="tpu_custom_call" | custom-call | tf_op jit(solution)/shard_map/pallas_call | solution.py:27
  28.1 1.3 %collective-permute-start.6 = (f32[1,4,32,128]{3,2,1,0:T(8,128)S(1)}, f32[1,4,32,128]{3,2,1,0:T(8,128)S(1)}, u32[]{:S(2)}, u32[]{:S(2)}) collective-permute-start(f32[1,4,32,128]{3,2,1,0:T(8,128)S(1)} %get-tuple-element.27.edge_x), channel_id=1, source_target_pairs={{0,2},{2,4},{4,6},{6,8},{8,10},{10,12},{12,14},{14,15},{15,13},{13... | collective-permute-start | bytes 196616 | tf_op jit(solution)/shard_map/ppermute | solution.py:476
  29.4 2.9 %collective-permute-done.4.near = f32[2,4,32,128]{3,2,1,0:T(8,128)S(1)} collective-permute-done((f32[2,4,32,128]{3,2,1,0:T(8,128)S(1)}, f32[2,4,32,128]{3,2,1,0:T(8,128)S(1)}, u32[]{:S(2)}, u32[]{:S(2)}) %collective-permute-start.4) | collective-permute-done | bytes 131104 | tf_op jit(solution)/shard_map/ppermute | solution.py:468
  32.3 0.0 collective-permute-start.5
  32.3 0.7 %collective-permute-done.6.near_x = f32[1,4,32,128]{3,2,1,0:T(8,128)S(1)} collective-permute-done((f32[1,4,32,128]{3,2,1,0:T(8,128)S(1)}, f32[1,4,32,128]{3,2,1,0:T(8,128)S(1)}, u32[]{:S(2)}, u32[]{:S(2)}) %collective-permute-start.6) | collective-permute-done | bytes 65568 | tf_op jit(solution)/shard_map/ppermute | solution.py:476
  33.0 0.0 collective-permute-start.7
  33.0 0.0 copy-done
  33.0 0.3 shard_map.141
  33.3 0.9 %collective-permute-done.7.sib_x = f32[1,4,32,128]{3,2,1,0:T(8,128)S(1)} collective-permute-done((f32[1,4,32,128]{3,2,1,0:T(8,128)S(1)}, f32[1,4,32,128]{3,2,1,0:T(8,128)S(1)}, u32[]{:S(2)}, u32[]{:S(2)}) %collective-permute-start.7) | collective-permute-done | bytes 65568 | tf_op jit(solution)/shard_map/ppermute | solution.py:477
  34.3 0.0 collective-permute-done.5.near_sib
  34.3 1.9 %shard_map.142 = (f32[2,32,128]{2,1,0:T(8,128)}, f32[2,32,128]{2,1,0:T(8,128)}, f32[2,32,128]{2,1,0:T(8,128)}, f32[2,32,128]{2,1,0:T(8,128)}, f32[33,2,32,128]{3,2,1,0:T(8,128)}) custom-call(f32[2,4,8,128]{3,2,1,0:T(8,128)S(1)} %get-tuple-element.21.amount, f32[2,32,128]{2,1,0:T(8,128)S(1)} %get-tuple-element.22.spot, ...), custom_call_target="tpu_custom_call" | custom-call | tf_op jit(solution)/shard_map/pallas_call | solution.py:27
  (5 shorter events, 0.1 us)
Async XLA Ops:
  1.8 8.4 %collective-permute-start = (f32[15,32,128]{2,1,0:T(8,128)S(1)}, f32[15,32,128]{2,1,0:T(8,128)S(1)}, u32[]{:S(2)}, u32[]{:S(2)}) collective-permute-start(f32[15,32,128]{2,1,0:T(8,128)S(1)} %get-tuple-element.23.loc), channel_id=1, source_target_pairs={{0,1},{1,0},{2,3},{3,2},{4,5},{5,4},{6,7},{7,6},{8,9},{9,8},{10,11... | collective-permute-start | bytes 737288 | tf_op jit(solution)/shard_map/ppermute | solution.py:452
  3.1 19.2 %all-to-all-start = ((f32[16,48,128]{2,1,0:T(8,128)}), f32[16,48,128]{2,1,0:T(8,128)S(1)}, u32[]{:S(2)}, u32[]{:S(2)}) async-start(f32[16,48,128]{2,1,0:T(8,128)} %shard_map.138), calls=%async_computation | async-start | bytes 786432 | tf_op jit(solution)/shard_map/all_to_all | solution.py:451
  10.3 12.6 %collective-permute-start.1 = (f32[19,32,128]{2,1,0:T(8,128)S(1)}, f32[19,32,128]{2,1,0:T(8,128)S(1)}, u32[]{:S(2)}, u32[]{:S(2)}) collective-permute-start(f32[19,32,128]{2,1,0:T(8,128)S(1)} %maximum_select_fusion), channel_id=1, source_target_pairs={{0,2},{2,4},{4,6},{6,8},{8,10},{10,12},{12,14},{14,15},{15,13},{13... | collective-permute-start | bytes 933896 | tf_op jit(solution)/shard_map/ppermute | solution.py:456
  22.3 2.2 %collective-permute-start.3 = (f32[768,128]{1,0:T(8,128)S(1)}, f32[768,128]{1,0:T(8,128)S(1)}, u32[]{:S(2)}, u32[]{:S(2)}) collective-permute-start(f32[768,128]{1,0:T(8,128)S(1)} %bitcast.9), channel_id=1, source_target_pairs={{0,1},{1,0},{2,3},{3,2},{4,5},{5,4},{6,7},{7,6},{8,9},{9,8},{10,11... | collective-permute-start | bytes 1179656 | tf_op jit(solution)/shard_map/ppermute | solution.py:458
  22.9 1.6 %collective-permute-start.2 = (f32[19,32,128]{2,1,0:T(8,128)S(1)}, f32[19,32,128]{2,1,0:T(8,128)S(1)}, u32[]{:S(2)}, u32[]{:S(2)}) collective-permute-start(f32[19,32,128]{2,1,0:T(8,128)S(1)} %collective-permute-done.1.near), channel_id=1, source_target_pairs={{0,1},{1,0},{2,3},{3,2},{4,5},{5,4},{6,7},{7,6},{8,9},{9,8},{10,11... | collective-permute-start | bytes 933896 | tf_op jit(solution)/shard_map/ppermute | solution.py:457
  25.2 7.9 %copy-start = (s32[33]{0:T(128)S(1)}, s32[33]{0:T(128)}, u32[]{:S(2)}) copy-start(s32[33]{0:T(128)} %param.19) | copy-start | bytes 400
  25.2 7.1 %collective-permute-start.4 = (f32[2,4,32,128]{3,2,1,0:T(8,128)S(1)}, f32[2,4,32,128]{3,2,1,0:T(8,128)S(1)}, u32[]{:S(2)}, u32[]{:S(2)}) collective-permute-start(f32[2,4,32,128]{3,2,1,0:T(8,128)S(1)} %get-tuple-element.25.edge), channel_id=1, source_target_pairs={{0,2},{2,4},{4,6},{6,8},{8,10},{10,12},{12,14},{14,15},{15,13},{13... | collective-permute-start | bytes 393224 | tf_op jit(solution)/shard_map/ppermute | solution.py:468
  28.1 4.9 %collective-permute-start.6 = (f32[1,4,32,128]{3,2,1,0:T(8,128)S(1)}, f32[1,4,32,128]{3,2,1,0:T(8,128)S(1)}, u32[]{:S(2)}, u32[]{:S(2)}) collective-permute-start(f32[1,4,32,128]{3,2,1,0:T(8,128)S(1)} %get-tuple-element.27.edge_x), channel_id=1, source_target_pairs={{0,2},{2,4},{4,6},{6,8},{8,10},{10,12},{12,14},{14,15},{15,13},{13... | collective-permute-start | bytes 196616 | tf_op jit(solution)/shard_map/ppermute | solution.py:476
  32.3 2.0 %collective-permute-start.5 = (f32[2,4,32,128]{3,2,1,0:T(8,128)S(1)}, f32[2,4,32,128]{3,2,1,0:T(8,128)S(1)}, u32[]{:S(2)}, u32[]{:S(2)}) collective-permute-start(f32[2,4,32,128]{3,2,1,0:T(8,128)S(1)} %collective-permute-done.4.near), channel_id=1, source_target_pairs={{0,1},{1,0},{2,3},{3,2},{4,5},{5,4},{6,7},{7,6},{8,9},{9,8},{10,11... | collective-permute-start | bytes 393224 | tf_op jit(solution)/shard_map/ppermute | solution.py:469
  33.0 1.3 %collective-permute-start.7 = (f32[1,4,32,128]{3,2,1,0:T(8,128)S(1)}, f32[1,4,32,128]{3,2,1,0:T(8,128)S(1)}, u32[]{:S(2)}, u32[]{:S(2)}) collective-permute-start(f32[1,4,32,128]{3,2,1,0:T(8,128)S(1)} %collective-permute-done.6.near_x), channel_id=1, source_target_pairs={{0,1},{1,0},{2,3},{3,2},{4,5},{5,4},{6,7},{7,6},{8,9},{9,8},{10,11... | collective-permute-start | bytes 196616 | tf_op jit(solution)/shard_map/ppermute | solution.py:477

commit v6 on v5

--- a/solution.py
+++ b/solution.py
@@ -54,22 +54,29 @@
 
 def gather(
     src_now, src_old, rcv_now, rcv_old, med, traces, rec_x, shot, wavelet,
-    wide, loc, amount, spot, traces_in, rec_in, shot_in, wavelet_in, sems,
+    send, loc, amount, spot, wide, packed, traces_in, rec_in, shot_in, wavelet_in, sems,
 ):
     rows, depth = src_now.shape[1:]
     steps, cells = traces.shape[1], loc.shape[1]
     inner = pl.ds(EDGE, rows)
-    pairs = [(traces, traces_in), (rec_x, rec_in), (shot, shot_in), (wavelet, wavelet_in)]
+    pairs = []
+    for n, own in enumerate((src_now, src_old, med.at[0], med.at[1], med.at[2])):
+        pairs.append((own, wide.at[pl.ds(n * SLAB, SLAB), inner]))
+    ready = len(pairs)
+    pairs += [(traces, traces_in), (rec_x, rec_in), (shot, shot_in), (wavelet, wavelet_in)]
     for n, own in enumerate((rcv_now, src_now, rcv_old, src_old)):
         pairs.append((own, loc.at[pl.ds(n * SLAB, SLAB)]))
     pairs += [(med.at[k], loc.at[pl.ds((4 + k) * SLAB, SLAB)]) for k in range(3)]
-    for n, own in enumerate((src_now, src_old, med.at[0], med.at[1], med.at[2])):
-        pairs.append((own, wide.at[pl.ds(n * SLAB, SLAB), inner]))
     copies = [pltpu.make_async_copy(a, b, sems.at[n]) for n, (a, b) in enumerate(pairs)]
     for copy in copies:
         copy.start()
     clear(wide, EDGE, rows)
-    for copy in copies[:2]:
+    for copy in copies[:ready]:
+        copy.wait()
+    pack(wide, packed)
+    leaving = pltpu.make_async_copy(packed, send, sems.at[len(pairs)])
+    leaving.start()
+    for copy in copies[ready : ready + 4]:
         copy.wait()
     lane = lax.broadcasted_iota(jnp.int32, (cells, depth), 1)
     place = lax.broadcasted_iota(jnp.int32, (cells, rec_x.shape[1]), 0)
@@ -80,8 +87,6 @@
             column = jnp.sum(jnp.where(hit, traces_in[h, s : s + 1, :], 0.0), axis=1, keepdims=True)
             surface = jnp.where(lane == steps * h + s, column, surface)
     loc[7 * SLAB] = surface
-    for copy in copies[2:4]:
-        copy.wait()
     core, chip = position()
     own = CHIP * chip + SLAB * core
     first = (CHIP * chip - SLAB, CHIP * chip, own - SLAB, own)
@@ -93,8 +98,9 @@
         for step in range(steps):
             hit = plane == shot_in[at_plane] - first[step]
             amount[chain, step] = jnp.where(hit, -wavelet_in[step], 0.0)
-    for copy in copies[4:]:
+    for copy in copies[ready + 4 :]:
         copy.wait()
+    leaving.wait()
 
 
 def pack(wide, send):
@@ -438,16 +444,16 @@
 
     rcv_now, rcv_old, medium, traces = map(turned, (rcv_now, rcv_old, medium, traces))
     scalars = [pltpu.SMEM(shot.shape, jnp.int32), pltpu.SMEM(wavelet.shape, jnp.float32)]
-    wide, loc, amount, spot = call(
+    send, loc, amount, spot = call(
         gather,
         (src_now, src_old, rcv_now, rcv_old, medium, traces, rec_x, shot, wavelet),
-        [(5 * SLAB, rows + 2 * EDGE, depth), (7 * SLAB + 1, rows, depth)]
+        [(devices, SLAB * FETCH, depth), (7 * SLAB + 1, rows, depth)]
         + [(2, STEPS, 2 * CHIP, depth), (2, rows, depth)],
-        [traces.shape],
-        [pltpu.VMEM(rec_x.shape, jnp.int32), *scalars, pltpu.SemaphoreType.DMA((16,))],
+        [(5 * SLAB, rows + 2 * EDGE, depth), (devices, SLAB * FETCH, depth), traces.shape],
+        [pltpu.VMEM(rec_x.shape, jnp.int32), *scalars, pltpu.SemaphoreType.DMA((17,))],
         far=9,
-    )
-    (send,) = call(pack, (wide,), [(devices, SLAB * FETCH, depth)], [])
+        far_out=(0,),
+    )
     got = lax.all_to_all(send, "wide", 0, 0, tiled=True).reshape(-1, depth)
     sib = lax.ppermute(loc, "wide", swap)
     low, high = jnp.where(core == 0, loc, sib), jnp.where(core == 0, sib, loc)

time: 36.7 us -> 36.6 us (level)
    pallas_call x6 -> x5, Pallas kernels: 5.11 us -> 4.96 us  [call(): pl.pallas_call(kernel, out_shape=[jax.ShapeDtypeStruct(s, jnp.float32) fo...]
  transfers between devices with their start and end apart: 9 -> 9, of which waited for: 6 -> 6; matrix products, arithmetic and copies ran while one was open for 0% -> 0% of each run, Pallas kernels for 4% -> 2%
where the time goes in v6:
time: 36.6 us; the launch traced here: 36 us
  waiting for transfers between devices  16.7 us (46%)
  starting transfers between devices  13.5 us (37%)
  Pallas kernels  4.96 us (14%)
  between operations  0.75 us (2%)
    all_to_all x1, waiting for transfers between devices, on_device(): got = lax.all_to_all(send, 'wide', 0, 0, tiled=True).reshape(-1, depth)  10.1 us
    all_to_all x1, starting transfers between devices, on_device(): got = lax.all_to_all(send, 'wide', 0, 0, tiled=True).reshape(-1, depth)  7.02 us
    pallas_call x5, Pallas kernels, call(): pl.pallas_call(kernel, out_shape=[jax.ShapeDtypeStruct(s, jnp.float32) fo...  4.96 us
    ppermute x1, waiting for transfers between devices, on_device(): mid_y = lax.ppermute(edge_y, 'wide', ring)  2.91 us
    ppermute x1, starting transfers between devices, on_device(): mid_y = lax.ppermute(edge_y, 'wide', ring)  2.54 us
    ppermute x1, starting transfers between devices, on_device(): near = lax.ppermute(jnp.where(turning, 0.0, ours), 'wide', ring)  1.95 us
    ppermute x1, waiting for transfers between devices, on_device(): near_sib = lax.ppermute(near, 'wide', swap)  1.6 us
    ppermute x1, starting transfers between devices, on_device(): mid_x = lax.ppermute(edge_x, 'wide', ring)  1.31 us
  transfers between devices with their start and end apart: 9, of which 6 were waited for; matrix products, arithmetic and copies ran while one was open for 0% of the time, Pallas kernels for 2%

profile of v6, /device:TPU:0, one launch (start us, length us, event | category | flops | bytes accessed | tf_op | source)
XLA Modules:
  0.0 36.0 jit_solution(12329885198595579845)
XLA Ops:
  0.6 1.8 %shard_map.137 = (f32[16,48,128]{2,1,0:T(8,128)}, f32[15,32,128]{2,1,0:T(8,128)S(1)}, f32[2,4,8,128]{3,2,1,0:T(8,128)S(1)}, f32[2,32,128]{2,1,0:T(8,128)S(1)}) custom-call(f32[2,32,128]{2,1,0:T(8,128)} %src_now.1, f32[2,32,128]{2,1,0:T(8,128)} %src_old.1, f32[2,32,128]{2,1,0:T(8,128)} %bitcast.14, f32[2,32,128]{2,1,0:T(8,128)} %bitcast.15, ...), custom_call_target="tpu_custom_call" | custom-call | tf_op jit(solution)/shard_map/pallas_call | solution.py:27
  2.4 0.5 %collective-permute-start = (f32[15,32,128]{2,1,0:T(8,128)S(1)}, f32[15,32,128]{2,1,0:T(8,128)S(1)}, u32[]{:S(2)}, u32[]{:S(2)}) collective-permute-start(f32[15,32,128]{2,1,0:T(8,128)S(1)} %get-tuple-element.23.loc), channel_id=1, source_target_pairs={{0,1},{1,0},{2,3},{3,2},{4,5},{5,4},{6,7},{7,6},{8,9},{9,8},{10,11... | collective-permute-start | bytes 737288 | tf_op jit(solution)/shard_map/ppermute | solution.py:458
  2.9 7.0 %all-to-all-start = ((f32[16,48,128]{2,1,0:T(8,128)}), f32[16,48,128]{2,1,0:T(8,128)S(1)}, u32[]{:S(2)}, u32[]{:S(2)}) async-start(f32[16,48,128]{2,1,0:T(8,128)} %get-tuple-element.24), calls=%async_computation | async-start | bytes 786432 | tf_op jit(solution)/shard_map/all_to_all | solution.py:457
  10.0 0.0 collective-permute-done.sib
  10.1 2.0 %collective-permute-start.1 = (f32[19,32,128]{2,1,0:T(8,128)S(1)}, f32[19,32,128]{2,1,0:T(8,128)S(1)}, u32[]{:S(2)}, u32[]{:S(2)}) collective-permute-start(f32[19,32,128]{2,1,0:T(8,128)S(1)} %maximum_select_fusion), channel_id=1, source_target_pairs={{0,2},{2,4},{4,6},{6,8},{8,10},{10,12},{12,14},{14,15},{15,13},{13... | collective-permute-start | bytes 933896 | tf_op jit(solution)/shard_map/ppermute | solution.py:462
  12.1 10.1 %all-to-all-done = f32[16,48,128]{2,1,0:T(8,128)S(1)} async-done(((f32[16,48,128]{2,1,0:T(8,128)}), f32[16,48,128]{2,1,0:T(8,128)S(1)}, u32[]{:S(2)}, u32[]{:S(2)}) %all-to-all-start) | async-done | bytes 393248 | tf_op jit(solution)/shard_map/all_to_all | solution.py:457
  22.2 0.1 collective-permute-start.3
  22.3 0.5 %collective-permute-done.1.near = f32[19,32,128]{2,1,0:T(8,128)S(1)} collective-permute-done((f32[19,32,128]{2,1,0:T(8,128)S(1)}, f32[19,32,128]{2,1,0:T(8,128)S(1)}, u32[]{:S(2)}, u32[]{:S(2)}) %collective-permute-start.1) | collective-permute-done | bytes 311328 | tf_op jit(solution)/shard_map/ppermute | solution.py:462
  22.7 0.0 collective-permute-start.2
  22.7 1.6 %collective-permute-done.2.near_sib = f32[19,32,128]{2,1,0:T(8,128)S(1)} collective-permute-done((f32[19,32,128]{2,1,0:T(8,128)S(1)}, f32[19,32,128]{2,1,0:T(8,128)S(1)}, u32[]{:S(2)}, u32[]{:S(2)}) %collective-permute-start.2) | collective-permute-done | bytes 311328 | tf_op jit(solution)/shard_map/ppermute | solution.py:463
  24.3 0.0 collective-permute-done.3.got_sib
  24.3 0.6 %shard_map.138 = (f32[2,4,32,128]{3,2,1,0:T(8,128)S(1)}, f32[33,32,128]{2,1,0:T(8,128)S(1)}) custom-call(f32[2,4,8,128]{3,2,1,0:T(8,128)S(1)} %get-tuple-element.21.amount, f32[2,32,128]{2,1,0:T(8,128)S(1)} %get-tuple-element.22.spot, f32[15,32,128]{2,1,0:T(8,128)S(1)} %get-tuple-element.23.loc, f32[15,32,128]{2,1,0:T(8,128)S(1)} %collective-permute-done.sib, ...), custom_call_target="tpu_custom_call" | custom-call | tf_op jit(solution)/shard_map/pallas_call | solution.py:27
  25.0 0.0 copy-start
  25.0 2.5 %collective-permute-start.4 = (f32[2,4,32,128]{3,2,1,0:T(8,128)S(1)}, f32[2,4,32,128]{3,2,1,0:T(8,128)S(1)}, u32[]{:S(2)}, u32[]{:S(2)}) collective-permute-start(f32[2,4,32,128]{3,2,1,0:T(8,128)S(1)} %get-tuple-element.25.edge), channel_id=1, source_target_pairs={{0,2},{2,4},{4,6},{6,8},{8,10},{10,12},{12,14},{14,15},{15,13},{13... | collective-permute-start | bytes 393224 | tf_op jit(solution)/shard_map/ppermute | solution.py:474
  27.6 0.4 %shard_map.139 = (f32[1,4,32,128]{3,2,1,0:T(8,128)S(1)}, f32[24,32,128]{2,1,0:T(8,128)S(1)}) custom-call(f32[2,4,8,128]{3,2,1,0:T(8,128)S(1)} %get-tuple-element.21.amount, f32[2,32,128]{2,1,0:T(8,128)S(1)} %get-tuple-element.22.spot, f32[15,32,128]{2,1,0:T(8,128)S(1)} %get-tuple-element.23.loc, f32[15,32,128]{2,1,0:T(8,128)S(1)} %collective-permute-done.sib, ...), custom_call_target="tpu_custom_call" | custom-call | tf_op jit(solution)/shard_map/pallas_call | solution.py:27
  27.9 1.3 %collective-permute-start.6 = (f32[1,4,32,128]{3,2,1,0:T(8,128)S(1)}, f32[1,4,32,128]{3,2,1,0:T(8,128)S(1)}, u32[]{:S(2)}, u32[]{:S(2)}) collective-permute-start(f32[1,4,32,128]{3,2,1,0:T(8,128)S(1)} %get-tuple-element.27.edge_x), channel_id=1, source_target_pairs={{0,2},{2,4},{4,6},{6,8},{8,10},{10,12},{12,14},{14,15},{15,13},{13... | collective-permute-start | bytes 196616 | tf_op jit(solution)/shard_map/ppermute | solution.py:482
  29.2 2.9 %collective-permute-done.4.near = f32[2,4,32,128]{3,2,1,0:T(8,128)S(1)} collective-permute-done((f32[2,4,32,128]{3,2,1,0:T(8,128)S(1)}, f32[2,4,32,128]{3,2,1,0:T(8,128)S(1)}, u32[]{:S(2)}, u32[]{:S(2)}) %collective-permute-start.4) | collective-permute-done | bytes 131104 | tf_op jit(solution)/shard_map/ppermute | solution.py:474
  32.1 0.0 collective-permute-start.5
  32.2 0.7 %collective-permute-done.6.near_x = f32[1,4,32,128]{3,2,1,0:T(8,128)S(1)} collective-permute-done((f32[1,4,32,128]{3,2,1,0:T(8,128)S(1)}, f32[1,4,32,128]{3,2,1,0:T(8,128)S(1)}, u32[]{:S(2)}, u32[]{:S(2)}) %collective-permute-start.6) | collective-permute-done | bytes 65568 | tf_op jit(solution)/shard_map/ppermute | solution.py:482
  32.9 0.0 collective-permute-start.7
  32.9 0.0 copy-done
  32.9 0.3 shard_map.140
  33.2 0.9 %collective-permute-done.7.sib_x = f32[1,4,32,128]{3,2,1,0:T(8,128)S(1)} collective-permute-done((f32[1,4,32,128]{3,2,1,0:T(8,128)S(1)}, f32[1,4,32,128]{3,2,1,0:T(8,128)S(1)}, u32[]{:S(2)}, u32[]{:S(2)}) %collective-permute-start.7) | collective-permute-done | bytes 65568 | tf_op jit(solution)/shard_map/ppermute | solution.py:483
  34.1 0.0 collective-permute-done.5.near_sib
  34.1 1.9 %shard_map.141 = (f32[2,32,128]{2,1,0:T(8,128)}, f32[2,32,128]{2,1,0:T(8,128)}, f32[2,32,128]{2,1,0:T(8,128)}, f32[2,32,128]{2,1,0:T(8,128)}, f32[33,2,32,128]{3,2,1,0:T(8,128)}) custom-call(f32[2,4,8,128]{3,2,1,0:T(8,128)S(1)} %get-tuple-element.21.amount, f32[2,32,128]{2,1,0:T(8,128)S(1)} %get-tuple-element.22.spot, ...), custom_call_target="tpu_custom_call" | custom-call | tf_op jit(solution)/shard_map/pallas_call | solution.py:27
  (5 shorter events, 0.1 us)
Async XLA Ops:
  2.4 7.6 %collective-permute-start = (f32[15,32,128]{2,1,0:T(8,128)S(1)}, f32[15,32,128]{2,1,0:T(8,128)S(1)}, u32[]{:S(2)}, u32[]{:S(2)}) collective-permute-start(f32[15,32,128]{2,1,0:T(8,128)S(1)} %get-tuple-element.23.loc), channel_id=1, source_target_pairs={{0,1},{1,0},{2,3},{3,2},{4,5},{5,4},{6,7},{7,6},{8,9},{9,8},{10,11... | collective-permute-start | bytes 737288 | tf_op jit(solution)/shard_map/ppermute | solution.py:458
  2.9 19.2 %all-to-all-start = ((f32[16,48,128]{2,1,0:T(8,128)}), f32[16,48,128]{2,1,0:T(8,128)S(1)}, u32[]{:S(2)}, u32[]{:S(2)}) async-start(f32[16,48,128]{2,1,0:T(8,128)} %get-tuple-element.24), calls=%async_computation | async-start | bytes 786432 | tf_op jit(solution)/shard_map/all_to_all | solution.py:457
  10.1 12.6 %collective-permute-start.1 = (f32[19,32,128]{2,1,0:T(8,128)S(1)}, f32[19,32,128]{2,1,0:T(8,128)S(1)}, u32[]{:S(2)}, u32[]{:S(2)}) collective-permute-start(f32[19,32,128]{2,1,0:T(8,128)S(1)} %maximum_select_fusion), channel_id=1, source_target_pairs={{0,2},{2,4},{4,6},{6,8},{8,10},{10,12},{12,14},{14,15},{15,13},{13... | collective-permute-start | bytes 933896 | tf_op jit(solution)/shard_map/ppermute | solution.py:462
  22.2 2.2 %collective-permute-start.3 = (f32[768,128]{1,0:T(8,128)S(1)}, f32[768,128]{1,0:T(8,128)S(1)}, u32[]{:S(2)}, u32[]{:S(2)}) collective-permute-start(f32[768,128]{1,0:T(8,128)S(1)} %bitcast.9), channel_id=1, source_target_pairs={{0,1},{1,0},{2,3},{3,2},{4,5},{5,4},{6,7},{7,6},{8,9},{9,8},{10,11... | collective-permute-start | bytes 1179656 | tf_op jit(solution)/shard_map/ppermute | solution.py:464
  22.7 1.6 %collective-permute-start.2 = (f32[19,32,128]{2,1,0:T(8,128)S(1)}, f32[19,32,128]{2,1,0:T(8,128)S(1)}, u32[]{:S(2)}, u32[]{:S(2)}) collective-permute-start(f32[19,32,128]{2,1,0:T(8,128)S(1)} %collective-permute-done.1.near), channel_id=1, source_target_pairs={{0,1},{1,0},{2,3},{3,2},{4,5},{5,4},{6,7},{7,6},{8,9},{9,8},{10,11... | collective-permute-start | bytes 933896 | tf_op jit(solution)/shard_map/ppermute | solution.py:463
  25.0 7.9 %copy-start = (s32[33]{0:T(128)S(1)}, s32[33]{0:T(128)}, u32[]{:S(2)}) copy-start(s32[33]{0:T(128)} %param.19) | copy-start | bytes 400
  25.0 7.1 %collective-permute-start.4 = (f32[2,4,32,128]{3,2,1,0:T(8,128)S(1)}, f32[2,4,32,128]{3,2,1,0:T(8,128)S(1)}, u32[]{:S(2)}, u32[]{:S(2)}) collective-permute-start(f32[2,4,32,128]{3,2,1,0:T(8,128)S(1)} %get-tuple-element.25.edge), channel_id=1, source_target_pairs={{0,2},{2,4},{4,6},{6,8},{8,10},{10,12},{12,14},{14,15},{15,13},{13... | collective-permute-start | bytes 393224 | tf_op jit(solution)/shard_map/ppermute | solution.py:474
  27.9 4.9 %collective-permute-start.6 = (f32[1,4,32,128]{3,2,1,0:T(8,128)S(1)}, f32[1,4,32,128]{3,2,1,0:T(8,128)S(1)}, u32[]{:S(2)}, u32[]{:S(2)}) collective-permute-start(f32[1,4,32,128]{3,2,1,0:T(8,128)S(1)} %get-tuple-element.27.edge_x), channel_id=1, source_target_pairs={{0,2},{2,4},{4,6},{6,8},{8,10},{10,12},{12,14},{14,15},{15,13},{13... | collective-permute-start | bytes 196616 | tf_op jit(solution)/shard_map/ppermute | solution.py:482
  32.1 2.0 %collective-permute-start.5 = (f32[2,4,32,128]{3,2,1,0:T(8,128)S(1)}, f32[2,4,32,128]{3,2,1,0:T(8,128)S(1)}, u32[]{:S(2)}, u32[]{:S(2)}) collective-permute-start(f32[2,4,32,128]{3,2,1,0:T(8,128)S(1)} %collective-permute-done.4.near), channel_id=1, source_target_pairs={{0,1},{1,0},{2,3},{3,2},{4,5},{5,4},{6,7},{7,6},{8,9},{9,8},{10,11... | collective-permute-start | bytes 393224 | tf_op jit(solution)/shard_map/ppermute | solution.py:475
  32.9 1.3 %collective-permute-start.7 = (f32[1,4,32,128]{3,2,1,0:T(8,128)S(1)}, f32[1,4,32,128]{3,2,1,0:T(8,128)S(1)}, u32[]{:S(2)}, u32[]{:S(2)}) collective-permute-start(f32[1,4,32,128]{3,2,1,0:T(8,128)S(1)} %collective-permute-done.6.near_x), channel_id=1, source_target_pairs={{0,1},{1,0},{2,3},{3,2},{4,5},{5,4},{6,7},{7,6},{8,9},{9,8},{10,11... | collective-permute-start | bytes 196616 | tf_op jit(solution)/shard_map/ppermute | solution.py:483

commit v7 on v5

--- a/solution.py
+++ b/solution.py
@@ -394,12 +394,6 @@
     last_steps(
         last, edges, 1, now_s, lambda i: carry[SPAN + i], med, new_s, end_s, 1, shots, ahead
     )
-    shots = [shot_at(amount, spot, 1, 2 + n) for n in range(2)]
-    last_steps(
-        last, (edge_x, near_x, sib_x), 0, now_x, lambda i: carry_x[i],
-        lambda k, i: carry_x[SPAN * (1 + k) + i], new_x, end_x, 0, shots,
-    )
-    copies += finish(end_x, new_x, src_next, src_prior, sems, lags + 2)
     for slot in range(lags):
         for p in range(SLAB):
             for b in range(0, rows, 8):
@@ -413,6 +407,12 @@
             pltpu.make_async_copy(planes.at[slot], image.at[slots[slot, 0].astype(jnp.int32)], sems.at[slot])
         )
         copies[-1].start()
+    shots = [shot_at(amount, spot, 1, 2 + n) for n in range(2)]
+    last_steps(
+        last, (edge_x, near_x, sib_x), 0, now_x, lambda i: carry_x[i],
+        lambda k, i: carry_x[SPAN * (1 + k) + i], new_x, end_x, 0, shots,
+    )
+    copies += finish(end_x, new_x, src_next, src_prior, sems, lags + 2)
     for copy in copies:
         copy.wait()
 

time: 36.7 us -> 36.6 us (level)
  no operation moved by 1% of the time
where the time goes in v7:
time: 36.6 us; the launch traced here: 36 us
  waiting for transfers between devices  16.7 us (46%)
  starting transfers between devices  13.5 us (37%)
  Pallas kernels  4.97 us (14%)
  between operations  0.75 us (2%)
    all_to_all x1, waiting for transfers between devices, on_device(): got = lax.all_to_all(send, 'wide', 0, 0, tiled=True).reshape(-1, depth)  10.1 us
    all_to_all x1, starting transfers between devices, on_device(): got = lax.all_to_all(send, 'wide', 0, 0, tiled=True).reshape(-1, depth)  7.02 us
    pallas_call x6, Pallas kernels, call(): pl.pallas_call(kernel, out_shape=[jax.ShapeDtypeStruct(s, jnp.float32) fo...  4.97 us
    ppermute x1, waiting for transfers between devices, on_device(): mid_y = lax.ppermute(edge_y, 'wide', ring)  2.91 us
    ppermute x1, starting transfers between devices, on_device(): mid_y = lax.ppermute(edge_y, 'wide', ring)  2.54 us
    ppermute x1, starting transfers between devices, on_device(): near = lax.ppermute(jnp.where(turning, 0.0, ours), 'wide', ring)  1.95 us
    ppermute x1, waiting for transfers between devices, on_device(): near_sib = lax.ppermute(near, 'wide', swap)  1.6 us
    ppermute x1, starting transfers between devices, on_device(): mid_x = lax.ppermute(edge_x, 'wide', ring)  1.31 us
  transfers between devices with their start and end apart: 9, of which 6 were waited for; matrix products, arithmetic and copies ran while one was open for 0% of the time, Pallas kernels for 4%

profile of v7, /device:TPU:0, one launch (start us, length us, event | category | flops | bytes accessed | tf_op | source)
XLA Modules:
  0.0 36.0 jit_solution(11739221063805045504)
XLA Ops:
  0.6 1.1 %shard_map.137 = (f32[10,48,128]{2,1,0:T(8,128)S(1)}, f32[15,32,128]{2,1,0:T(8,128)S(1)}, f32[2,4,8,128]{3,2,1,0:T(8,128)S(1)}, f32[2,32,128]{2,1,0:T(8,128)S(1)}) custom-call(f32[2,32,128]{2,1,0:T(8,128)} %src_now.1, f32[2,32,128]{2,1,0:T(8,128)} %src_old.1, f32[2,32,128]{2,1,0:T(8,128)} %bitcast.14, f32[2,32,128]{2,1,0:T(8,128)} %bitcast.15, ...), custom_call_target="tpu_custom_call" | custom-call | tf_op jit(solution)/shard_map/pallas_call | solution.py:27
  1.8 0.5 %collective-permute-start = (f32[15,32,128]{2,1,0:T(8,128)S(1)}, f32[15,32,128]{2,1,0:T(8,128)S(1)}, u32[]{:S(2)}, u32[]{:S(2)}) collective-permute-start(f32[15,32,128]{2,1,0:T(8,128)S(1)} %get-tuple-element.23.loc), channel_id=1, source_target_pairs={{0,1},{1,0},{2,3},{3,2},{4,5},{5,4},{6,7},{7,6},{8,9},{9,8},{10,11... | collective-permute-start | bytes 737288 | tf_op jit(solution)/shard_map/ppermute | solution.py:452
  2.3 0.8 %shard_map.138 = f32[16,48,128]{2,1,0:T(8,128)} custom-call(f32[10,48,128]{2,1,0:T(8,128)S(1)} %get-tuple-element.24.wide), custom_call_target="tpu_custom_call" | custom-call | tf_op jit(solution)/shard_map/pallas_call | solution.py:27
  3.1 7.0 %all-to-all-start = ((f32[16,48,128]{2,1,0:T(8,128)}), f32[16,48,128]{2,1,0:T(8,128)S(1)}, u32[]{:S(2)}, u32[]{:S(2)}) async-start(f32[16,48,128]{2,1,0:T(8,128)} %shard_map.138), calls=%async_computation | async-start | bytes 786432 | tf_op jit(solution)/shard_map/all_to_all | solution.py:451
  10.1 0.0 collective-permute-done.sib
  10.3 2.0 %collective-permute-start.1 = (f32[19,32,128]{2,1,0:T(8,128)S(1)}, f32[19,32,128]{2,1,0:T(8,128)S(1)}, u32[]{:S(2)}, u32[]{:S(2)}) collective-permute-start(f32[19,32,128]{2,1,0:T(8,128)S(1)} %maximum_select_fusion), channel_id=1, source_target_pairs={{0,2},{2,4},{4,6},{6,8},{8,10},{10,12},{12,14},{14,15},{15,13},{13... | collective-permute-start | bytes 933896 | tf_op jit(solution)/shard_map/ppermute | solution.py:456
  12.2 10.1 %all-to-all-done = f32[16,48,128]{2,1,0:T(8,128)S(1)} async-done(((f32[16,48,128]{2,1,0:T(8,128)}), f32[16,48,128]{2,1,0:T(8,128)S(1)}, u32[]{:S(2)}, u32[]{:S(2)}) %all-to-all-start) | async-done | bytes 393248 | tf_op jit(solution)/shard_map/all_to_all | solution.py:451
  22.3 0.1 collective-permute-start.3
  22.4 0.5 %collective-permute-done.1.near = f32[19,32,128]{2,1,0:T(8,128)S(1)} collective-permute-done((f32[19,32,128]{2,1,0:T(8,128)S(1)}, f32[19,32,128]{2,1,0:T(8,128)S(1)}, u32[]{:S(2)}, u32[]{:S(2)}) %collective-permute-start.1) | collective-permute-done | bytes 311328 | tf_op jit(solution)/shard_map/ppermute | solution.py:456
  22.9 0.0 collective-permute-start.2
  22.9 1.6 %collective-permute-done.2.near_sib = f32[19,32,128]{2,1,0:T(8,128)S(1)} collective-permute-done((f32[19,32,128]{2,1,0:T(8,128)S(1)}, f32[19,32,128]{2,1,0:T(8,128)S(1)}, u32[]{:S(2)}, u32[]{:S(2)}) %collective-permute-start.2) | collective-permute-done | bytes 311328 | tf_op jit(solution)/shard_map/ppermute | solution.py:457
  24.5 0.0 collective-permute-done.3.got_sib
  24.5 0.6 %shard_map.139 = (f32[2,4,32,128]{3,2,1,0:T(8,128)S(1)}, f32[33,32,128]{2,1,0:T(8,128)S(1)}) custom-call(f32[2,4,8,128]{3,2,1,0:T(8,128)S(1)} %get-tuple-element.21.amount, f32[2,32,128]{2,1,0:T(8,128)S(1)} %get-tuple-element.22.spot, f32[15,32,128]{2,1,0:T(8,128)S(1)} %get-tuple-element.23.loc, f32[15,32,128]{2,1,0:T(8,128)S(1)} %collective-permute-done.sib, ...), custom_call_target="tpu_custom_call" | custom-call | tf_op jit(solution)/shard_map/pallas_call | solution.py:27
  25.2 0.0 copy-start
  25.2 2.5 %collective-permute-start.4 = (f32[2,4,32,128]{3,2,1,0:T(8,128)S(1)}, f32[2,4,32,128]{3,2,1,0:T(8,128)S(1)}, u32[]{:S(2)}, u32[]{:S(2)}) collective-permute-start(f32[2,4,32,128]{3,2,1,0:T(8,128)S(1)} %get-tuple-element.25.edge), channel_id=1, source_target_pairs={{0,2},{2,4},{4,6},{6,8},{8,10},{10,12},{12,14},{14,15},{15,13},{13... | collective-permute-start | bytes 393224 | tf_op jit(solution)/shard_map/ppermute | solution.py:468
  27.7 0.4 %shard_map.140 = (f32[1,4,32,128]{3,2,1,0:T(8,128)S(1)}, f32[24,32,128]{2,1,0:T(8,128)S(1)}) custom-call(f32[2,4,8,128]{3,2,1,0:T(8,128)S(1)} %get-tuple-element.21.amount, f32[2,32,128]{2,1,0:T(8,128)S(1)} %get-tuple-element.22.spot, f32[15,32,128]{2,1,0:T(8,128)S(1)} %get-tuple-element.23.loc, f32[15,32,128]{2,1,0:T(8,128)S(1)} %collective-permute-done.sib, ...), custom_call_target="tpu_custom_call" | custom-call | tf_op jit(solution)/shard_map/pallas_call | solution.py:27
  28.1 1.3 %collective-permute-start.6 = (f32[1,4,32,128]{3,2,1,0:T(8,128)S(1)}, f32[1,4,32,128]{3,2,1,0:T(8,128)S(1)}, u32[]{:S(2)}, u32[]{:S(2)}) collective-permute-start(f32[1,4,32,128]{3,2,1,0:T(8,128)S(1)} %get-tuple-element.27.edge_x), channel_id=1, source_target_pairs={{0,2},{2,4},{4,6},{6,8},{8,10},{10,12},{12,14},{14,15},{15,13},{13... | collective-permute-start | bytes 196616 | tf_op jit(solution)/shard_map/ppermute | solution.py:476
  29.4 2.9 %collective-permute-done.4.near = f32[2,4,32,128]{3,2,1,0:T(8,128)S(1)} collective-permute-done((f32[2,4,32,128]{3,2,1,0:T(8,128)S(1)}, f32[2,4,32,128]{3,2,1,0:T(8,128)S(1)}, u32[]{:S(2)}, u32[]{:S(2)}) %collective-permute-start.4) | collective-permute-done | bytes 131104 | tf_op jit(solution)/shard_map/ppermute | solution.py:468
  32.3 0.0 collective-permute-start.5
  32.3 0.7 %collective-permute-done.6.near_x = f32[1,4,32,128]{3,2,1,0:T(8,128)S(1)} collective-permute-done((f32[1,4,32,128]{3,2,1,0:T(8,128)S(1)}, f32[1,4,32,128]{3,2,1,0:T(8,128)S(1)}, u32[]{:S(2)}, u32[]{:S(2)}) %collective-permute-start.6) | collective-permute-done | bytes 65568 | tf_op jit(solution)/shard_map/ppermute | solution.py:476
  33.0 0.0 collective-permute-start.7
  33.0 0.0 copy-done
  33.0 0.3 shard_map.141
  33.3 0.9 %collective-permute-done.7.sib_x = f32[1,4,32,128]{3,2,1,0:T(8,128)S(1)} collective-permute-done((f32[1,4,32,128]{3,2,1,0:T(8,128)S(1)}, f32[1,4,32,128]{3,2,1,0:T(8,128)S(1)}, u32[]{:S(2)}, u32[]{:S(2)}) %collective-permute-start.7) | collective-permute-done | bytes 65568 | tf_op jit(solution)/shard_map/ppermute | solution.py:477
  34.3 0.0 collective-permute-done.5.near_sib
  34.3 1.7 %shard_map.142 = (f32[2,32,128]{2,1,0:T(8,128)}, f32[2,32,128]{2,1,0:T(8,128)}, f32[2,32,128]{2,1,0:T(8,128)}, f32[2,32,128]{2,1,0:T(8,128)}, f32[33,2,32,128]{3,2,1,0:T(8,128)}) custom-call(f32[2,4,8,128]{3,2,1,0:T(8,128)S(1)} %get-tuple-element.21.amount, f32[2,32,128]{2,1,0:T(8,128)S(1)} %get-tuple-element.22.spot, ...), custom_call_target="tpu_custom_call" | custom-call | tf_op jit(solution)/shard_map/pallas_call | solution.py:27
  (5 shorter events, 0.1 us)
Async XLA Ops:
  1.8 8.4 %collective-permute-start = (f32[15,32,128]{2,1,0:T(8,128)S(1)}, f32[15,32,128]{2,1,0:T(8,128)S(1)}, u32[]{:S(2)}, u32[]{:S(2)}) collective-permute-start(f32[15,32,128]{2,1,0:T(8,128)S(1)} %get-tuple-element.23.loc), channel_id=1, source_target_pairs={{0,1},{1,0},{2,3},{3,2},{4,5},{5,4},{6,7},{7,6},{8,9},{9,8},{10,11... | collective-permute-start | bytes 737288 | tf_op jit(solution)/shard_map/ppermute | solution.py:452
  3.1 19.2 %all-to-all-start = ((f32[16,48,128]{2,1,0:T(8,128)}), f32[16,48,128]{2,1,0:T(8,128)S(1)}, u32[]{:S(2)}, u32[]{:S(2)}) async-start(f32[16,48,128]{2,1,0:T(8,128)} %shard_map.138), calls=%async_computation | async-start | bytes 786432 | tf_op jit(solution)/shard_map/all_to_all | solution.py:451
  10.3 12.6 %collective-permute-start.1 = (f32[19,32,128]{2,1,0:T(8,128)S(1)}, f32[19,32,128]{2,1,0:T(8,128)S(1)}, u32[]{:S(2)}, u32[]{:S(2)}) collective-permute-start(f32[19,32,128]{2,1,0:T(8,128)S(1)} %maximum_select_fusion), channel_id=1, source_target_pairs={{0,2},{2,4},{4,6},{6,8},{8,10},{10,12},{12,14},{14,15},{15,13},{13... | collective-permute-start | bytes 933896 | tf_op jit(solution)/shard_map/ppermute | solution.py:456
  22.3 2.2 %collective-permute-start.3 = (f32[768,128]{1,0:T(8,128)S(1)}, f32[768,128]{1,0:T(8,128)S(1)}, u32[]{:S(2)}, u32[]{:S(2)}) collective-permute-start(f32[768,128]{1,0:T(8,128)S(1)} %bitcast.9), channel_id=1, source_target_pairs={{0,1},{1,0},{2,3},{3,2},{4,5},{5,4},{6,7},{7,6},{8,9},{9,8},{10,11... | collective-permute-start | bytes 1179656 | tf_op jit(solution)/shard_map/ppermute | solution.py:458
  22.9 1.6 %collective-permute-start.2 = (f32[19,32,128]{2,1,0:T(8,128)S(1)}, f32[19,32,128]{2,1,0:T(8,128)S(1)}, u32[]{:S(2)}, u32[]{:S(2)}) collective-permute-start(f32[19,32,128]{2,1,0:T(8,128)S(1)} %collective-permute-done.1.near), channel_id=1, source_target_pairs={{0,1},{1,0},{2,3},{3,2},{4,5},{5,4},{6,7},{7,6},{8,9},{9,8},{10,11... | collective-permute-start | bytes 933896 | tf_op jit(solution)/shard_map/ppermute | solution.py:457
  25.2 7.9 %copy-start = (s32[33]{0:T(128)S(1)}, s32[33]{0:T(128)}, u32[]{:S(2)}) copy-start(s32[33]{0:T(128)} %param.19) | copy-start | bytes 400
  25.2 7.1 %collective-permute-start.4 = (f32[2,4,32,128]{3,2,1,0:T(8,128)S(1)}, f32[2,4,32,128]{3,2,1,0:T(8,128)S(1)}, u32[]{:S(2)}, u32[]{:S(2)}) collective-permute-start(f32[2,4,32,128]{3,2,1,0:T(8,128)S(1)} %get-tuple-element.25.edge), channel_id=1, source_target_pairs={{0,2},{2,4},{4,6},{6,8},{8,10},{10,12},{12,14},{14,15},{15,13},{13... | collective-permute-start | bytes 393224 | tf_op jit(solution)/shard_map/ppermute | solution.py:468
  28.1 4.9 %collective-permute-start.6 = (f32[1,4,32,128]{3,2,1,0:T(8,128)S(1)}, f32[1,4,32,128]{3,2,1,0:T(8,128)S(1)}, u32[]{:S(2)}, u32[]{:S(2)}) collective-permute-start(f32[1,4,32,128]{3,2,1,0:T(8,128)S(1)} %get-tuple-element.27.edge_x), channel_id=1, source_target_pairs={{0,2},{2,4},{4,6},{6,8},{8,10},{10,12},{12,14},{14,15},{15,13},{13... | collective-permute-start | bytes 196616 | tf_op jit(solution)/shard_map/ppermute | solution.py:476
  32.3 2.0 %collective-permute-start.5 = (f32[2,4,32,128]{3,2,1,0:T(8,128)S(1)}, f32[2,4,32,128]{3,2,1,0:T(8,128)S(1)}, u32[]{:S(2)}, u32[]{:S(2)}) collective-permute-start(f32[2,4,32,128]{3,2,1,0:T(8,128)S(1)} %collective-permute-done.4.near), channel_id=1, source_target_pairs={{0,1},{1,0},{2,3},{3,2},{4,5},{5,4},{6,7},{7,6},{8,9},{9,8},{10,11... | collective-permute-start | bytes 393224 | tf_op jit(solution)/shard_map/ppermute | solution.py:469
  33.0 1.3 %collective-permute-start.7 = (f32[1,4,32,128]{3,2,1,0:T(8,128)S(1)}, f32[1,4,32,128]{3,2,1,0:T(8,128)S(1)}, u32[]{:S(2)}, u32[]{:S(2)}) collective-permute-start(f32[1,4,32,128]{3,2,1,0:T(8,128)S(1)} %collective-permute-done.6.near_x), channel_id=1, source_target_pairs={{0,1},{1,0},{2,3},{3,2},{4,5},{5,4},{6,7},{7,6},{8,9},{9,8},{10,11... | collective-permute-start | bytes 196616 | tf_op jit(solution)/shard_map/ppermute | solution.py:477
